TPU v7x, 256 devices: a whole 4x4x8 slice. The times are simulated.
256 devices in a mesh: ctx: 32 (over x_hi, z, core), head: 8 (over y, x_lo).
Axes of the slice: x: 4 (x_hi: 2, x_lo: 2; x = x_hi * 2 + x_lo), y: 4, z: 8, core: 2. Of those that a mesh axis runs over, the one named last changes fastest.
Arguments:
- patches: bfloat16 [5120, 4608], P('ctx'), may hold values from -6 to 6
- vis_pos: int32 [5120], P('ctx'), may hold values from 0 to 8191, as said below
- span_of: int32 [32, 2], P('ctx'), may hold values from 0 to 63, as said below
- text_rows: bfloat16 [8192, 4096], P('ctx', 'head'), may hold values from -250 to 250
- proj_weight: bfloat16 [4608, 4096], P(None, 'head'), may hold values from -0.09375 to 0.09375
- norm_gain: float32 [4096], replicated, may hold values from 0.1 to 1.9
- qkv_weight: bfloat16 [4096, 8, 6, 128], P(None, 'head'), may hold values from -3 to 3
Outputs:
- context: bfloat16 [8192, 4096], P('ctx', 'head')
Inputs may be any that keep to these rules, and one draw needn't show every extreme that they name: vis_pos holds distinct positions. Span c is positions c * 128 to c * 128 + 127; at most 8 of the patch rows of one index of ctx lie in the two spans of one owner, and exactly 8 for one owner of each index. span_of lists every span number once.
All inputs are finite; a program needn't handle non-finite values.
Results may differ from a plain program's by a relative error of at most 0.012.
The roundings to bfloat16 on the way count: a program that leaves them out, or rounds other values in their place, can miss the bound.
Values may be sent and summed in bfloat16 or wider, within the bound.
No kernel may reach another device: no remote copies, remote signals or barrier semaphores. Data moves between devices by JAX's collectives and lax.ppermute only.
A program may use at most 64 MiB of HBM per device.

v0:
```python
import functools
import math

import jax
import jax.numpy as jnp
from jax import lax
from jax.experimental import pallas as pl
from jax.experimental.pallas import tpu as pltpu
from jax.sharding import PartitionSpec as P

HEADS = 32
KVH = 8
HD = 128
GROUPS = HEADS // KVH
WIDE = (GROUPS + 2) * HD
SPAN = 128
ROWS = 2 * SPAN
OWNERS = 32
CAP = ROWS // OWNERS
SLOTS = OWNERS * CAP
Z = 8
Y = 4
HEAD_DEVS = 8
COLS = 512
MAIL = WIDE + HD
QCOLS = GROUPS * ROWS
STATE = HD + 8

rope_theta = 500000.0
norm_eps = 1e-05
masked_score = -1e30
EXP_SCALE = HD ** (-0.5) * math.log2(math.e)
VMEM_LIMIT = 16 * 1024 * 1024
ATTEND_LIMIT = 8 * 1024 * 1024

bf16 = jnp.bfloat16
f32 = jnp.float32


def ctx_perm(move):
    return [(i, move(i)) for i in range(OWNERS)]


def z_move():
    return ctx_perm(lambda i: (i // 16) * 16 + ((i // 2 % Z + 1 - 2 * (i % 2)) % Z) * 2 + i % 2)


def core_swap():
    return ctx_perm(lambda i: i ^ 1)


def xhi_swap():
    return ctx_perm(lambda i: i ^ 16)


def y_shift(step):
    return [(i, (i // 2 + step) % Y * 2 + i % 2) for i in range(HEAD_DEVS)]


def xlo_swap():
    return [(i, i ^ 1) for i in range(HEAD_DEVS)]


def rotary_tables(positions):
    frequency = rope_theta ** (-jnp.arange(0, HD, 2, dtype=f32) / HD)
    angles = positions.astype(f32)[:, None] * frequency[None, :]
    cosine, sine = jnp.cos(angles), jnp.sin(angles)
    return jnp.concatenate([cosine, cosine], axis=1), jnp.concatenate([-sine, sine], axis=1)


def gather_first(own):
    return [
        lax.ppermute(own, "head", xlo_swap()),
        lax.ppermute(own, "head", y_shift(1)),
        lax.ppermute(own, "head", y_shift(-1)),
    ]


def gather_second(side, down, up):
    return [
        lax.ppermute(down, "head", y_shift(1)),
        lax.ppermute(side, "head", y_shift(-1)),
        lax.ppermute(down, "head", xlo_swap()),
    ]


def gather_third(top, low):
    return [lax.ppermute(top, "head", y_shift(1)), lax.ppermute(low, "head", y_shift(-1))]


def block_order(place):
    y, x = place // 2, place % 2

    def at(step, flip):
        return (y + step + Y) % Y * 2 + (x + flip) % 2

    return [at(0, 0), at(0, 1), at(-1, 0), at(1, 0), at(2, 0), at(1, 1), at(-1, 1), at(2, 1)]


def qkv_kernel(rows, count, *refs):
    blocks, refs = refs[:count], refs[count:]
    weight_ref, gain_ref, cos_ref, sin_ref = refs[:4]
    order = block_order(lax.axis_index("head")) if count > 1 else list(range(HEAD_DEVS))

    def block(k):
        if count == 1:
            return blocks[0][:, k * COLS : (k + 1) * COLS].astype(f32)
        if k < 7:
            return blocks[k][...].astype(f32)
        return jnp.concatenate([blocks[7][...], blocks[8][...]], axis=0).astype(f32)

    squares = jnp.zeros((rows, COLS), f32)
    for k in range(8):
        wide = block(k)
        squares = squares + wide * wide
    total = jnp.sum(squares, axis=1, keepdims=True)
    inverse = lax.rsqrt(total * (1.0 / (8 * COLS)) + norm_eps)
    pairs = (GROUPS + 2) // 2
    projected = [jnp.zeros((rows, 2 * HD), f32) for pair in range(pairs)]
    for k in range(8):
        normed = (block(k) * inverse * gain_ref[order[k]]).astype(bf16)
        for pair in range(pairs):
            weight = jnp.concatenate(
                [weight_ref[2 * pair, order[k]], weight_ref[2 * pair + 1, order[k]]], axis=1
            )
            projected[pair] = projected[pair] + jnp.dot(
                normed, weight, preferred_element_type=f32
            )
    cosine, sine = cos_ref[...], sin_ref[...]
    parts = []
    for j in range(GROUPS + 2):
        slab = projected[j // 2][:, j % 2 * HD : (j % 2 + 1) * HD]
        if j <= GROUPS:
            slab = slab * cosine + pltpu.roll(slab, HD // 2, 1) * sine
        parts.append(slab)
    query_ref, kv_ref = refs[4:6]
    for j in range(GROUPS + 2):
        if j == GROUPS:
            kv_ref[:ROWS, :] = parts[j].astype(bf16)
            continue
        for s in range(2):
            turned = parts[j][s * SPAN : (s + 1) * SPAN, :].T.astype(bf16)
            if j < GROUPS:
                start = (s * GROUPS + j) * SPAN
                query_ref[:, start : start + SPAN] = turned
            else:
                kv_ref[ROWS + s * SPAN : ROWS + (s + 1) * SPAN, :] = turned


def vmem(count):
    return [pl.BlockSpec(memory_space=pltpu.VMEM)] * count


def load_kernel(weight_ref, out_ref, sems):
    copies = [
        pltpu.make_async_copy(weight_ref.at[j], out_ref.at[j], sems.at[j]) for j in range(GROUPS + 2)
    ]
    for copy in copies:
        copy.start()
    for copy in copies:
        copy.wait()


def load_weight(weight):
    return pl.pallas_call(
        load_kernel,
        out_shape=jax.ShapeDtypeStruct(weight.shape, bf16),
        in_specs=[pl.BlockSpec(memory_space=pltpu.HBM)],
        out_specs=pl.BlockSpec(memory_space=pltpu.VMEM),
        scratch_shapes=[pltpu.SemaphoreType.DMA((GROUPS + 2,))],
        compiler_params=pltpu.CompilerParams(vmem_limit_bytes=ATTEND_LIMIT),
        cost_estimate=pl.CostEstimate(flops=0, bytes_accessed=2 * weight.size * 2, transcendentals=0),
        name="load_weight",
    )(weight)


def project_qkv(blocks, weight, gain, cosine, sine):
    rows = blocks[0].shape[0]
    return pl.pallas_call(
        functools.partial(qkv_kernel, rows, len(blocks)),
        out_shape=(
            jax.ShapeDtypeStruct((HD, QCOLS), bf16),
            jax.ShapeDtypeStruct((2 * ROWS, HD), bf16),
        ),
        in_specs=vmem(len(blocks) + 4),
        out_specs=tuple(vmem(2)),
        compiler_params=pltpu.CompilerParams(vmem_limit_bytes=VMEM_LIMIT),
        cost_estimate=pl.CostEstimate(
            flops=2 * rows * 8 * COLS * WIDE, bytes_accessed=8 * COLS * WIDE * 2 + rows * 8192, transcendentals=0
        ),
        name="norm_qkv",
    )(*blocks, weight, gain, cosine, sine)


def route_kernel(rows_ref, slot_ref, mark_ref, out_ref):
    count = rows_ref.shape[0]
    places = lax.broadcasted_iota(jnp.int32, (SLOTS, count), 0)
    pick = jnp.where(places == slot_ref[...], 1.0, 0.0).astype(bf16)
    out_ref[:, :COLS] = jnp.dot(pick, rows_ref[...], preferred_element_type=f32).astype(bf16)
    out_ref[:, COLS:] = jnp.dot(pick, mark_ref[...], preferred_element_type=f32).astype(bf16)


def place_kernel(mail_ref, text_ref, out_ref):
    mail = mail_ref[...]
    marks = mail[:, COLS : COLS + 1].astype(f32)
    rows = (lax.broadcasted_iota(jnp.int32, (SLOTS, ROWS), 1) + 1).astype(f32)
    place = jnp.where(marks == rows, 1.0, 0.0).astype(bf16)
    placed = lax.dot_general(place, mail, (((0,), (0,)), ((), ())), preferred_element_type=f32)
    visual = placed[:, COLS:] > 0.5
    for j in range(COLS // HD):
        cols = slice(j * HD, (j + 1) * HD)
        out_ref[:, cols] = jnp.where(visual, placed[:, cols], text_ref[:, cols].astype(f32)).astype(bf16)


def whole(kernel, shape, name, *args):
    return pl.pallas_call(
        kernel,
        out_shape=jax.ShapeDtypeStruct(shape, bf16),
        in_specs=vmem(len(args)),
        out_specs=pl.BlockSpec(memory_space=pltpu.VMEM),
        compiler_params=pltpu.CompilerParams(vmem_limit_bytes=ATTEND_LIMIT),
        cost_estimate=pl.CostEstimate(flops=2 * SLOTS * ROWS * COLS, bytes_accessed=4 * ROWS * COLS, transcendentals=0),
        name=name,
    )(*args)


def attend_kernel(first, given, key_row, *refs):
    key_ref, span_ref = refs[:2]
    query_refs = refs[2:4]
    kv_refs = refs[4 : 4 + given]
    ins, outs = refs[4 + given : -2], refs[-2:]
    parts = [(kv, start) for kv in kv_refs for start in range(0, kv.shape[0], 2 * ROWS)]
    keys = jnp.concatenate([kv[start : start + ROWS, :] for kv, start in parts], axis=0)
    values = jnp.concatenate(
        [kv[start + ROWS + s * SPAN : start + ROWS + (s + 1) * SPAN, :] for kv, start in parts for s in range(2)],
        axis=1,
    )
    count = len(parts)
    row = lax.broadcasted_iota(jnp.int32, (SPAN, SPAN), 0).astype(f32)
    lane = lax.broadcasted_iota(jnp.int32, (SPAN, SPAN), 1).astype(f32)
    for half in range(2):
        for tile in range(QCOLS // SPAN):
            cols = slice(tile * SPAN, (tile + 1) * SPAN)
            query_span = span_ref[half : half + 1, cols]
            score = jnp.dot(keys, query_refs[half][:, cols], preferred_element_type=f32)
            pieces = []
            for j in range(2 * count):
                key_span = key_ref[key_row + j : key_row + j + 1, :]
                if first:
                    allowed = key_span * SPAN + row <= query_span * SPAN + lane
                else:
                    allowed = key_span < query_span
                pieces.append(jnp.where(allowed, score[j * SPAN : (j + 1) * SPAN, :], masked_score))
            score = jnp.concatenate(pieces, axis=0)
            high = jnp.max(score, axis=0, keepdims=True)
            if first:
                new_top = high
            else:
                top = ins[half][HD : HD + 1, cols]
                new_top = jnp.maximum(top, high)
                shrink = jnp.exp2((top - new_top) * EXP_SCALE)
            terms = jnp.exp2((score - new_top) * EXP_SCALE)
            total = jnp.sum(terms, axis=0, keepdims=True)
            accum = jnp.dot(values, terms.astype(bf16), preferred_element_type=f32)
            if not first:
                total = total + ins[half][HD + 1 : HD + 2, cols] * shrink
                accum = accum + ins[half][:HD, cols] * shrink
            outs[half][:HD, cols] = accum
            outs[half][HD : HD + 1, cols] = new_top
            outs[half][HD + 1 : HD + 2, cols] = total
            outs[half][HD + 2 : STATE, cols] = jnp.zeros((STATE - HD - 2, SPAN), f32)


def attend(key_spans, query_spans, queries, blocks, key_row, states):
    first = states is None
    count = len(blocks)
    given = () if first else tuple(states)
    return pl.pallas_call(
        functools.partial(attend_kernel, first, count, key_row),
        out_shape=(jax.ShapeDtypeStruct((STATE, QCOLS), f32),) * 2,
        in_specs=vmem(4 + count + len(given)),
        out_specs=tuple(vmem(2)),
        compiler_params=pltpu.CompilerParams(vmem_limit_bytes=ATTEND_LIMIT),
        cost_estimate=pl.CostEstimate(
            flops=4 * count * ROWS * 2 * QCOLS * HD,
            bytes_accessed=count * 4 * ROWS * HD + 2 * STATE * QCOLS * 8,
            transcendentals=count * ROWS * 2 * QCOLS,
        ),
        name="attend",
    )(key_spans, query_spans, *queries, *blocks, *given)


def finish_kernel(mine_ref, theirs_ref, out_ref):
    top_a, top_b = mine_ref[HD : HD + 1, :], theirs_ref[HD : HD + 1, :]
    top = jnp.maximum(top_a, top_b)
    scale_a = jnp.exp2((top_a - top) * EXP_SCALE)
    scale_b = jnp.exp2((top_b - top) * EXP_SCALE)
    total = mine_ref[HD + 1 : HD + 2, :] * scale_a + theirs_ref[HD + 1 : HD + 2, :] * scale_b
    accum = (mine_ref[:HD, :] * scale_a + theirs_ref[:HD, :] * scale_b) / total
    for s in range(2):
        for g in range(GROUPS):
            start = (s * GROUPS + g) * SPAN
            out_ref[s * SPAN : (s + 1) * SPAN, g * HD : (g + 1) * HD] = accum[
                :, start : start + SPAN
            ].T.astype(bf16)


def finish(mine, theirs):
    return pl.pallas_call(
        finish_kernel,
        out_shape=jax.ShapeDtypeStruct((ROWS, GROUPS * HD), bf16),
        in_specs=vmem(2),
        out_specs=pl.BlockSpec(memory_space=pltpu.VMEM),
        compiler_params=pltpu.CompilerParams(vmem_limit_bytes=VMEM_LIMIT),
        name="finish",
    )(mine, theirs)


def on_device(patches, vis_pos, span_of, text_rows, proj_weight, norm_gain, qkv_weight):
    place = lax.axis_index("ctx")
    x_hi, z, core = place // 16, place // 2 % Z, place % 2
    weight = jnp.transpose(qkv_weight, (2, 0, 1, 3)).reshape(GROUPS + 2, HEAD_DEVS, COLS, HD)
    gain = norm_gain.reshape(HEAD_DEVS, 1, COLS)

    table = lax.all_to_all(
        jnp.broadcast_to(span_of[:, None, :], (OWNERS, 1, 2)), "ctx", split_axis=0, concat_axis=0, tiled=True
    ).reshape(2 * OWNERS)
    visual = jnp.dot(patches, proj_weight, preferred_element_type=f32).astype(bf16)

    entries = jnp.arange(2 * OWNERS, dtype=jnp.int32)
    matches = table[None, :] == (vis_pos // SPAN)[:, None]
    entry = jnp.sum(jnp.where(matches, entries[None, :], 0), axis=1)
    owner = entry // 2
    count = vis_pos.shape[0]
    before = jnp.arange(count)[None, :] < jnp.arange(count)[:, None]
    rank = jnp.sum((owner[:, None] == owner[None, :]) & before, axis=1, dtype=jnp.int32)
    slots = (owner * CAP + rank)[None, :]
    marks = (entry % 2 * SPAN + vis_pos % SPAN + 1).astype(bf16)
    marks = jnp.broadcast_to(marks[:, None], (count, HD))

    taken = [(0, 0, 0), (0, 1, 0), (0, 1, 1), (1, 0, 0)]
    for hop in range(1, 3):
        taken += [(0, hop + 1, 0), (0, hop + 1, 1), (1, hop, 0), (1, hop, 1)]
    taken += [(1, 3, 0), (1, 3, 1), (0, 4, 0), (1, 4, 0)]
    back = 2 * core - 1
    sources = [
        (((x_hi + flip) % 2) * Z + (z + back * hop + Z) % Z) * 2 + (core + turn) % 2 for flip, hop, turn in taken
    ]
    mine = place
    other = place + 1 - 2 * core
    wanted = jnp.stack([2 * source + s for source in [*sources, mine, other] for s in range(2)])
    spans = jnp.sum(jnp.where(wanted[:, None] == entries[None, :], table[None, :], 0), axis=1).astype(f32)
    key_spans = jnp.broadcast_to(spans[:OWNERS, None], (OWNERS, SPAN))
    query_spans = jnp.broadcast_to(
        spans[OWNERS:].reshape(2, 2, 1), (2, 2, GROUPS * SPAN)
    ).reshape(2, QCOLS)

    row_pos = (span_of.reshape(2, 1) * SPAN + jnp.arange(SPAN, dtype=jnp.int32)[None, :]).reshape(ROWS)
    cosine, sine = rotary_tables(row_pos)

    mail = whole(route_kernel, (SLOTS, COLS + HD), "route_rows", visual, slots, marks)
    mail = lax.all_to_all(
        mail.reshape(OWNERS, CAP, COLS + HD), "ctx", split_axis=0, concat_axis=0, tiled=True
    ).reshape(SLOTS, COLS + HD)
    sequence = whole(place_kernel, (ROWS, COLS), "place_rows", mail, text_rows)
    first = lax.optimization_barrier(gather_first(sequence))
    second = lax.optimization_barrier(gather_second(*first))
    halves = (second[2][:SPAN], second[1][SPAN:])
    weight, gain, cosine, sine, halves = lax.optimization_barrier((weight, gain, cosine, sine, halves))
    third = gather_third(*halves)
    queries, own = project_qkv(
        [sequence, *first, *second, *third], load_weight(weight), gain, cosine, sine
    )

    side = lax.ppermute(own, "ctx", xhi_swap())
    stream = jnp.concatenate([own, lax.ppermute(own, "ctx", core_swap())], axis=0)
    stream, queries = lax.optimization_barrier((stream, queries))
    moved = lax.ppermute(stream, "ctx", z_move())
    other_queries = lax.ppermute(queries, "ctx", core_swap())
    step = functools.partial(attend, key_spans, query_spans, (queries, other_queries))
    states = step([own], 0, None)
    side, unused = lax.optimization_barrier((side, moved))
    side_stream = jnp.concatenate([side, lax.ppermute(side, "ctx", core_swap())], axis=0)
    side_held, side_moved = side, lax.ppermute(side_stream, "ctx", z_move())
    key_row = 2
    for hop in range(1, 4):
        size = 4 * ROWS if hop < 3 else 2 * ROWS
        moved, states = lax.optimization_barrier((moved, states))
        moved_next = lax.ppermute(moved[:size], "ctx", z_move())
        states = step([moved], key_row, states)
        key_row += 4
        states = step([side_held], key_row, states)
        key_row += 2 if hop == 1 else 4
        side_moved, states = lax.optimization_barrier((side_moved, states))
        side_next = lax.ppermute(side_moved[:size], "ctx", z_move())
        moved, side_held, side_moved = moved_next, side_moved, side_next
    states = step([side_held], key_row, states)
    states = step([moved, side_moved], key_row + 4, states)
    kept, given = states
    theirs = lax.ppermute(given, "ctx", core_swap())
    return finish(kept, theirs)


def solution(mesh):
    in_specs = (
        P("ctx", None),
        P("ctx"),
        P("ctx", None),
        P("ctx", "head"),
        P(None, "head"),
        P(),
        P(None, "head", None, None),
    )
    out_specs = P("ctx", "head")
    return jax.shard_map(
        on_device, mesh=mesh, in_specs=in_specs, out_specs=out_specs, check_vma=False
    )
```

profile of v0, /device:TPU:1, one launch (start us, length us, event | category | flops | bytes accessed | tf_op | source)
XLA Modules:
  0.0 119.3 jit_solution(11090122129071920165)
XLA Ops:
  0.0 1.4 %broadcast_in_dim.39 = s32[32,1,2]{2,1,0:T(1,128)} broadcast(s32[2]{0:T(128)} %bitcast.68), dimensions={2} | broadcast | bytes 264 | tf_op jit(solution)/shard_map/broadcast_in_dim | solution.py:326
  1.4 12.6 %all-to-all-start = ((s32[32,1,2]{2,1,0:T(1,128)}), s32[32,1,2]{2,1,0:T(1,128)S(1)}, u32[]{:S(2)}, u32[]{:S(2)}) async-start(s32[32,1,2]{2,1,0:T(1,128)} %broadcast_in_dim.39), calls=%async_computation | async-start | bytes 32768 | tf_op jit(solution)/shard_map/all_to_all | solution.py:325
  14.0 3.3 %convolution_convert_fusion.rows_ref = bf16[160,512]{1,0:T(8,128)(2,1)S(1)} fusion(bf16[160,4608]{1,0:T(8,128)(2,1)S(1)} %copy-done, bf16[4608,512]{1,0:T(8,128)(2,1)} %param.11), kind=kOutput, calls=%fused_computation | convolution fusion | flops 755056640 | bytes 6356992 | tf_op jit(solution)/shard_map/dot_general | solution.py:328
  17.3 6.0 %all-to-all-done = s32[32,1,2]{2,1,0:T(1,128)S(1)} async-done(((s32[32,1,2]{2,1,0:T(1,128)}), s32[32,1,2]{2,1,0:T(1,128)S(1)}, u32[]{:S(2)}, u32[]{:S(2)}) %all-to-all-start) | async-done | bytes 288 | tf_op jit(solution)/shard_map/all_to_all | solution.py:325
  26.0 4.3 %all-to-all-start.1 = ((bf16[32,8,640]{2,1,0:T(8,128)(2,1)}), bf16[32,8,640]{2,1,0:T(8,128)(2,1)S(1)}, u32[]{:S(2)}, u32[]{:S(2)}) async-start(bf16[32,8,640]{2,1,0:T(8,128)(2,1)} %bitcast.39), calls=%async_computation.1 | async-start | bytes 655360 | tf_op jit(solution)/shard_map/all_to_all | solution.py:362
  30.3 14.6 %all-to-all-done.1 = bf16[32,8,640]{2,1,0:T(8,128)(2,1)S(1)} async-done(((bf16[32,8,640]{2,1,0:T(8,128)(2,1)}), bf16[32,8,640]{2,1,0:T(8,128)(2,1)S(1)}, u32[]{:S(2)}, u32[]{:S(2)}) %all-to-all-start.1) | async-done | bytes 327712 | tf_op jit(solution)/shard_map/all_to_all | solution.py:362
  45.7 1.3 %collective-permute-start.1 = (bf16[256,512]{1,0:T(8,128)(2,1)S(1)}, bf16[256,512]{1,0:T(8,128)(2,1)S(1)}, u32[]{:S(2)}, u32[]{:S(2)}) collective-permute-start(bf16[256,512]{1,0:T(8,128)(2,1)S(1)} %place_rows.1.refs_0_), channel_id=1, source_target_pairs={{0,2},{1,3},{2,4},{3,5},{4,6},{5,7},{6,0},{7,1},{8,10},{9,11},{10,... | collective-permute-start | bytes 786440 | tf_op jit(solution)/shard_map/ppermute | solution.py:74
  47.0 1.4 %collective-permute-start.2 = (bf16[256,512]{1,0:T(8,128)(2,1)S(1)}, bf16[256,512]{1,0:T(8,128)(2,1)S(1)}, u32[]{:S(2)}, u32[]{:S(2)}) collective-permute-start(bf16[256,512]{1,0:T(8,128)(2,1)S(1)} %place_rows.1.refs_0_), channel_id=1, source_target_pairs={{0,6},{1,7},{2,0},{3,1},{4,2},{5,3},{6,4},{7,5},{8,14},{9,15},{10,... | collective-permute-start | bytes 786440 | tf_op jit(solution)/shard_map/ppermute | solution.py:75
  48.5 2.9 %collective-permute-done.refs_1_ = bf16[256,512]{1,0:T(8,128)(2,1)S(1)} collective-permute-done((bf16[256,512]{1,0:T(8,128)(2,1)S(1)}, bf16[256,512]{1,0:T(8,128)(2,1)S(1)}, u32[]{:S(2)}, u32[]{:S(2)}) %collective-permute-start) | collective-permute-done | bytes 262176 | tf_op jit(solution)/shard_map/ppermute | solution.py:73
  51.4 1.4 %collective-permute-done.1.refs_2_ = bf16[256,512]{1,0:T(8,128)(2,1)S(1)} collective-permute-done((bf16[256,512]{1,0:T(8,128)(2,1)S(1)}, bf16[256,512]{1,0:T(8,128)(2,1)S(1)}, u32[]{:S(2)}, u32[]{:S(2)}) %collective-permute-start.1) | collective-permute-done | bytes 262176 | tf_op jit(solution)/shard_map/ppermute | solution.py:74
  55.0 1.7 %collective-permute-start.4 = (bf16[256,512]{1,0:T(8,128)(2,1)S(1)}, bf16[256,512]{1,0:T(8,128)(2,1)S(1)}, u32[]{:S(2)}, u32[]{:S(2)}) collective-permute-start(bf16[256,512]{1,0:T(8,128)(2,1)S(1)} %collective-permute-done.refs_1_), channel_id=1, source_target_pairs={{0,6},{1,7},{2,0},{3,1},{4,2},{5,3},{6,4},{7,5},{8,14},{9,15},{10,... | collective-permute-start | bytes 786440 | tf_op jit(solution)/shard_map/ppermute | solution.py:82
  57.3 1.9 %collective-permute-done.3.refs_4_ = bf16[256,512]{1,0:T(8,128)(2,1)S(1)} collective-permute-done((bf16[256,512]{1,0:T(8,128)(2,1)S(1)}, bf16[256,512]{1,0:T(8,128)(2,1)S(1)}, u32[]{:S(2)}, u32[]{:S(2)}) %collective-permute-start.3) | collective-permute-done | bytes 262176 | tf_op jit(solution)/shard_map/ppermute | solution.py:81
  61.6 1.7 %collective-permute-start.7 = (bf16[128,512]{1,0:T(8,128)(2,1)S(1)}, bf16[128,512]{1,0:T(8,128)(2,1)S(1)}, u32[]{:S(2)}, u32[]{:S(2)}) collective-permute-start(bf16[128,512]{1,0:T(8,128)(2,1)S(1)} %slice.23), channel_id=1, source_target_pairs={{0,6},{1,7},{2,0},{3,1},{4,2},{5,3},{6,4},{7,5},{8,14},{9,15},{10,... | collective-permute-start | bytes 393224 | tf_op jit(solution)/shard_map/ppermute | solution.py:88
  63.3 2.8 %copy-done.1 = bf16[4096,1,6,128]{3,0,2,1:T(8,128)(2,1)S(1)} copy-done((bf16[4096,1,6,128]{3,0,2,1:T(8,128)(2,1)S(1)}, bf16[4096,1,6,128]{3,0,2,1:T(8,128)(2,1)}, u32[]{:S(2)}) %copy-start.1) | copy-done | bytes 6291480
  66.8 2.5 %norm_qkv.1 = (bf16[128,1024]{1,0:T(8,128)(2,1)S(1)}, bf16[512,128]{1,0:T(8,128)(2,1)S(1)}) custom-call(bf16[256,512]{1,0:T(8,128)(2,1)S(1)} %place_rows.1.refs_0_, bf16[256,512]{1,0:T(8,128)(2,1)S(1)} %collective-permute-done.refs_1_, bf16[256,512]{1,0:T(8,128)(2,1)S(1)} %collective-permute-done.1.refs_2_, ...), custom_call_target="tpu_custom_call" | custom-call | flops 1610612736 | bytes 8388608 | tf_op jit(solution)/shard_map/norm_qkv/pallas_call | solution.py:179
  69.3 5.6 %collective-permute-start.8 = (bf16[512,128]{1,0:T(8,128)(2,1)S(1)}, bf16[512,128]{1,0:T(8,128)(2,1)S(1)}, u32[]{:S(2)}, u32[]{:S(2)}) collective-permute-start(bf16[512,128]{1,0:T(8,128)(2,1)S(1)} %get-tuple-element.70.refs_4_), channel_id=1, source_target_pairs={{0,8},{8,0},{16,24},{24,16},{32,40},{40,32},{48,56},{56,48},{64,72... | collective-permute-start | bytes 393224 | tf_op jit(solution)/shard_map/ppermute | solution.py:376
  76.3 5.2 %collective-permute-done.12.refs_4_ = bf16[512,128]{1,0:T(8,128)(2,1)S(1)} collective-permute-done((bf16[512,128]{1,0:T(8,128)(2,1)S(1)}, bf16[512,128]{1,0:T(8,128)(2,1)S(1)}, u32[]{:S(2)}, u32[]{:S(2)}) %collective-permute-start.12) | collective-permute-done | bytes 131104 | tf_op jit(solution)/shard_map/ppermute | solution.py:375
  81.7 2.4 %collective-permute-start.13 = (bf16[512,128]{1,0:T(8,128)(2,1)S(1)}, bf16[512,128]{1,0:T(8,128)(2,1)S(1)}, u32[]{:S(2)}, u32[]{:S(2)}) collective-permute-start(bf16[512,128]{1,0:T(8,128)(2,1)S(1)} %collective-permute-done.12.refs_4_), channel_id=1, source_target_pairs={{0,8},{8,0},{16,24},{24,16},{32,40},{40,32},{48,56},{56,48},{64,72... | collective-permute-start | bytes 393224 | tf_op jit(solution)/shard_map/ppermute | solution.py:383
  85.1 1.9 %collective-permute-start.14 = (bf16[1024,128]{1,0:T(8,128)(2,1)S(1)}, bf16[1024,128]{1,0:T(8,128)(2,1)S(1)}, u32[]{:S(2)}, u32[]{:S(2)}) collective-permute-start(bf16[1024,128]{1,0:T(8,128)(2,1)S(1)} %pad_maximum_fusion.1), channel_id=1, source_target_pairs={{0,16},{8,120},{16,32},{24,8},{32,48},{40,24},{48,64},{56,40},{64,... | collective-permute-start | bytes 786440 | tf_op jit(solution)/shard_map/ppermute | solution.py:384
  89.2 1.9 %attend.10 = (f32[136,1024]{1,0:T(8,128)S(1)}, f32[136,1024]{1,0:T(8,128)S(1)}) custom-call(f32[32,128]{1,0:T(8,128)S(1)} %broadcast_in_dim.70.refs_0_, f32[2,1024]{1,0:T(2,128)S(1)} %bitcast.57, bf16[128,1024]{1,0:T(8,128)(2,1)S(1)} %get-tuple-element.72.refs_2_, bf16[128,1024]{1,0:T(8,128)(2,1)S(1)} %collective-permute-done.9.refs_3_, ...), custom_call_target="tpu_custom_call" | custom-call | flops 268435456 | bytes 2359296 | tf_op jit(solution)/shard_map/attend/pallas_call | solution.py:278
  92.1 1.4 %collective-permute-start.16 = (bf16[1024,128]{1,0:T(8,128)(2,1)S(1)}, bf16[1024,128]{1,0:T(8,128)(2,1)S(1)}, u32[]{:S(2)}, u32[]{:S(2)}) collective-permute-start(bf16[1024,128]{1,0:T(8,128)(2,1)S(1)} %collective-permute-done.14.refs_4_), channel_id=1, source_target_pairs={{0,16},{8,120},{16,32},{24,8},{32,48},{40,24},{48,64},{56,40},{64,... | collective-permute-start | bytes 786440 | tf_op jit(solution)/shard_map/ppermute | solution.py:395
  93.8 2.4 %collective-permute-start.15 = (bf16[1024,128]{1,0:T(8,128)(2,1)S(1)}, bf16[1024,128]{1,0:T(8,128)(2,1)S(1)}, u32[]{:S(2)}, u32[]{:S(2)}) collective-permute-start(bf16[1024,128]{1,0:T(8,128)(2,1)S(1)} %collective-permute-done.11.refs_4_), channel_id=1, source_target_pairs={{0,16},{8,120},{16,32},{24,8},{32,48},{40,24},{48,64},{56,40},{64,... | collective-permute-start | bytes 786440 | tf_op jit(solution)/shard_map/ppermute | solution.py:389
  96.3 2.0 %attend.12 = (f32[136,1024]{1,0:T(8,128)S(1)}, f32[136,1024]{1,0:T(8,128)S(1)}) custom-call(f32[32,128]{1,0:T(8,128)S(1)} %broadcast_in_dim.70.refs_0_, f32[2,1024]{1,0:T(2,128)S(1)} %bitcast.59, bf16[128,1024]{1,0:T(8,128)(2,1)S(1)} %get-tuple-element.72.refs_2_, bf16[128,1024]{1,0:T(8,128)(2,1)S(1)} %collective-permute-done.9.refs_3_, ...), custom_call_target="tpu_custom_call" | custom-call | flops 268435456 | bytes 2359296 | tf_op jit(solution)/shard_map/attend/pallas_call | solution.py:278
  98.2 2.0 %attend.13 = (f32[136,1024]{1,0:T(8,128)S(1)}, f32[136,1024]{1,0:T(8,128)S(1)}) custom-call(f32[32,128]{1,0:T(8,128)S(1)} %broadcast_in_dim.70.refs_0_, f32[2,1024]{1,0:T(2,128)S(1)} %bitcast.60, bf16[128,1024]{1,0:T(8,128)(2,1)S(1)} %get-tuple-element.72.refs_2_, bf16[128,1024]{1,0:T(8,128)(2,1)S(1)} %collective-permute-done.9.refs_3_, ...), custom_call_target="tpu_custom_call" | custom-call | flops 268435456 | bytes 2359296 | tf_op jit(solution)/shard_map/attend/pallas_call | solution.py:278
  100.5 2.3 %collective-permute-start.17 = (bf16[512,128]{1,0:T(8,128)(2,1)S(1)}, bf16[512,128]{1,0:T(8,128)(2,1)S(1)}, u32[]{:S(2)}, u32[]{:S(2)}) collective-permute-start(bf16[512,128]{1,0:T(8,128)(2,1)S(1)} %slice.24), channel_id=1, source_target_pairs={{0,16},{8,120},{16,32},{24,8},{32,48},{40,24},{48,64},{56,40},{64,... | collective-permute-start | bytes 393224 | tf_op jit(solution)/shard_map/ppermute | solution.py:389
  102.8 2.0 %attend.14 = (f32[136,1024]{1,0:T(8,128)S(1)}, f32[136,1024]{1,0:T(8,128)S(1)}) custom-call(f32[32,128]{1,0:T(8,128)S(1)} %broadcast_in_dim.70.refs_0_, f32[2,1024]{1,0:T(2,128)S(1)} %bitcast.61, bf16[128,1024]{1,0:T(8,128)(2,1)S(1)} %get-tuple-element.72.refs_2_, bf16[128,1024]{1,0:T(8,128)(2,1)S(1)} %collective-permute-done.9.refs_3_, ...), custom_call_target="tpu_custom_call" | custom-call | flops 268435456 | bytes 2359296 | tf_op jit(solution)/shard_map/attend/pallas_call | solution.py:278
  104.8 1.9 %attend.15 = (f32[136,1024]{1,0:T(8,128)S(1)}, f32[136,1024]{1,0:T(8,128)S(1)}) custom-call(f32[32,128]{1,0:T(8,128)S(1)} %broadcast_in_dim.70.refs_0_, f32[2,1024]{1,0:T(2,128)S(1)} %bitcast.62, bf16[128,1024]{1,0:T(8,128)(2,1)S(1)} %get-tuple-element.72.refs_2_, bf16[128,1024]{1,0:T(8,128)(2,1)S(1)} %collective-permute-done.9.refs_3_, ...), custom_call_target="tpu_custom_call" | custom-call | flops 268435456 | bytes 2359296 | tf_op jit(solution)/shard_map/attend/pallas_call | solution.py:278
  107.1 2.0 %attend.16 = (f32[136,1024]{1,0:T(8,128)S(1)}, f32[136,1024]{1,0:T(8,128)S(1)}) custom-call(f32[32,128]{1,0:T(8,128)S(1)} %broadcast_in_dim.70.refs_0_, f32[2,1024]{1,0:T(2,128)S(1)} %bitcast.63, bf16[128,1024]{1,0:T(8,128)(2,1)S(1)} %get-tuple-element.72.refs_2_, bf16[128,1024]{1,0:T(8,128)(2,1)S(1)} %collective-permute-done.9.refs_3_, ...), custom_call_target="tpu_custom_call" | custom-call | flops 268435456 | bytes 2359296 | tf_op jit(solution)/shard_map/attend/pallas_call | solution.py:278
  109.1 1.8 %collective-permute-done.19.refs_5_ = bf16[512,128]{1,0:T(8,128)(2,1)S(1)} collective-permute-done((bf16[512,128]{1,0:T(8,128)(2,1)S(1)}, bf16[512,128]{1,0:T(8,128)(2,1)S(1)}, u32[]{:S(2)}, u32[]{:S(2)}) %collective-permute-start.19) | collective-permute-done | bytes 131104 | tf_op jit(solution)/shard_map/ppermute | solution.py:395
  110.8 1.9 %attend.17 = (f32[136,1024]{1,0:T(8,128)S(1)}, f32[136,1024]{1,0:T(8,128)S(1)}) custom-call(f32[32,128]{1,0:T(8,128)S(1)} %broadcast_in_dim.70.refs_0_, f32[2,1024]{1,0:T(2,128)S(1)} %bitcast.64, bf16[128,1024]{1,0:T(8,128)(2,1)S(1)} %get-tuple-element.72.refs_2_, bf16[128,1024]{1,0:T(8,128)(2,1)S(1)} %collective-permute-done.9.refs_3_, ...), custom_call_target="tpu_custom_call" | custom-call | flops 536870912 | bytes 2490368 | tf_op jit(solution)/shard_map/attend/pallas_call | solution.py:278
  112.8 4.1 %collective-permute-start.20 = (f32[136,1024]{1,0:T(8,128)S(1)}, f32[136,1024]{1,0:T(8,128)S(1)}, u32[]{:S(2)}, u32[]{:S(2)}) collective-permute-start(f32[136,1024]{1,0:T(8,128)S(1)} %get-tuple-element.110), channel_id=1, source_target_pairs={{0,8},{8,0},{16,24},{24,16},{32,40},{40,32},{48,56},{56,48},{64,72... | collective-permute-start | bytes 1671176 | tf_op jit(solution)/shard_map/ppermute | solution.py:400
  116.8 1.6 %collective-permute-done.20.theirs_ref = f32[136,1024]{1,0:T(8,128)S(1)} collective-permute-done((f32[136,1024]{1,0:T(8,128)S(1)}, f32[136,1024]{1,0:T(8,128)S(1)}, u32[]{:S(2)}, u32[]{:S(2)}) %collective-permute-start.20) | collective-permute-done | bytes 557088 | tf_op jit(solution)/shard_map/ppermute | solution.py:400
  (70 shorter events, 16.9 us)
Async XLA Ops:
  0.0 14.0 %copy-start = (bf16[160,4608]{1,0:T(8,128)(2,1)S(1)}, bf16[160,4608]{1,0:T(8,128)(2,1)}, u32[]{:S(2)}) copy-start(bf16[160,4608]{1,0:T(8,128)(2,1)} %param.7) | copy-start | bytes 4423684
  0.0 30.3 %copy-start.5 = (s32[1,2]{1,0:T(1,128)S(1)}, s32[1,2]{1,0:T(1,128)}, u32[]{:S(2)}) copy-start(s32[1,2]{1,0:T(1,128)} %param.9) | copy-start | bytes 28
  0.0 17.3 %copy-start.4 = (s32[160]{0:T(256)S(1)}, s32[160]{0:T(256)}, u32[]{:S(2)}) copy-start(s32[160]{0:T(256)} %param.8) | copy-start | bytes 1924
  0.0 44.9 %copy-start.2 = (bf16[256,512]{1,0:T(8,128)(2,1)S(1)}, bf16[256,512]{1,0:T(8,128)(2,1)}, u32[]{:S(2)}) copy-start(bf16[256,512]{1,0:T(8,128)(2,1)} %text_ref.1) | copy-start | bytes 786436
  1.4 21.9 %all-to-all-start = ((s32[32,1,2]{2,1,0:T(1,128)}), s32[32,1,2]{2,1,0:T(1,128)S(1)}, u32[]{:S(2)}, u32[]{:S(2)}) async-start(s32[32,1,2]{2,1,0:T(1,128)} %broadcast_in_dim.39), calls=%async_computation | async-start | bytes 32768 | tf_op jit(solution)/shard_map/all_to_all | solution.py:325
  26.0 19.0 %all-to-all-start.1 = ((bf16[32,8,640]{2,1,0:T(8,128)(2,1)}), bf16[32,8,640]{2,1,0:T(8,128)(2,1)S(1)}, u32[]{:S(2)}, u32[]{:S(2)}) async-start(bf16[32,8,640]{2,1,0:T(8,128)(2,1)} %bitcast.39), calls=%async_computation.1 | async-start | bytes 655360 | tf_op jit(solution)/shard_map/all_to_all | solution.py:362
  45.3 6.1 %collective-permute-start = (bf16[256,512]{1,0:T(8,128)(2,1)S(1)}, bf16[256,512]{1,0:T(8,128)(2,1)S(1)}, u32[]{:S(2)}, u32[]{:S(2)}) collective-permute-start(bf16[256,512]{1,0:T(8,128)(2,1)S(1)} %place_rows.1.refs_0_), channel_id=1, source_target_pairs={{0,1},{1,0},{2,3},{3,2},{4,5},{5,4},{6,7},{7,6},{8,9},{9,8},{10,11... | collective-permute-start | bytes 786440 | tf_op jit(solution)/shard_map/ppermute | solution.py:73
  45.7 7.1 %collective-permute-start.1 = (bf16[256,512]{1,0:T(8,128)(2,1)S(1)}, bf16[256,512]{1,0:T(8,128)(2,1)S(1)}, u32[]{:S(2)}, u32[]{:S(2)}) collective-permute-start(bf16[256,512]{1,0:T(8,128)(2,1)S(1)} %place_rows.1.refs_0_), channel_id=1, source_target_pairs={{0,2},{1,3},{2,4},{3,5},{4,6},{5,7},{6,0},{7,1},{8,10},{9,11},{10,... | collective-permute-start | bytes 786440 | tf_op jit(solution)/shard_map/ppermute | solution.py:74
  47.0 5.8 %collective-permute-start.2 = (bf16[256,512]{1,0:T(8,128)(2,1)S(1)}, bf16[256,512]{1,0:T(8,128)(2,1)S(1)}, u32[]{:S(2)}, u32[]{:S(2)}) collective-permute-start(bf16[256,512]{1,0:T(8,128)(2,1)S(1)} %place_rows.1.refs_0_), channel_id=1, source_target_pairs={{0,6},{1,7},{2,0},{3,1},{4,2},{5,3},{6,4},{7,5},{8,14},{9,15},{10,... | collective-permute-start | bytes 786440 | tf_op jit(solution)/shard_map/ppermute | solution.py:75
  52.8 6.4 %collective-permute-start.3 = (bf16[256,512]{1,0:T(8,128)(2,1)S(1)}, bf16[256,512]{1,0:T(8,128)(2,1)S(1)}, u32[]{:S(2)}, u32[]{:S(2)}) collective-permute-start(bf16[256,512]{1,0:T(8,128)(2,1)S(1)} %collective-permute-done.1.refs_2_), channel_id=1, source_target_pairs={{0,2},{1,3},{2,4},{3,5},{4,6},{5,7},{6,0},{7,1},{8,10},{9,11},{10,... | collective-permute-start | bytes 786440 | tf_op jit(solution)/shard_map/ppermute | solution.py:81
  53.8 5.4 %collective-permute-start.5 = (bf16[256,512]{1,0:T(8,128)(2,1)S(1)}, bf16[256,512]{1,0:T(8,128)(2,1)S(1)}, u32[]{:S(2)}, u32[]{:S(2)}) collective-permute-start(bf16[256,512]{1,0:T(8,128)(2,1)S(1)} %collective-permute-done.1.refs_2_), channel_id=1, source_target_pairs={{0,1},{1,0},{2,3},{3,2},{4,5},{5,4},{6,7},{7,6},{8,9},{9,8},{10,11... | collective-permute-start | bytes 786440 | tf_op jit(solution)/shard_map/ppermute | solution.py:83
  55.0 5.5 %collective-permute-start.4 = (bf16[256,512]{1,0:T(8,128)(2,1)S(1)}, bf16[256,512]{1,0:T(8,128)(2,1)S(1)}, u32[]{:S(2)}, u32[]{:S(2)}) collective-permute-start(bf16[256,512]{1,0:T(8,128)(2,1)S(1)} %collective-permute-done.refs_1_), channel_id=1, source_target_pairs={{0,6},{1,7},{2,0},{3,1},{4,2},{5,3},{6,4},{7,5},{8,14},{9,15},{10,... | collective-permute-start | bytes 786440 | tf_op jit(solution)/shard_map/ppermute | solution.py:82
  60.5 6.0 %collective-permute-start.6 = (bf16[128,512]{1,0:T(8,128)(2,1)S(1)}, bf16[128,512]{1,0:T(8,128)(2,1)S(1)}, u32[]{:S(2)}, u32[]{:S(2)}) collective-permute-start(bf16[128,512]{1,0:T(8,128)(2,1)S(1)} %slice.22), channel_id=1, source_target_pairs={{0,2},{1,3},{2,4},{3,5},{4,6},{5,7},{6,0},{7,1},{8,10},{9,11},{10,... | collective-permute-start | bytes 393224 | tf_op jit(solution)/shard_map/ppermute | solution.py:88
  61.6 5.0 %collective-permute-start.7 = (bf16[128,512]{1,0:T(8,128)(2,1)S(1)}, bf16[128,512]{1,0:T(8,128)(2,1)S(1)}, u32[]{:S(2)}, u32[]{:S(2)}) collective-permute-start(bf16[128,512]{1,0:T(8,128)(2,1)S(1)} %slice.23), channel_id=1, source_target_pairs={{0,6},{1,7},{2,0},{3,1},{4,2},{5,3},{6,4},{7,5},{8,14},{9,15},{10,... | collective-permute-start | bytes 393224 | tf_op jit(solution)/shard_map/ppermute | solution.py:88
  63.3 2.8 %copy-start.1 = (bf16[4096,1,6,128]{3,0,2,1:T(8,128)(2,1)S(1)}, bf16[4096,1,6,128]{3,0,2,1:T(8,128)(2,1)}, u32[]{:S(2)}) copy-start(bf16[4096,1,6,128]{3,0,2,1:T(8,128)(2,1)} %param.13) | copy-start | bytes 18874372
  66.1 0.7 copy-start.3
  69.3 6.6 %collective-permute-start.8 = (bf16[512,128]{1,0:T(8,128)(2,1)S(1)}, bf16[512,128]{1,0:T(8,128)(2,1)S(1)}, u32[]{:S(2)}, u32[]{:S(2)}) collective-permute-start(bf16[512,128]{1,0:T(8,128)(2,1)S(1)} %get-tuple-element.70.refs_4_), channel_id=1, source_target_pairs={{0,8},{8,0},{16,24},{24,16},{32,40},{40,32},{48,56},{56,48},{64,72... | collective-permute-start | bytes 393224 | tf_op jit(solution)/shard_map/ppermute | solution.py:376
  75.9 5.8 %collective-permute-start.10 = (bf16[1024,128]{1,0:T(8,128)(2,1)S(1)}, bf16[1024,128]{1,0:T(8,128)(2,1)S(1)}, u32[]{:S(2)}, u32[]{:S(2)}) collective-permute-start(bf16[1024,128]{1,0:T(8,128)(2,1)S(1)} %pad_maximum_fusion), channel_id=1, source_target_pairs={{0,16},{8,120},{16,32},{24,8},{32,48},{40,24},{48,64},{56,40},{64,... | collective-permute-start | bytes 786440 | tf_op jit(solution)/shard_map/ppermute | solution.py:378
  76.2 5.4 %collective-permute-start.12 = (bf16[512,128]{1,0:T(8,128)(2,1)S(1)}, bf16[512,128]{1,0:T(8,128)(2,1)S(1)}, u32[]{:S(2)}, u32[]{:S(2)}) collective-permute-start(bf16[512,128]{1,0:T(8,128)(2,1)S(1)} %get-tuple-element.70.refs_4_), channel_id=1, source_target_pairs={{0,128},{8,136},{16,144},{24,152},{32,160},{40,168},{48,176},{56,1... | collective-permute-start | bytes 393224 | tf_op jit(solution)/shard_map/ppermute | solution.py:375
  81.7 3.4 %collective-permute-start.13 = (bf16[512,128]{1,0:T(8,128)(2,1)S(1)}, bf16[512,128]{1,0:T(8,128)(2,1)S(1)}, u32[]{:S(2)}, u32[]{:S(2)}) collective-permute-start(bf16[512,128]{1,0:T(8,128)(2,1)S(1)} %collective-permute-done.12.refs_4_), channel_id=1, source_target_pairs={{0,8},{8,0},{16,24},{24,16},{32,40},{40,32},{48,56},{56,48},{64,72... | collective-permute-start | bytes 393224 | tf_op jit(solution)/shard_map/ppermute | solution.py:383
  84.6 2.6 %collective-permute-start.9 = (bf16[128,1024]{1,0:T(8,128)(2,1)S(1)}, bf16[128,1024]{1,0:T(8,128)(2,1)S(1)}, u32[]{:S(2)}, u32[]{:S(2)}) collective-permute-start(bf16[128,1024]{1,0:T(8,128)(2,1)S(1)} %get-tuple-element.72.refs_2_), channel_id=1, source_target_pairs={{0,8},{8,0},{16,24},{24,16},{32,40},{40,32},{48,56},{56,48},{64,72... | collective-permute-start | bytes 786440 | tf_op jit(solution)/shard_map/ppermute | solution.py:379
  85.1 6.9 %collective-permute-start.14 = (bf16[1024,128]{1,0:T(8,128)(2,1)S(1)}, bf16[1024,128]{1,0:T(8,128)(2,1)S(1)}, u32[]{:S(2)}, u32[]{:S(2)}) collective-permute-start(bf16[1024,128]{1,0:T(8,128)(2,1)S(1)} %pad_maximum_fusion.1), channel_id=1, source_target_pairs={{0,16},{8,120},{16,32},{24,8},{32,48},{40,24},{48,64},{56,40},{64,... | collective-permute-start | bytes 786440 | tf_op jit(solution)/shard_map/ppermute | solution.py:384
  88.2 5.6 %collective-permute-start.11 = (bf16[1024,128]{1,0:T(8,128)(2,1)S(1)}, bf16[1024,128]{1,0:T(8,128)(2,1)S(1)}, u32[]{:S(2)}, u32[]{:S(2)}) collective-permute-start(bf16[1024,128]{1,0:T(8,128)(2,1)S(1)} %collective-permute-done.10.refs_4_), channel_id=1, source_target_pairs={{0,16},{8,120},{16,32},{24,8},{32,48},{40,24},{48,64},{56,40},{64,... | collective-permute-start | bytes 786440 | tf_op jit(solution)/shard_map/ppermute | solution.py:389
  92.1 8.1 %collective-permute-start.16 = (bf16[1024,128]{1,0:T(8,128)(2,1)S(1)}, bf16[1024,128]{1,0:T(8,128)(2,1)S(1)}, u32[]{:S(2)}, u32[]{:S(2)}) collective-permute-start(bf16[1024,128]{1,0:T(8,128)(2,1)S(1)} %collective-permute-done.14.refs_4_), channel_id=1, source_target_pairs={{0,16},{8,120},{16,32},{24,8},{32,48},{40,24},{48,64},{56,40},{64,... | collective-permute-start | bytes 786440 | tf_op jit(solution)/shard_map/ppermute | solution.py:395
  93.8 6.6 %collective-permute-start.15 = (bf16[1024,128]{1,0:T(8,128)(2,1)S(1)}, bf16[1024,128]{1,0:T(8,128)(2,1)S(1)}, u32[]{:S(2)}, u32[]{:S(2)}) collective-permute-start(bf16[1024,128]{1,0:T(8,128)(2,1)S(1)} %collective-permute-done.11.refs_4_), channel_id=1, source_target_pairs={{0,16},{8,120},{16,32},{24,8},{32,48},{40,24},{48,64},{56,40},{64,... | collective-permute-start | bytes 786440 | tf_op jit(solution)/shard_map/ppermute | solution.py:389
  100.2 6.4 %collective-permute-start.18 = (bf16[1024,128]{1,0:T(8,128)(2,1)S(1)}, bf16[1024,128]{1,0:T(8,128)(2,1)S(1)}, u32[]{:S(2)}, u32[]{:S(2)}) collective-permute-start(bf16[1024,128]{1,0:T(8,128)(2,1)S(1)} %collective-permute-done.16.refs_4_), channel_id=1, source_target_pairs={{0,16},{8,120},{16,32},{24,8},{32,48},{40,24},{48,64},{56,40},{64,... | collective-permute-start | bytes 786440 | tf_op jit(solution)/shard_map/ppermute | solution.py:395
  100.5 8.6 %collective-permute-start.17 = (bf16[512,128]{1,0:T(8,128)(2,1)S(1)}, bf16[512,128]{1,0:T(8,128)(2,1)S(1)}, u32[]{:S(2)}, u32[]{:S(2)}) collective-permute-start(bf16[512,128]{1,0:T(8,128)(2,1)S(1)} %slice.24), channel_id=1, source_target_pairs={{0,16},{8,120},{16,32},{24,8},{32,48},{40,24},{48,64},{56,40},{64,... | collective-permute-start | bytes 393224 | tf_op jit(solution)/shard_map/ppermute | solution.py:389
  106.7 4.2 %collective-permute-start.19 = (bf16[512,128]{1,0:T(8,128)(2,1)S(1)}, bf16[512,128]{1,0:T(8,128)(2,1)S(1)}, u32[]{:S(2)}, u32[]{:S(2)}) collective-permute-start(bf16[512,128]{1,0:T(8,128)(2,1)S(1)} %slice.25), channel_id=1, source_target_pairs={{0,16},{8,120},{16,32},{24,8},{32,48},{40,24},{48,64},{56,40},{64,... | collective-permute-start | bytes 393224 | tf_op jit(solution)/shard_map/ppermute | solution.py:395
  112.8 5.7 %collective-permute-start.20 = (f32[136,1024]{1,0:T(8,128)S(1)}, f32[136,1024]{1,0:T(8,128)S(1)}, u32[]{:S(2)}, u32[]{:S(2)}) collective-permute-start(f32[136,1024]{1,0:T(8,128)S(1)} %get-tuple-element.110), channel_id=1, source_target_pairs={{0,8},{8,0},{16,24},{24,16},{32,40},{40,32},{48,56},{56,48},{64,72... | collective-permute-start | bytes 1671176 | tf_op jit(solution)/shard_map/ppermute | solution.py:400
where the time goes:
time: 120 us; the launch traced here: 119 us
  starting transfers between devices  48.6 us (40%)
  waiting for transfers between devices  38.8 us (32%)
  Pallas kernels  20.8 us (17%)
  local copies, waits for them, and re-layouts  5.55 us (5%)
  matrix products  3.26 us (3%)
  other arithmetic  1.98 us (2%)
    pallas_call x9, Pallas kernels, attend(): pl.pallas_call(functools.partial(attend_kernel, first, count, key_row), o...  15.6 us
    all_to_all x1, waiting for transfers between devices, on_device(): lax.all_to_all(mail.reshape(OWNERS, CAP, COLS + HD), 'ctx', split_axis=0,...  14.6 us
    all_to_all x1, starting transfers between devices, on_device(): lax.all_to_all(jnp.broadcast_to(span_of[:, None, :], (OWNERS, 1, 2)), 'ct...  12.6 us
    all_to_all x1, waiting for transfers between devices, on_device(): lax.all_to_all(jnp.broadcast_to(span_of[:, None, :], (OWNERS, 1, 2)), 'ct...  5.96 us
    ppermute x3, starting transfers between devices, on_device(): moved_next = lax.ppermute(moved[:size], 'ctx', z_move())  5.68 us
    ppermute x1, starting transfers between devices, on_device(): lax.ppermute(own, 'ctx', core_swap())  5.59 us
    ppermute x1, waiting for transfers between devices, on_device(): side = lax.ppermute(own, 'ctx', xhi_swap())  5.25 us
    all_to_all x1, starting transfers between devices, on_device(): lax.all_to_all(mail.reshape(OWNERS, CAP, COLS + HD), 'ctx', split_axis=0,...  4.32 us
  transfers between devices with their start and end apart: 23, of which 14 were waited for; matrix products, arithmetic and copies ran while one was open for 4% of the time, Pallas kernels for 12%

commit v1 on v0

--- a/solution.py
+++ b/solution.py
@@ -26,6 +26,9 @@
 QCOLS = GROUPS * ROWS
 STATE = HD + 8
 
+MESSAGES = [(0, 1), (0, 2), (1, 1), (0, 3), (1, 2), (1, 3)]
+GO_AFTER = {(0, 1): 0, (1, 1): 1, (0, 2): 1, (0, 3): 2, (1, 2): 3, (1, 3): 4}
+
 rope_theta = 500000.0
 norm_eps = 1e-05
 masked_score = -1e30
@@ -43,6 +46,10 @@
 
 def z_move():
     return ctx_perm(lambda i: (i // 16) * 16 + ((i // 2 % Z + 1 - 2 * (i % 2)) % Z) * 2 + i % 2)
+
+
+def z_cross():
+    return [(i, j ^ 16) for i, j in z_move()]
 
 
 def core_swap():
@@ -192,12 +199,32 @@
     )(*blocks, weight, gain, cosine, sine)
 
 
-def route_kernel(rows_ref, slot_ref, mark_ref, out_ref):
+def entry_kernel(span_ref, out_ref):
+    lane = lax.broadcasted_iota(jnp.int32, (OWNERS, HD), 1) - 2 * lax.axis_index("ctx")
+    first = jnp.broadcast_to(span_ref[:, :1], (OWNERS, HD))
+    second = jnp.broadcast_to(span_ref[:, 1:], (OWNERS, HD))
+    out_ref[...] = jnp.where(lane == 0, first, jnp.where(lane == 1, second, 0))
+
+
+def route_kernel(rows_ref, pos_ref, table_ref, out_ref):
     count = rows_ref.shape[0]
-    places = lax.broadcasted_iota(jnp.int32, (SLOTS, count), 0)
-    pick = jnp.where(places == slot_ref[...], 1.0, 0.0).astype(bf16)
-    out_ref[:, :COLS] = jnp.dot(pick, rows_ref[...], preferred_element_type=f32).astype(bf16)
-    out_ref[:, COLS:] = jnp.dot(pick, mark_ref[...], preferred_element_type=f32).astype(bf16)
+    lane = lax.broadcasted_iota(jnp.int32, (count, HD), 1)
+    table = jnp.sum(table_ref[...].astype(f32), axis=0, keepdims=True)
+    matches = (pos_ref[...] // SPAN).astype(f32) == jnp.where(lane < 2 * OWNERS, table, -1.0)
+    entry = jnp.sum(jnp.where(matches, lane.astype(f32), 0.0), axis=1, keepdims=True).astype(jnp.int32)
+    owner = entry // 2
+    same = jnp.where(lane // 2 == owner, 1.0, 0.0).astype(bf16)
+    square = (count, count)
+    before = lax.broadcasted_iota(jnp.int32, square, 1) < lax.broadcasted_iota(jnp.int32, square, 0)
+    ranks = jnp.dot(jnp.where(before, 1.0, 0.0).astype(bf16), same, preferred_element_type=f32)
+    rank = jnp.sum(jnp.where(matches, ranks, 0.0), axis=1, keepdims=True).astype(jnp.int32)
+    slot = owner * CAP + rank
+    pick = jnp.where(lax.broadcasted_iota(jnp.int32, (count, SLOTS), 1) == slot, 1.0, 0.0).astype(bf16)
+    mark = (entry % 2 * SPAN + pos_ref[...] % SPAN + 1).astype(f32)
+    marks = jnp.broadcast_to(mark, (count, HD)).astype(bf16)
+    across = (((0,), (0,)), ((), ()))
+    out_ref[:, :COLS] = lax.dot_general(pick, rows_ref[...], across, preferred_element_type=f32).astype(bf16)
+    out_ref[:, COLS:] = lax.dot_general(pick, marks, across, preferred_element_type=f32).astype(bf16)
 
 
 def place_kernel(mail_ref, text_ref, out_ref):
@@ -224,67 +251,74 @@
     )(*args)
 
 
-def attend_kernel(first, given, key_row, *refs):
+def attend_kernel(first, given, key_row, halves, *refs):
     key_ref, span_ref = refs[:2]
     query_refs = refs[2:4]
     kv_refs = refs[4 : 4 + given]
-    ins, outs = refs[4 + given : -2], refs[-2:]
+    ins, outs = refs[4 + given : -len(halves)], refs[-len(halves) :]
     parts = [(kv, start) for kv in kv_refs for start in range(0, kv.shape[0], 2 * ROWS)]
     keys = jnp.concatenate([kv[start : start + ROWS, :] for kv, start in parts], axis=0)
     values = jnp.concatenate(
         [kv[start + ROWS + s * SPAN : start + ROWS + (s + 1) * SPAN, :] for kv, start in parts for s in range(2)],
         axis=1,
     )
-    count = len(parts)
+    count = 2 * len(parts)
     row = lax.broadcasted_iota(jnp.int32, (SPAN, SPAN), 0).astype(f32)
     lane = lax.broadcasted_iota(jnp.int32, (SPAN, SPAN), 1).astype(f32)
-    for half in range(2):
+    for place, half in enumerate(halves):
         for tile in range(QCOLS // SPAN):
             cols = slice(tile * SPAN, (tile + 1) * SPAN)
             query_span = span_ref[half : half + 1, cols]
             score = jnp.dot(keys, query_refs[half][:, cols], preferred_element_type=f32)
-            pieces = []
-            for j in range(2 * count):
-                key_span = key_ref[key_row + j : key_row + j + 1, :]
-                if first:
-                    allowed = key_span * SPAN + row <= query_span * SPAN + lane
-                else:
-                    allowed = key_span < query_span
-                pieces.append(jnp.where(allowed, score[j * SPAN : (j + 1) * SPAN, :], masked_score))
-            score = jnp.concatenate(pieces, axis=0)
-            high = jnp.max(score, axis=0, keepdims=True)
+            pieces = [score[j * SPAN : (j + 1) * SPAN, :] for j in range(count)]
+            key_spans = [key_ref[key_row + j : key_row + j + 1, :] for j in range(count)]
             if first:
-                new_top = high
+                pieces = [
+                    jnp.where(span * SPAN + row <= query_span * SPAN + lane, piece, masked_score)
+                    for span, piece in zip(key_spans, pieces)
+                ]
+                new_top = functools.reduce(
+                    jnp.maximum, [jnp.max(piece, axis=0, keepdims=True) for piece in pieces]
+                )
+                shifts = [new_top] * count
             else:
-                top = ins[half][HD : HD + 1, cols]
-                new_top = jnp.maximum(top, high)
+                top = ins[place][HD : HD + 1, cols]
+                allowed = [span < query_span for span in key_spans]
+                highs = [
+                    jnp.where(ok, jnp.max(piece, axis=0, keepdims=True), masked_score)
+                    for ok, piece in zip(allowed, pieces)
+                ]
+                new_top = functools.reduce(jnp.maximum, highs, top)
                 shrink = jnp.exp2((top - new_top) * EXP_SCALE)
-            terms = jnp.exp2((score - new_top) * EXP_SCALE)
+                shifts = [jnp.where(ok, new_top, -masked_score) for ok in allowed]
+            terms = jnp.concatenate(
+                [jnp.exp2((piece - shift) * EXP_SCALE) for piece, shift in zip(pieces, shifts)], axis=0
+            )
             total = jnp.sum(terms, axis=0, keepdims=True)
             accum = jnp.dot(values, terms.astype(bf16), preferred_element_type=f32)
             if not first:
-                total = total + ins[half][HD + 1 : HD + 2, cols] * shrink
-                accum = accum + ins[half][:HD, cols] * shrink
-            outs[half][:HD, cols] = accum
-            outs[half][HD : HD + 1, cols] = new_top
-            outs[half][HD + 1 : HD + 2, cols] = total
-            outs[half][HD + 2 : STATE, cols] = jnp.zeros((STATE - HD - 2, SPAN), f32)
-
-
-def attend(key_spans, query_spans, queries, blocks, key_row, states):
+                total = total + ins[place][HD + 1 : HD + 2, cols] * shrink
+                accum = accum + ins[place][:HD, cols] * shrink
+            out = outs[place]
+            out[:HD, cols] = accum
+            out[HD : HD + 1, cols] = new_top
+            out[HD + 1 : HD + 2, cols] = total
+            out[HD + 2 : STATE, cols] = jnp.zeros((STATE - HD - 2, SPAN), f32)
+
+
+def attend(key_spans, query_spans, queries, blocks, key_row, states, halves=(0, 1)):
     first = states is None
-    count = len(blocks)
-    given = () if first else tuple(states)
+    given = () if first else tuple(states[half] for half in halves)
     return pl.pallas_call(
-        functools.partial(attend_kernel, first, count, key_row),
-        out_shape=(jax.ShapeDtypeStruct((STATE, QCOLS), f32),) * 2,
-        in_specs=vmem(4 + count + len(given)),
-        out_specs=tuple(vmem(2)),
+        functools.partial(attend_kernel, first, len(blocks), key_row, halves),
+        out_shape=(jax.ShapeDtypeStruct((STATE, QCOLS), f32),) * len(halves),
+        in_specs=vmem(4 + len(blocks) + len(given)),
+        out_specs=tuple(vmem(len(halves))),
         compiler_params=pltpu.CompilerParams(vmem_limit_bytes=ATTEND_LIMIT),
         cost_estimate=pl.CostEstimate(
-            flops=4 * count * ROWS * 2 * QCOLS * HD,
-            bytes_accessed=count * 4 * ROWS * HD + 2 * STATE * QCOLS * 8,
-            transcendentals=count * ROWS * 2 * QCOLS,
+            flops=16 * ROWS * len(halves) * QCOLS * HD,
+            bytes_accessed=8 * ROWS * HD + 2 * STATE * QCOLS * 8,
+            transcendentals=2 * ROWS * len(halves) * QCOLS,
         ),
         name="attend",
     )(key_spans, query_spans, *queries, *blocks, *given)
@@ -316,32 +350,34 @@
     )(mine, theirs)
 
 
+def send_on(block, before, size):
+    block, unused = lax.optimization_barrier((block, before))
+    return lax.ppermute(block[:size], "ctx", z_move())
+
+
 def on_device(patches, vis_pos, span_of, text_rows, proj_weight, norm_gain, qkv_weight):
     place = lax.axis_index("ctx")
     x_hi, z, core = place // 16, place // 2 % Z, place % 2
     weight = jnp.transpose(qkv_weight, (2, 0, 1, 3)).reshape(GROUPS + 2, HEAD_DEVS, COLS, HD)
     gain = norm_gain.reshape(HEAD_DEVS, 1, COLS)
 
-    table = lax.all_to_all(
-        jnp.broadcast_to(span_of[:, None, :], (OWNERS, 1, 2)), "ctx", split_axis=0, concat_axis=0, tiled=True
-    ).reshape(2 * OWNERS)
+    lanes = jnp.arange(HD, dtype=jnp.int32)[None, :]
+    my_rows = pl.pallas_call(
+        entry_kernel,
+        out_shape=jax.ShapeDtypeStruct((OWNERS, HD), jnp.int32),
+        in_specs=vmem(1),
+        out_specs=pl.BlockSpec(memory_space=pltpu.VMEM),
+        name="my_entry",
+    )(span_of)
+    table_rows = lax.all_to_all(
+        my_rows.reshape(OWNERS, 1, HD), "ctx", split_axis=0, concat_axis=0, tiled=True
+    ).reshape(OWNERS, HD)
     visual = jnp.dot(patches, proj_weight, preferred_element_type=f32).astype(bf16)
 
-    entries = jnp.arange(2 * OWNERS, dtype=jnp.int32)
-    matches = table[None, :] == (vis_pos // SPAN)[:, None]
-    entry = jnp.sum(jnp.where(matches, entries[None, :], 0), axis=1)
-    owner = entry // 2
-    count = vis_pos.shape[0]
-    before = jnp.arange(count)[None, :] < jnp.arange(count)[:, None]
-    rank = jnp.sum((owner[:, None] == owner[None, :]) & before, axis=1, dtype=jnp.int32)
-    slots = (owner * CAP + rank)[None, :]
-    marks = (entry % 2 * SPAN + vis_pos % SPAN + 1).astype(bf16)
-    marks = jnp.broadcast_to(marks[:, None], (count, HD))
-
-    taken = [(0, 0, 0), (0, 1, 0), (0, 1, 1), (1, 0, 0)]
-    for hop in range(1, 3):
-        taken += [(0, hop + 1, 0), (0, hop + 1, 1), (1, hop, 0), (1, hop, 1)]
-    taken += [(1, 3, 0), (1, 3, 1), (0, 4, 0), (1, 4, 0)]
+    taken = [(0, 0, 0)]
+    for flip, hop in MESSAGES:
+        taken += [(flip, hop, 0), (flip, hop, 1)]
+    taken += [(1, 0, 0), (0, 4, 0), (1, 4, 0)]
     back = 2 * core - 1
     sources = [
         (((x_hi + flip) % 2) * Z + (z + back * hop + Z) % Z) * 2 + (core + turn) % 2 for flip, hop, turn in taken
@@ -349,7 +385,8 @@
     mine = place
     other = place + 1 - 2 * core
     wanted = jnp.stack([2 * source + s for source in [*sources, mine, other] for s in range(2)])
-    spans = jnp.sum(jnp.where(wanted[:, None] == entries[None, :], table[None, :], 0), axis=1).astype(f32)
+    table = jnp.sum(table_rows, axis=0)[None, :]
+    spans = jnp.sum(jnp.where(wanted[:, None] == lanes, table, 0), axis=1).astype(f32)
     key_spans = jnp.broadcast_to(spans[:OWNERS, None], (OWNERS, SPAN))
     query_spans = jnp.broadcast_to(
         spans[OWNERS:].reshape(2, 2, 1), (2, 2, GROUPS * SPAN)
@@ -358,7 +395,7 @@
     row_pos = (span_of.reshape(2, 1) * SPAN + jnp.arange(SPAN, dtype=jnp.int32)[None, :]).reshape(ROWS)
     cosine, sine = rotary_tables(row_pos)
 
-    mail = whole(route_kernel, (SLOTS, COLS + HD), "route_rows", visual, slots, marks)
+    mail = whole(route_kernel, (SLOTS, COLS + HD), "route_rows", visual, vis_pos[:, None], table_rows)
     mail = lax.all_to_all(
         mail.reshape(OWNERS, CAP, COLS + HD), "ctx", split_axis=0, concat_axis=0, tiled=True
     ).reshape(SLOTS, COLS + HD)
@@ -372,32 +409,31 @@
         [sequence, *first, *second, *third], load_weight(weight), gain, cosine, sine
     )
 
+    stream = jnp.concatenate([own, lax.ppermute(own, "ctx", core_swap())], axis=0)
+    stream, queries, own = lax.optimization_barrier((stream, queries, own))
+    moved = lax.ppermute(stream, "ctx", z_move())
+    crossed = lax.ppermute(stream, "ctx", z_cross())
+    other_queries = lax.ppermute(queries, "ctx", core_swap())
     side = lax.ppermute(own, "ctx", xhi_swap())
-    stream = jnp.concatenate([own, lax.ppermute(own, "ctx", core_swap())], axis=0)
-    stream, queries = lax.optimization_barrier((stream, queries))
-    moved = lax.ppermute(stream, "ctx", z_move())
-    other_queries = lax.ppermute(queries, "ctx", core_swap())
     step = functools.partial(attend, key_spans, query_spans, (queries, other_queries))
     states = step([own], 0, None)
-    side, unused = lax.optimization_barrier((side, moved))
-    side_stream = jnp.concatenate([side, lax.ppermute(side, "ctx", core_swap())], axis=0)
-    side_held, side_moved = side, lax.ppermute(side_stream, "ctx", z_move())
     key_row = 2
-    for hop in range(1, 4):
-        size = 4 * ROWS if hop < 3 else 2 * ROWS
-        moved, states = lax.optimization_barrier((moved, states))
-        moved_next = lax.ppermute(moved[:size], "ctx", z_move())
-        states = step([moved], key_row, states)
+    history = [states]
+    held = {(0, 1): moved, (1, 1): crossed}
+    for message in MESSAGES:
+        held_now = dict(held)
+        for (line, hop), block in held_now.items():
+            if GO_AFTER.get((line, hop)) == len(history) - 1:
+                held[line, hop + 1] = send_on(block, states, 4 * ROWS if hop < 3 else 2 * ROWS)
+        states = step([held[message]], key_row, states)
         key_row += 4
-        states = step([side_held], key_row, states)
-        key_row += 2 if hop == 1 else 4
-        side_moved, states = lax.optimization_barrier((side_moved, states))
-        side_next = lax.ppermute(side_moved[:size], "ctx", z_move())
-        moved, side_held, side_moved = moved_next, side_moved, side_next
-    states = step([side_held], key_row, states)
-    states = step([moved, side_moved], key_row + 4, states)
-    kept, given = states
+        history.append(states)
+    states = step([side], key_row, states)
+    key_row += 2
+    moved, crossed = held[0, 4], held[1, 4]
+    (given,) = step([moved, crossed], key_row, states, (1,))
     theirs = lax.ppermute(given, "ctx", core_swap())
+    (kept,) = step([moved, crossed], key_row, states, (0,))
     return finish(kept, theirs)
 
 

time: 120 us -> 114 us (0.950)
  waiting for transfers between devices: 38.8 us -> 33.1 us
  starting transfers between devices: 48.6 us -> 51.9 us
  local copies, waits for them, and re-layouts: 5.55 us -> 3.57 us
    ppermute x1, waiting for transfers between devices: 5.25 us -> 0.01 us  [on_device(): side = lax.ppermute(own, 'ctx', xhi_swap())]
    ppermute x1, waiting for transfers between devices: 0.09 us -> 2.85 us  [on_device(): moved = lax.ppermute(stream, 'ctx', z_move())]
    ppermute x8 -> x7, waiting for transfers between devices: 2.82 us -> 0.89 us  [the longest x6 0.82 us: send_on(): return lax.ppermute(block[:size], 'ctx', z_move())]
    ppermute x8 -> x7, starting transfers between devices: 11.9 us -> 13.8 us  [the longest x6 12.4 us: send_on(): return lax.ppermute(block[:size], 'ctx', z_move())]
    broadcast_in_dim x3 -> x1, local copies, waits for them, and re-layouts: 1.58 us -> 0.11 us  [on_device(): vis_pos[:, None]]
    pallas_call x9 -> x11, Pallas kernels: 15.6 us -> 15 us  [the longest x10 13.5 us: attend(): pl.pallas_call(functools.partial(attend_kernel, first, len(blocks), key_r...]
  transfers between devices with their start and end apart: 23 -> 22, of which waited for: 14 -> 12; matrix products, arithmetic and copies ran while one was open for 4% -> 4% of each run, Pallas kernels for 12% -> 11%
where the time goes in v1:
time: 114 us
  starting transfers between devices  51.9 us (46%)
  waiting for transfers between devices  33.1 us (29%)
  Pallas kernels  20.7 us (18%)
  local copies, waits for them, and re-layouts  3.57 us (3%)
  matrix products  3.26 us (3%)
    all_to_all x1, waiting for transfers between devices, on_device(): lax.all_to_all(mail.reshape(OWNERS, CAP, COLS + HD), 'ctx', split_axis=0,...  14.6 us
    pallas_call x10, Pallas kernels, attend(): pl.pallas_call(functools.partial(attend_kernel, first, len(blocks), key_r...  13.5 us
    all_to_all x1, starting transfers between devices, on_device(): lax.all_to_all(my_rows.reshape(OWNERS, 1, HD), 'ctx', split_axis=0, conca...  12.6 us
    ppermute x6, starting transfers between devices, send_on(): return lax.ppermute(block[:size], 'ctx', z_move())  12.4 us
    all_to_all x1, waiting for transfers between devices, on_device(): lax.all_to_all(my_rows.reshape(OWNERS, 1, HD), 'ctx', split_axis=0, conca...  5.86 us
    ppermute x1, starting transfers between devices, on_device(): lax.ppermute(own, 'ctx', core_swap())  5.6 us
    all_to_all x1, starting transfers between devices, on_device(): lax.all_to_all(mail.reshape(OWNERS, CAP, COLS + HD), 'ctx', split_axis=0,...  4.31 us
    ppermute x1, starting transfers between devices, on_device(): theirs = lax.ppermute(given, 'ctx', core_swap())  4.21 us
  transfers between devices with their start and end apart: 22, of which 12 were waited for; matrix products, arithmetic and copies ran while one was open for 4% of the time, Pallas kernels for 11%

profile of v1, /device:TPU:1, one launch (start us, length us, event | category | flops | bytes accessed | tf_op | source)
XLA Modules:
  0.0 113.7 jit_solution(6293527291965342398)
XLA Ops:
  0.0 1.5 %my_entry.1 = s32[32,128]{1,0:T(8,128)} custom-call(s32[1,2]{1,0:T(1,128)} %span_ref.1), custom_call_target="tpu_custom_call" | custom-call | tf_op jit(solution)/shard_map/my_entry/pallas_call | solution.py:365
  1.5 12.6 %all-to-all-start = ((s32[32,1,128]{2,1,0:T(1,128)}), s32[32,1,128]{2,1,0:T(1,128)S(1)}, u32[]{:S(2)}, u32[]{:S(2)}) async-start(s32[32,1,128]{2,1,0:T(1,128)} %bitcast.71), calls=%async_computation | async-start | bytes 32768 | tf_op jit(solution)/shard_map/all_to_all | solution.py:372
  14.1 3.3 %convolution_convert_fusion.rows_ref = bf16[160,512]{1,0:T(8,128)(2,1)S(1)} fusion(bf16[160,4608]{1,0:T(8,128)(2,1)S(1)} %copy-done, bf16[4608,512]{1,0:T(8,128)(2,1)} %param.11), kind=kOutput, calls=%fused_computation | convolution fusion | flops 755056640 | bytes 6356992 | tf_op jit(solution)/shard_map/dot_general | solution.py:375
  17.5 5.9 %all-to-all-done = s32[32,1,128]{2,1,0:T(1,128)S(1)} async-done(((s32[32,1,128]{2,1,0:T(1,128)}), s32[32,1,128]{2,1,0:T(1,128)S(1)}, u32[]{:S(2)}, u32[]{:S(2)}) %all-to-all-start) | async-done | bytes 16416 | tf_op jit(solution)/shard_map/all_to_all | solution.py:372
  23.3 1.5 %route_rows.1 = bf16[256,640]{1,0:T(8,128)(2,1)} custom-call(bf16[160,512]{1,0:T(8,128)(2,1)S(1)} %convolution_convert_fusion.rows_ref, s32[160,1]{1,0:T(8,128)S(1)} %copy.12.pos_ref, s32[32,128]{1,0:T(8,128)S(1)} %bitcast.59), custom_call_target="tpu_custom_call" | custom-call | flops 67108864 | bytes 524288 | tf_op jit(solution)/shard_map/route_rows/pallas_call | solution.py:243
  24.8 4.3 %all-to-all-start.1 = ((bf16[32,8,640]{2,1,0:T(8,128)(2,1)}), bf16[32,8,640]{2,1,0:T(8,128)(2,1)S(1)}, u32[]{:S(2)}, u32[]{:S(2)}) async-start(bf16[32,8,640]{2,1,0:T(8,128)(2,1)} %bitcast.40), calls=%async_computation.1 | async-start | bytes 655360 | tf_op jit(solution)/shard_map/all_to_all | solution.py:399
  29.2 14.6 %all-to-all-done.1 = bf16[32,8,640]{2,1,0:T(8,128)(2,1)S(1)} async-done(((bf16[32,8,640]{2,1,0:T(8,128)(2,1)}), bf16[32,8,640]{2,1,0:T(8,128)(2,1)S(1)}, u32[]{:S(2)}, u32[]{:S(2)}) %all-to-all-start.1) | async-done | bytes 327712 | tf_op jit(solution)/shard_map/all_to_all | solution.py:399
  44.6 1.3 %collective-permute-start.1 = (bf16[256,512]{1,0:T(8,128)(2,1)S(1)}, bf16[256,512]{1,0:T(8,128)(2,1)S(1)}, u32[]{:S(2)}, u32[]{:S(2)}) collective-permute-start(bf16[256,512]{1,0:T(8,128)(2,1)S(1)} %place_rows.1.refs_0_), channel_id=1, source_target_pairs={{0,2},{1,3},{2,4},{3,5},{4,6},{5,7},{6,0},{7,1},{8,10},{9,11},{10,... | collective-permute-start | bytes 786440 | tf_op jit(solution)/shard_map/ppermute | solution.py:81
  45.9 1.4 %collective-permute-start.2 = (bf16[256,512]{1,0:T(8,128)(2,1)S(1)}, bf16[256,512]{1,0:T(8,128)(2,1)S(1)}, u32[]{:S(2)}, u32[]{:S(2)}) collective-permute-start(bf16[256,512]{1,0:T(8,128)(2,1)S(1)} %place_rows.1.refs_0_), channel_id=1, source_target_pairs={{0,6},{1,7},{2,0},{3,1},{4,2},{5,3},{6,4},{7,5},{8,14},{9,15},{10,... | collective-permute-start | bytes 786440 | tf_op jit(solution)/shard_map/ppermute | solution.py:82
  47.4 2.9 %collective-permute-done.refs_1_ = bf16[256,512]{1,0:T(8,128)(2,1)S(1)} collective-permute-done((bf16[256,512]{1,0:T(8,128)(2,1)S(1)}, bf16[256,512]{1,0:T(8,128)(2,1)S(1)}, u32[]{:S(2)}, u32[]{:S(2)}) %collective-permute-start) | collective-permute-done | bytes 262176 | tf_op jit(solution)/shard_map/ppermute | solution.py:80
  50.3 1.4 %collective-permute-done.1.refs_2_ = bf16[256,512]{1,0:T(8,128)(2,1)S(1)} collective-permute-done((bf16[256,512]{1,0:T(8,128)(2,1)S(1)}, bf16[256,512]{1,0:T(8,128)(2,1)S(1)}, u32[]{:S(2)}, u32[]{:S(2)}) %collective-permute-start.1) | collective-permute-done | bytes 262176 | tf_op jit(solution)/shard_map/ppermute | solution.py:81
  52.7 1.2 %collective-permute-start.5 = (bf16[256,512]{1,0:T(8,128)(2,1)S(1)}, bf16[256,512]{1,0:T(8,128)(2,1)S(1)}, u32[]{:S(2)}, u32[]{:S(2)}) collective-permute-start(bf16[256,512]{1,0:T(8,128)(2,1)S(1)} %collective-permute-done.1.refs_2_), channel_id=1, source_target_pairs={{0,1},{1,0},{2,3},{3,2},{4,5},{5,4},{6,7},{7,6},{8,9},{9,8},{10,11... | collective-permute-start | bytes 786440 | tf_op jit(solution)/shard_map/ppermute | solution.py:90
  53.8 1.7 %collective-permute-start.4 = (bf16[256,512]{1,0:T(8,128)(2,1)S(1)}, bf16[256,512]{1,0:T(8,128)(2,1)S(1)}, u32[]{:S(2)}, u32[]{:S(2)}) collective-permute-start(bf16[256,512]{1,0:T(8,128)(2,1)S(1)} %collective-permute-done.refs_1_), channel_id=1, source_target_pairs={{0,6},{1,7},{2,0},{3,1},{4,2},{5,3},{6,4},{7,5},{8,14},{9,15},{10,... | collective-permute-start | bytes 786440 | tf_op jit(solution)/shard_map/ppermute | solution.py:89
  56.2 1.9 %collective-permute-done.3.refs_4_ = bf16[256,512]{1,0:T(8,128)(2,1)S(1)} collective-permute-done((bf16[256,512]{1,0:T(8,128)(2,1)S(1)}, bf16[256,512]{1,0:T(8,128)(2,1)S(1)}, u32[]{:S(2)}, u32[]{:S(2)}) %collective-permute-start.3) | collective-permute-done | bytes 262176 | tf_op jit(solution)/shard_map/ppermute | solution.py:88
  58.1 1.3 %collective-permute-done.4.refs_5_ = bf16[256,512]{1,0:T(8,128)(2,1)S(1)} collective-permute-done((bf16[256,512]{1,0:T(8,128)(2,1)S(1)}, bf16[256,512]{1,0:T(8,128)(2,1)S(1)}, u32[]{:S(2)}, u32[]{:S(2)}) %collective-permute-start.4) | collective-permute-done | bytes 262176 | tf_op jit(solution)/shard_map/ppermute | solution.py:89
  59.4 1.1 collective-permute-start.6
  60.5 1.7 %collective-permute-start.7 = (bf16[128,512]{1,0:T(8,128)(2,1)S(1)}, bf16[128,512]{1,0:T(8,128)(2,1)S(1)}, u32[]{:S(2)}, u32[]{:S(2)}) collective-permute-start(bf16[128,512]{1,0:T(8,128)(2,1)S(1)} %slice.23), channel_id=1, source_target_pairs={{0,6},{1,7},{2,0},{3,1},{4,2},{5,3},{6,4},{7,5},{8,14},{9,15},{10,... | collective-permute-start | bytes 393224 | tf_op jit(solution)/shard_map/ppermute | solution.py:95
  62.1 2.8 %copy-done.1 = bf16[4096,1,6,128]{3,0,2,1:T(8,128)(2,1)S(1)} copy-done((bf16[4096,1,6,128]{3,0,2,1:T(8,128)(2,1)S(1)}, bf16[4096,1,6,128]{3,0,2,1:T(8,128)(2,1)}, u32[]{:S(2)}) %copy-start.1) | copy-done | bytes 6291480
  65.6 2.5 %norm_qkv.1 = (bf16[128,1024]{1,0:T(8,128)(2,1)S(1)}, bf16[512,128]{1,0:T(8,128)(2,1)S(1)}) custom-call(bf16[256,512]{1,0:T(8,128)(2,1)S(1)} %place_rows.1.refs_0_, bf16[256,512]{1,0:T(8,128)(2,1)S(1)} %collective-permute-done.refs_1_, bf16[256,512]{1,0:T(8,128)(2,1)S(1)} %collective-permute-done.1.refs_2_, ...), custom_call_target="tpu_custom_call" | custom-call | flops 1610612736 | bytes 8388608 | tf_op jit(solution)/shard_map/norm_qkv/pallas_call | solution.py:186
  68.1 5.6 %collective-permute-start.8 = (bf16[512,128]{1,0:T(8,128)(2,1)S(1)}, bf16[512,128]{1,0:T(8,128)(2,1)S(1)}, u32[]{:S(2)}, u32[]{:S(2)}) collective-permute-start(bf16[512,128]{1,0:T(8,128)(2,1)S(1)} %get-tuple-element.60.refs_4_), channel_id=1, source_target_pairs={{0,8},{8,0},{16,24},{24,16},{32,40},{40,32},{48,56},{56,48},{64,72... | collective-permute-start | bytes 393224 | tf_op jit(solution)/shard_map/ppermute | solution.py:412
  75.8 1.5 %collective-permute-start.14 = (bf16[1024,128]{1,0:T(8,128)(2,1)S(1)}, bf16[1024,128]{1,0:T(8,128)(2,1)S(1)}, u32[]{:S(2)}, u32[]{:S(2)}) collective-permute-start(bf16[1024,128]{1,0:T(8,128)(2,1)S(1)} %pad_maximum_fusion), channel_id=1, source_target_pairs={{0,144},{8,248},{16,160},{24,136},{32,176},{40,152},{48,192},{56,1... | collective-permute-start | bytes 786440 | tf_op jit(solution)/shard_map/ppermute | solution.py:415
  78.4 2.8 %collective-permute-done.10.refs_4_ = bf16[1024,128]{1,0:T(8,128)(2,1)S(1)} collective-permute-done((bf16[1024,128]{1,0:T(8,128)(2,1)S(1)}, bf16[1024,128]{1,0:T(8,128)(2,1)S(1)}, u32[]{:S(2)}, u32[]{:S(2)}) %collective-permute-start.10) | collective-permute-done | bytes 262176 | tf_op jit(solution)/shard_map/ppermute | solution.py:414
  82.2 1.6 %attend.11 = (f32[136,1024]{1,0:T(8,128)S(1)}, f32[136,1024]{1,0:T(8,128)S(1)}) custom-call(f32[32,128]{1,0:T(8,128)S(1)} %broadcast_in_dim.36.refs_0_, f32[2,1024]{1,0:T(2,128)S(1)} %bitcast.62, bf16[128,1024]{1,0:T(8,128)(2,1)S(1)} %get-tuple-element.58.refs_2_, bf16[128,1024]{1,0:T(8,128)(2,1)S(1)} %collective-permute-done.9.refs_3_, ...), custom_call_target="tpu_custom_call" | custom-call | flops 1073741824 | bytes 2490368 | tf_op jit(solution)/shard_map/attend/pallas_call | solution.py:312
  83.8 5.0 %collective-permute-start.15 = (bf16[1024,128]{1,0:T(8,128)(2,1)S(1)}, bf16[1024,128]{1,0:T(8,128)(2,1)S(1)}, u32[]{:S(2)}, u32[]{:S(2)}) collective-permute-start(bf16[1024,128]{1,0:T(8,128)(2,1)S(1)} %collective-permute-done.14.refs_4_), channel_id=1, source_target_pairs={{0,16},{8,120},{16,32},{24,8},{32,48},{40,24},{48,64},{56,40},{64,... | collective-permute-start | bytes 786440 | tf_op jit(solution)/shard_map/ppermute | solution.py:355
  88.9 1.5 %attend.12 = (f32[136,1024]{1,0:T(8,128)S(1)}, f32[136,1024]{1,0:T(8,128)S(1)}) custom-call(f32[32,128]{1,0:T(8,128)S(1)} %broadcast_in_dim.36.refs_0_, f32[2,1024]{1,0:T(2,128)S(1)} %bitcast.63, bf16[128,1024]{1,0:T(8,128)(2,1)S(1)} %get-tuple-element.58.refs_2_, bf16[128,1024]{1,0:T(8,128)(2,1)S(1)} %collective-permute-done.9.refs_3_, ...), custom_call_target="tpu_custom_call" | custom-call | flops 1073741824 | bytes 2490368 | tf_op jit(solution)/shard_map/attend/pallas_call | solution.py:312
  90.4 1.6 %attend.13 = (f32[136,1024]{1,0:T(8,128)S(1)}, f32[136,1024]{1,0:T(8,128)S(1)}) custom-call(f32[32,128]{1,0:T(8,128)S(1)} %broadcast_in_dim.36.refs_0_, f32[2,1024]{1,0:T(2,128)S(1)} %bitcast.64, bf16[128,1024]{1,0:T(8,128)(2,1)S(1)} %get-tuple-element.58.refs_2_, bf16[128,1024]{1,0:T(8,128)(2,1)S(1)} %collective-permute-done.9.refs_3_, ...), custom_call_target="tpu_custom_call" | custom-call | flops 1073741824 | bytes 2490368 | tf_op jit(solution)/shard_map/attend/pallas_call | solution.py:312
  92.1 3.1 %collective-permute-start.16 = (bf16[1024,128]{1,0:T(8,128)(2,1)S(1)}, bf16[1024,128]{1,0:T(8,128)(2,1)S(1)}, u32[]{:S(2)}, u32[]{:S(2)}) collective-permute-start(bf16[1024,128]{1,0:T(8,128)(2,1)S(1)} %collective-permute-done.15.refs_4_), channel_id=1, source_target_pairs={{0,16},{8,120},{16,32},{24,8},{32,48},{40,24},{48,64},{56,40},{64,... | collective-permute-start | bytes 786440 | tf_op jit(solution)/shard_map/ppermute | solution.py:355
  96.2 1.6 %attend.14 = (f32[136,1024]{1,0:T(8,128)S(1)}, f32[136,1024]{1,0:T(8,128)S(1)}) custom-call(f32[32,128]{1,0:T(8,128)S(1)} %broadcast_in_dim.36.refs_0_, f32[2,1024]{1,0:T(2,128)S(1)} %bitcast.65, bf16[128,1024]{1,0:T(8,128)(2,1)S(1)} %get-tuple-element.58.refs_2_, bf16[128,1024]{1,0:T(8,128)(2,1)S(1)} %collective-permute-done.9.refs_3_, ...), custom_call_target="tpu_custom_call" | custom-call | flops 1073741824 | bytes 2490368 | tf_op jit(solution)/shard_map/attend/pallas_call | solution.py:312
  98.6 3.2 %collective-permute-start.17 = (bf16[512,128]{1,0:T(8,128)(2,1)S(1)}, bf16[512,128]{1,0:T(8,128)(2,1)S(1)}, u32[]{:S(2)}, u32[]{:S(2)}) collective-permute-start(bf16[512,128]{1,0:T(8,128)(2,1)S(1)} %slice.25), channel_id=1, source_target_pairs={{0,16},{8,120},{16,32},{24,8},{32,48},{40,24},{48,64},{56,40},{64,... | collective-permute-start | bytes 393224 | tf_op jit(solution)/shard_map/ppermute | solution.py:355
  101.9 1.6 %attend.15 = (f32[136,1024]{1,0:T(8,128)S(1)}, f32[136,1024]{1,0:T(8,128)S(1)}) custom-call(f32[32,128]{1,0:T(8,128)S(1)} %broadcast_in_dim.36.refs_0_, f32[2,1024]{1,0:T(2,128)S(1)} %bitcast.66, bf16[128,1024]{1,0:T(8,128)(2,1)S(1)} %get-tuple-element.58.refs_2_, bf16[128,1024]{1,0:T(8,128)(2,1)S(1)} %collective-permute-done.9.refs_3_, ...), custom_call_target="tpu_custom_call" | custom-call | flops 1073741824 | bytes 2490368 | tf_op jit(solution)/shard_map/attend/pallas_call | solution.py:312
  103.5 1.6 %attend.16 = (f32[136,1024]{1,0:T(8,128)S(1)}, f32[136,1024]{1,0:T(8,128)S(1)}) custom-call(f32[32,128]{1,0:T(8,128)S(1)} %broadcast_in_dim.36.refs_0_, f32[2,1024]{1,0:T(2,128)S(1)} %bitcast.67, bf16[128,1024]{1,0:T(8,128)(2,1)S(1)} %get-tuple-element.58.refs_2_, bf16[128,1024]{1,0:T(8,128)(2,1)S(1)} %collective-permute-done.9.refs_3_, ...), custom_call_target="tpu_custom_call" | custom-call | flops 1073741824 | bytes 2490368 | tf_op jit(solution)/shard_map/attend/pallas_call | solution.py:312
  107.1 4.2 %collective-permute-start.19 = (f32[136,1024]{1,0:T(8,128)S(1)}, f32[136,1024]{1,0:T(8,128)S(1)}, u32[]{:S(2)}, u32[]{:S(2)}) collective-permute-start(f32[136,1024]{1,0:T(8,128)S(1)} %attend.19), channel_id=1, source_target_pairs={{0,8},{8,0},{16,24},{24,16},{32,40},{40,32},{48,56},{56,48},{64,72... | collective-permute-start | bytes 1671176 | tf_op jit(solution)/shard_map/ppermute | solution.py:435
  (61 shorter events, 13.9 us)
Async XLA Ops:
  0.0 14.1 %copy-start = (bf16[160,4608]{1,0:T(8,128)(2,1)S(1)}, bf16[160,4608]{1,0:T(8,128)(2,1)}, u32[]{:S(2)}) copy-start(bf16[160,4608]{1,0:T(8,128)(2,1)} %param.7) | copy-start | bytes 4423684
  0.0 29.2 %copy-start.5 = (s32[1,2]{1,0:T(1,128)S(1)}, s32[1,2]{1,0:T(1,128)}, u32[]{:S(2)}) copy-start(s32[1,2]{1,0:T(1,128)} %span_ref.1) | copy-start | bytes 28
  0.0 17.3 %copy-start.4 = (s32[160]{0:T(256)S(1)}, s32[160]{0:T(256)}, u32[]{:S(2)}) copy-start(s32[160]{0:T(256)} %param.8) | copy-start | bytes 1924
  0.0 43.8 %copy-start.2 = (bf16[256,512]{1,0:T(8,128)(2,1)S(1)}, bf16[256,512]{1,0:T(8,128)(2,1)}, u32[]{:S(2)}) copy-start(bf16[256,512]{1,0:T(8,128)(2,1)} %text_ref.1) | copy-start | bytes 786436
  1.5 21.9 %all-to-all-start = ((s32[32,1,128]{2,1,0:T(1,128)}), s32[32,1,128]{2,1,0:T(1,128)S(1)}, u32[]{:S(2)}, u32[]{:S(2)}) async-start(s32[32,1,128]{2,1,0:T(1,128)} %bitcast.71), calls=%async_computation | async-start | bytes 32768 | tf_op jit(solution)/shard_map/all_to_all | solution.py:372
  24.8 18.9 %all-to-all-start.1 = ((bf16[32,8,640]{2,1,0:T(8,128)(2,1)}), bf16[32,8,640]{2,1,0:T(8,128)(2,1)S(1)}, u32[]{:S(2)}, u32[]{:S(2)}) async-start(bf16[32,8,640]{2,1,0:T(8,128)(2,1)} %bitcast.40), calls=%async_computation.1 | async-start | bytes 655360 | tf_op jit(solution)/shard_map/all_to_all | solution.py:399
  44.2 6.1 %collective-permute-start = (bf16[256,512]{1,0:T(8,128)(2,1)S(1)}, bf16[256,512]{1,0:T(8,128)(2,1)S(1)}, u32[]{:S(2)}, u32[]{:S(2)}) collective-permute-start(bf16[256,512]{1,0:T(8,128)(2,1)S(1)} %place_rows.1.refs_0_), channel_id=1, source_target_pairs={{0,1},{1,0},{2,3},{3,2},{4,5},{5,4},{6,7},{7,6},{8,9},{9,8},{10,11... | collective-permute-start | bytes 786440 | tf_op jit(solution)/shard_map/ppermute | solution.py:80
  44.6 7.1 %collective-permute-start.1 = (bf16[256,512]{1,0:T(8,128)(2,1)S(1)}, bf16[256,512]{1,0:T(8,128)(2,1)S(1)}, u32[]{:S(2)}, u32[]{:S(2)}) collective-permute-start(bf16[256,512]{1,0:T(8,128)(2,1)S(1)} %place_rows.1.refs_0_), channel_id=1, source_target_pairs={{0,2},{1,3},{2,4},{3,5},{4,6},{5,7},{6,0},{7,1},{8,10},{9,11},{10,... | collective-permute-start | bytes 786440 | tf_op jit(solution)/shard_map/ppermute | solution.py:81
  45.9 5.8 %collective-permute-start.2 = (bf16[256,512]{1,0:T(8,128)(2,1)S(1)}, bf16[256,512]{1,0:T(8,128)(2,1)S(1)}, u32[]{:S(2)}, u32[]{:S(2)}) collective-permute-start(bf16[256,512]{1,0:T(8,128)(2,1)S(1)} %place_rows.1.refs_0_), channel_id=1, source_target_pairs={{0,6},{1,7},{2,0},{3,1},{4,2},{5,3},{6,4},{7,5},{8,14},{9,15},{10,... | collective-permute-start | bytes 786440 | tf_op jit(solution)/shard_map/ppermute | solution.py:82
  51.7 6.4 %collective-permute-start.3 = (bf16[256,512]{1,0:T(8,128)(2,1)S(1)}, bf16[256,512]{1,0:T(8,128)(2,1)S(1)}, u32[]{:S(2)}, u32[]{:S(2)}) collective-permute-start(bf16[256,512]{1,0:T(8,128)(2,1)S(1)} %collective-permute-done.1.refs_2_), channel_id=1, source_target_pairs={{0,2},{1,3},{2,4},{3,5},{4,6},{5,7},{6,0},{7,1},{8,10},{9,11},{10,... | collective-permute-start | bytes 786440 | tf_op jit(solution)/shard_map/ppermute | solution.py:88
  52.7 5.4 %collective-permute-start.5 = (bf16[256,512]{1,0:T(8,128)(2,1)S(1)}, bf16[256,512]{1,0:T(8,128)(2,1)S(1)}, u32[]{:S(2)}, u32[]{:S(2)}) collective-permute-start(bf16[256,512]{1,0:T(8,128)(2,1)S(1)} %collective-permute-done.1.refs_2_), channel_id=1, source_target_pairs={{0,1},{1,0},{2,3},{3,2},{4,5},{5,4},{6,7},{7,6},{8,9},{9,8},{10,11... | collective-permute-start | bytes 786440 | tf_op jit(solution)/shard_map/ppermute | solution.py:90
  53.8 5.5 %collective-permute-start.4 = (bf16[256,512]{1,0:T(8,128)(2,1)S(1)}, bf16[256,512]{1,0:T(8,128)(2,1)S(1)}, u32[]{:S(2)}, u32[]{:S(2)}) collective-permute-start(bf16[256,512]{1,0:T(8,128)(2,1)S(1)} %collective-permute-done.refs_1_), channel_id=1, source_target_pairs={{0,6},{1,7},{2,0},{3,1},{4,2},{5,3},{6,4},{7,5},{8,14},{9,15},{10,... | collective-permute-start | bytes 786440 | tf_op jit(solution)/shard_map/ppermute | solution.py:89
  59.4 6.0 %collective-permute-start.6 = (bf16[128,512]{1,0:T(8,128)(2,1)S(1)}, bf16[128,512]{1,0:T(8,128)(2,1)S(1)}, u32[]{:S(2)}, u32[]{:S(2)}) collective-permute-start(bf16[128,512]{1,0:T(8,128)(2,1)S(1)} %slice.22), channel_id=1, source_target_pairs={{0,2},{1,3},{2,4},{3,5},{4,6},{5,7},{6,0},{7,1},{8,10},{9,11},{10,... | collective-permute-start | bytes 393224 | tf_op jit(solution)/shard_map/ppermute | solution.py:95
  60.5 5.0 %collective-permute-start.7 = (bf16[128,512]{1,0:T(8,128)(2,1)S(1)}, bf16[128,512]{1,0:T(8,128)(2,1)S(1)}, u32[]{:S(2)}, u32[]{:S(2)}) collective-permute-start(bf16[128,512]{1,0:T(8,128)(2,1)S(1)} %slice.23), channel_id=1, source_target_pairs={{0,6},{1,7},{2,0},{3,1},{4,2},{5,3},{6,4},{7,5},{8,14},{9,15},{10,... | collective-permute-start | bytes 393224 | tf_op jit(solution)/shard_map/ppermute | solution.py:95
  62.1 2.8 %copy-start.1 = (bf16[4096,1,6,128]{3,0,2,1:T(8,128)(2,1)S(1)}, bf16[4096,1,6,128]{3,0,2,1:T(8,128)(2,1)}, u32[]{:S(2)}) copy-start(bf16[4096,1,6,128]{3,0,2,1:T(8,128)(2,1)} %param.13) | copy-start | bytes 18874372
  64.9 0.7 copy-start.3
  68.1 6.6 %collective-permute-start.8 = (bf16[512,128]{1,0:T(8,128)(2,1)S(1)}, bf16[512,128]{1,0:T(8,128)(2,1)S(1)}, u32[]{:S(2)}, u32[]{:S(2)}) collective-permute-start(bf16[512,128]{1,0:T(8,128)(2,1)S(1)} %get-tuple-element.60.refs_4_), channel_id=1, source_target_pairs={{0,8},{8,0},{16,24},{24,16},{32,40},{40,32},{48,56},{56,48},{64,72... | collective-permute-start | bytes 393224 | tf_op jit(solution)/shard_map/ppermute | solution.py:412
  74.8 2.5 %collective-permute-start.9 = (bf16[128,1024]{1,0:T(8,128)(2,1)S(1)}, bf16[128,1024]{1,0:T(8,128)(2,1)S(1)}, u32[]{:S(2)}, u32[]{:S(2)}) collective-permute-start(bf16[128,1024]{1,0:T(8,128)(2,1)S(1)} %get-tuple-element.58.refs_2_), channel_id=1, source_target_pairs={{0,8},{8,0},{16,24},{24,16},{32,40},{40,32},{48,56},{56,48},{64,72... | collective-permute-start | bytes 786440 | tf_op jit(solution)/shard_map/ppermute | solution.py:416
  75.7 5.5 %collective-permute-start.10 = (bf16[1024,128]{1,0:T(8,128)(2,1)S(1)}, bf16[1024,128]{1,0:T(8,128)(2,1)S(1)}, u32[]{:S(2)}, u32[]{:S(2)}) collective-permute-start(bf16[1024,128]{1,0:T(8,128)(2,1)S(1)} %pad_maximum_fusion), channel_id=1, source_target_pairs={{0,16},{8,120},{16,32},{24,8},{32,48},{40,24},{48,64},{56,40},{64,... | collective-permute-start | bytes 786440 | tf_op jit(solution)/shard_map/ppermute | solution.py:414
  75.8 8.0 %collective-permute-start.14 = (bf16[1024,128]{1,0:T(8,128)(2,1)S(1)}, bf16[1024,128]{1,0:T(8,128)(2,1)S(1)}, u32[]{:S(2)}, u32[]{:S(2)}) collective-permute-start(bf16[1024,128]{1,0:T(8,128)(2,1)S(1)} %pad_maximum_fusion), channel_id=1, source_target_pairs={{0,144},{8,248},{16,160},{24,136},{32,176},{40,152},{48,192},{56,1... | collective-permute-start | bytes 786440 | tf_op jit(solution)/shard_map/ppermute | solution.py:415
  81.2 7.6 %collective-permute-start.11 = (bf16[1024,128]{1,0:T(8,128)(2,1)S(1)}, bf16[1024,128]{1,0:T(8,128)(2,1)S(1)}, u32[]{:S(2)}, u32[]{:S(2)}) collective-permute-start(bf16[1024,128]{1,0:T(8,128)(2,1)S(1)} %collective-permute-done.10.refs_4_), channel_id=1, source_target_pairs={{0,16},{8,120},{16,32},{24,8},{32,48},{40,24},{48,64},{56,40},{64,... | collective-permute-start | bytes 786440 | tf_op jit(solution)/shard_map/ppermute | solution.py:355
  83.8 8.3 %collective-permute-start.15 = (bf16[1024,128]{1,0:T(8,128)(2,1)S(1)}, bf16[1024,128]{1,0:T(8,128)(2,1)S(1)}, u32[]{:S(2)}, u32[]{:S(2)}) collective-permute-start(bf16[1024,128]{1,0:T(8,128)(2,1)S(1)} %collective-permute-done.14.refs_4_), channel_id=1, source_target_pairs={{0,16},{8,120},{16,32},{24,8},{32,48},{40,24},{48,64},{56,40},{64,... | collective-permute-start | bytes 786440 | tf_op jit(solution)/shard_map/ppermute | solution.py:355
  88.8 7.4 %collective-permute-start.12 = (bf16[1024,128]{1,0:T(8,128)(2,1)S(1)}, bf16[1024,128]{1,0:T(8,128)(2,1)S(1)}, u32[]{:S(2)}, u32[]{:S(2)}) collective-permute-start(bf16[1024,128]{1,0:T(8,128)(2,1)S(1)} %collective-permute-done.11.refs_4_), channel_id=1, source_target_pairs={{0,16},{8,120},{16,32},{24,8},{32,48},{40,24},{48,64},{56,40},{64,... | collective-permute-start | bytes 786440 | tf_op jit(solution)/shard_map/ppermute | solution.py:355
  92.1 6.4 %collective-permute-start.16 = (bf16[1024,128]{1,0:T(8,128)(2,1)S(1)}, bf16[1024,128]{1,0:T(8,128)(2,1)S(1)}, u32[]{:S(2)}, u32[]{:S(2)}) collective-permute-start(bf16[1024,128]{1,0:T(8,128)(2,1)S(1)} %collective-permute-done.15.refs_4_), channel_id=1, source_target_pairs={{0,16},{8,120},{16,32},{24,8},{32,48},{40,24},{48,64},{56,40},{64,... | collective-permute-start | bytes 786440 | tf_op jit(solution)/shard_map/ppermute | solution.py:355
  95.2 9.9 %collective-permute-start.18 = (bf16[512,128]{1,0:T(8,128)(2,1)S(1)}, bf16[512,128]{1,0:T(8,128)(2,1)S(1)}, u32[]{:S(2)}, u32[]{:S(2)}) collective-permute-start(bf16[512,128]{1,0:T(8,128)(2,1)S(1)} %get-tuple-element.60.refs_4_), channel_id=1, source_target_pairs={{0,128},{8,136},{16,144},{24,152},{32,160},{40,168},{48,176},{56,1... | collective-permute-start | bytes 393224 | tf_op jit(solution)/shard_map/ppermute | solution.py:417
  98.6 7.5 %collective-permute-start.17 = (bf16[512,128]{1,0:T(8,128)(2,1)S(1)}, bf16[512,128]{1,0:T(8,128)(2,1)S(1)}, u32[]{:S(2)}, u32[]{:S(2)}) collective-permute-start(bf16[512,128]{1,0:T(8,128)(2,1)S(1)} %slice.25), channel_id=1, source_target_pairs={{0,16},{8,120},{16,32},{24,8},{32,48},{40,24},{48,64},{56,40},{64,... | collective-permute-start | bytes 393224 | tf_op jit(solution)/shard_map/ppermute | solution.py:355
  101.8 4.3 %collective-permute-start.13 = (bf16[512,128]{1,0:T(8,128)(2,1)S(1)}, bf16[512,128]{1,0:T(8,128)(2,1)S(1)}, u32[]{:S(2)}, u32[]{:S(2)}) collective-permute-start(bf16[512,128]{1,0:T(8,128)(2,1)S(1)} %slice.24), channel_id=1, source_target_pairs={{0,16},{8,120},{16,32},{24,8},{32,48},{40,24},{48,64},{56,40},{64,... | collective-permute-start | bytes 393224 | tf_op jit(solution)/shard_map/ppermute | solution.py:355
  107.1 5.8 %collective-permute-start.19 = (f32[136,1024]{1,0:T(8,128)S(1)}, f32[136,1024]{1,0:T(8,128)S(1)}, u32[]{:S(2)}, u32[]{:S(2)}) collective-permute-start(f32[136,1024]{1,0:T(8,128)S(1)} %attend.19), channel_id=1, source_target_pairs={{0,8},{8,0},{16,24},{24,16},{32,40},{40,32},{48,56},{56,48},{64,72... | collective-permute-start | bytes 1671176 | tf_op jit(solution)/shard_map/ppermute | solution.py:435

commit v2 on v1

--- a/solution.py
+++ b/solution.py
@@ -27,7 +27,7 @@
 STATE = HD + 8
 
 MESSAGES = [(0, 1), (0, 2), (1, 1), (0, 3), (1, 2), (1, 3)]
-GO_AFTER = {(0, 1): 0, (1, 1): 1, (0, 2): 1, (0, 3): 2, (1, 2): 3, (1, 3): 4}
+SENDS = [(0, 0, 1, 2), (1, 0, 2, 3), (1, 1, 1, 2), (1, 1, 1, 3), (2, 0, 3, 4), (3, 1, 2, 4)]
 
 rope_theta = 500000.0
 norm_eps = 1e-05
@@ -44,8 +44,8 @@
     return [(i, move(i)) for i in range(OWNERS)]
 
 
-def z_move():
-    return ctx_perm(lambda i: (i // 16) * 16 + ((i // 2 % Z + 1 - 2 * (i % 2)) % Z) * 2 + i % 2)
+def z_move(steps=1):
+    return ctx_perm(lambda i: (i // 16) * 16 + ((i // 2 % Z + steps * (1 - 2 * (i % 2))) % Z) * 2 + i % 2)
 
 
 def z_cross():
@@ -350,9 +350,9 @@
     )(mine, theirs)
 
 
-def send_on(block, before, size):
+def send_on(block, before, size, steps):
     block, unused = lax.optimization_barrier((block, before))
-    return lax.ppermute(block[:size], "ctx", z_move())
+    return lax.ppermute(block[:size], "ctx", z_move(steps))
 
 
 def on_device(patches, vis_pos, span_of, text_rows, proj_weight, norm_gain, qkv_weight):
@@ -421,10 +421,9 @@
     history = [states]
     held = {(0, 1): moved, (1, 1): crossed}
     for message in MESSAGES:
-        held_now = dict(held)
-        for (line, hop), block in held_now.items():
-            if GO_AFTER.get((line, hop)) == len(history) - 1:
-                held[line, hop + 1] = send_on(block, states, 4 * ROWS if hop < 3 else 2 * ROWS)
+        for after, line, old, new in SENDS:
+            if after == len(history) - 1:
+                held[line, new] = send_on(held[line, old], states, 4 * ROWS if new < 4 else 2 * ROWS, new - old)
         states = step([held[message]], key_row, states)
         key_row += 4
         history.append(states)

time: 114 us -> 112 us (0.982)
  starting transfers between devices: 51.9 us -> 49.8 us
    ppermute x1, starting transfers between devices: 4.21 us -> 1.39 us  [on_device(): theirs = lax.ppermute(given, 'ctx', core_swap())]
  transfers between devices with their start and end apart: 22 -> 22, of which waited for: 12 -> 11; matrix products, arithmetic and copies ran while one was open for 4% -> 4% of each run, Pallas kernels for 11% -> 12%
where the time goes in v2:
time: 112 us
  starting transfers between devices  49.8 us (44%)
  waiting for transfers between devices  33.3 us (30%)
  Pallas kernels  20.8 us (19%)
  local copies, waits for them, and re-layouts  3.57 us (3%)
  matrix products  3.26 us (3%)
    all_to_all x1, waiting for transfers between devices, on_device(): lax.all_to_all(mail.reshape(OWNERS, CAP, COLS + HD), 'ctx', split_axis=0,...  14.6 us
    pallas_call x10, Pallas kernels, attend(): pl.pallas_call(functools.partial(attend_kernel, first, len(blocks), key_r...  13.6 us
    all_to_all x1, starting transfers between devices, on_device(): lax.all_to_all(my_rows.reshape(OWNERS, 1, HD), 'ctx', split_axis=0, conca...  12.6 us
    ppermute x6, starting transfers between devices, send_on(): return lax.ppermute(block[:size], 'ctx', z_move(steps))  12.2 us
    all_to_all x1, waiting for transfers between devices, on_device(): lax.all_to_all(my_rows.reshape(OWNERS, 1, HD), 'ctx', split_axis=0, conca...  5.86 us
    ppermute x1, starting transfers between devices, on_device(): lax.ppermute(own, 'ctx', core_swap())  5.6 us
    all_to_all x1, starting transfers between devices, on_device(): lax.all_to_all(mail.reshape(OWNERS, CAP, COLS + HD), 'ctx', split_axis=0,...  4.31 us
    dot_general x1, matrix products, on_device(): jnp.dot(patches, proj_weight, preferred_element_type=f32).astype(bf16)  3.26 us
  transfers between devices with their start and end apart: 22, of which 11 were waited for; matrix products, arithmetic and copies ran while one was open for 4% of the time, Pallas kernels for 12%

profile of v2, /device:TPU:1, one launch (start us, length us, event | category | flops | bytes accessed | tf_op | source)
XLA Modules:
  0.0 112.0 jit_solution(8360253929789250429)
XLA Ops:
  0.0 1.5 %my_entry.1 = s32[32,128]{1,0:T(8,128)} custom-call(s32[1,2]{1,0:T(1,128)} %span_ref.1), custom_call_target="tpu_custom_call" | custom-call | tf_op jit(solution)/shard_map/my_entry/pallas_call | solution.py:365
  1.5 12.6 %all-to-all-start = ((s32[32,1,128]{2,1,0:T(1,128)}), s32[32,1,128]{2,1,0:T(1,128)S(1)}, u32[]{:S(2)}, u32[]{:S(2)}) async-start(s32[32,1,128]{2,1,0:T(1,128)} %bitcast.71), calls=%async_computation | async-start | bytes 32768 | tf_op jit(solution)/shard_map/all_to_all | solution.py:372
  14.1 3.3 %convolution_convert_fusion.rows_ref = bf16[160,512]{1,0:T(8,128)(2,1)S(1)} fusion(bf16[160,4608]{1,0:T(8,128)(2,1)S(1)} %copy-done, bf16[4608,512]{1,0:T(8,128)(2,1)} %param.11), kind=kOutput, calls=%fused_computation | convolution fusion | flops 755056640 | bytes 6356992 | tf_op jit(solution)/shard_map/dot_general | solution.py:375
  17.5 5.9 %all-to-all-done = s32[32,1,128]{2,1,0:T(1,128)S(1)} async-done(((s32[32,1,128]{2,1,0:T(1,128)}), s32[32,1,128]{2,1,0:T(1,128)S(1)}, u32[]{:S(2)}, u32[]{:S(2)}) %all-to-all-start) | async-done | bytes 16416 | tf_op jit(solution)/shard_map/all_to_all | solution.py:372
  23.3 1.5 %route_rows.1 = bf16[256,640]{1,0:T(8,128)(2,1)} custom-call(bf16[160,512]{1,0:T(8,128)(2,1)S(1)} %convolution_convert_fusion.rows_ref, s32[160,1]{1,0:T(8,128)S(1)} %copy.12.pos_ref, s32[32,128]{1,0:T(8,128)S(1)} %bitcast.59), custom_call_target="tpu_custom_call" | custom-call | flops 67108864 | bytes 524288 | tf_op jit(solution)/shard_map/route_rows/pallas_call | solution.py:243
  24.8 4.3 %all-to-all-start.1 = ((bf16[32,8,640]{2,1,0:T(8,128)(2,1)}), bf16[32,8,640]{2,1,0:T(8,128)(2,1)S(1)}, u32[]{:S(2)}, u32[]{:S(2)}) async-start(bf16[32,8,640]{2,1,0:T(8,128)(2,1)} %bitcast.40), calls=%async_computation.1 | async-start | bytes 655360 | tf_op jit(solution)/shard_map/all_to_all | solution.py:399
  29.2 14.6 %all-to-all-done.1 = bf16[32,8,640]{2,1,0:T(8,128)(2,1)S(1)} async-done(((bf16[32,8,640]{2,1,0:T(8,128)(2,1)}), bf16[32,8,640]{2,1,0:T(8,128)(2,1)S(1)}, u32[]{:S(2)}, u32[]{:S(2)}) %all-to-all-start.1) | async-done | bytes 327712 | tf_op jit(solution)/shard_map/all_to_all | solution.py:399
  44.6 1.3 %collective-permute-start.1 = (bf16[256,512]{1,0:T(8,128)(2,1)S(1)}, bf16[256,512]{1,0:T(8,128)(2,1)S(1)}, u32[]{:S(2)}, u32[]{:S(2)}) collective-permute-start(bf16[256,512]{1,0:T(8,128)(2,1)S(1)} %place_rows.1.refs_0_), channel_id=1, source_target_pairs={{0,2},{1,3},{2,4},{3,5},{4,6},{5,7},{6,0},{7,1},{8,10},{9,11},{10,... | collective-permute-start | bytes 786440 | tf_op jit(solution)/shard_map/ppermute | solution.py:81
  45.9 1.4 %collective-permute-start.2 = (bf16[256,512]{1,0:T(8,128)(2,1)S(1)}, bf16[256,512]{1,0:T(8,128)(2,1)S(1)}, u32[]{:S(2)}, u32[]{:S(2)}) collective-permute-start(bf16[256,512]{1,0:T(8,128)(2,1)S(1)} %place_rows.1.refs_0_), channel_id=1, source_target_pairs={{0,6},{1,7},{2,0},{3,1},{4,2},{5,3},{6,4},{7,5},{8,14},{9,15},{10,... | collective-permute-start | bytes 786440 | tf_op jit(solution)/shard_map/ppermute | solution.py:82
  47.4 2.9 %collective-permute-done.refs_1_ = bf16[256,512]{1,0:T(8,128)(2,1)S(1)} collective-permute-done((bf16[256,512]{1,0:T(8,128)(2,1)S(1)}, bf16[256,512]{1,0:T(8,128)(2,1)S(1)}, u32[]{:S(2)}, u32[]{:S(2)}) %collective-permute-start) | collective-permute-done | bytes 262176 | tf_op jit(solution)/shard_map/ppermute | solution.py:80
  50.3 1.4 %collective-permute-done.1.refs_2_ = bf16[256,512]{1,0:T(8,128)(2,1)S(1)} collective-permute-done((bf16[256,512]{1,0:T(8,128)(2,1)S(1)}, bf16[256,512]{1,0:T(8,128)(2,1)S(1)}, u32[]{:S(2)}, u32[]{:S(2)}) %collective-permute-start.1) | collective-permute-done | bytes 262176 | tf_op jit(solution)/shard_map/ppermute | solution.py:81
  52.7 1.2 %collective-permute-start.5 = (bf16[256,512]{1,0:T(8,128)(2,1)S(1)}, bf16[256,512]{1,0:T(8,128)(2,1)S(1)}, u32[]{:S(2)}, u32[]{:S(2)}) collective-permute-start(bf16[256,512]{1,0:T(8,128)(2,1)S(1)} %collective-permute-done.1.refs_2_), channel_id=1, source_target_pairs={{0,1},{1,0},{2,3},{3,2},{4,5},{5,4},{6,7},{7,6},{8,9},{9,8},{10,11... | collective-permute-start | bytes 786440 | tf_op jit(solution)/shard_map/ppermute | solution.py:90
  53.8 1.7 %collective-permute-start.4 = (bf16[256,512]{1,0:T(8,128)(2,1)S(1)}, bf16[256,512]{1,0:T(8,128)(2,1)S(1)}, u32[]{:S(2)}, u32[]{:S(2)}) collective-permute-start(bf16[256,512]{1,0:T(8,128)(2,1)S(1)} %collective-permute-done.refs_1_), channel_id=1, source_target_pairs={{0,6},{1,7},{2,0},{3,1},{4,2},{5,3},{6,4},{7,5},{8,14},{9,15},{10,... | collective-permute-start | bytes 786440 | tf_op jit(solution)/shard_map/ppermute | solution.py:89
  56.2 1.9 %collective-permute-done.3.refs_4_ = bf16[256,512]{1,0:T(8,128)(2,1)S(1)} collective-permute-done((bf16[256,512]{1,0:T(8,128)(2,1)S(1)}, bf16[256,512]{1,0:T(8,128)(2,1)S(1)}, u32[]{:S(2)}, u32[]{:S(2)}) %collective-permute-start.3) | collective-permute-done | bytes 262176 | tf_op jit(solution)/shard_map/ppermute | solution.py:88
  58.1 1.3 %collective-permute-done.4.refs_5_ = bf16[256,512]{1,0:T(8,128)(2,1)S(1)} collective-permute-done((bf16[256,512]{1,0:T(8,128)(2,1)S(1)}, bf16[256,512]{1,0:T(8,128)(2,1)S(1)}, u32[]{:S(2)}, u32[]{:S(2)}) %collective-permute-start.4) | collective-permute-done | bytes 262176 | tf_op jit(solution)/shard_map/ppermute | solution.py:89
  60.5 1.7 %collective-permute-start.7 = (bf16[128,512]{1,0:T(8,128)(2,1)S(1)}, bf16[128,512]{1,0:T(8,128)(2,1)S(1)}, u32[]{:S(2)}, u32[]{:S(2)}) collective-permute-start(bf16[128,512]{1,0:T(8,128)(2,1)S(1)} %slice.23), channel_id=1, source_target_pairs={{0,6},{1,7},{2,0},{3,1},{4,2},{5,3},{6,4},{7,5},{8,14},{9,15},{10,... | collective-permute-start | bytes 393224 | tf_op jit(solution)/shard_map/ppermute | solution.py:95
  62.1 2.8 %copy-done.1 = bf16[4096,1,6,128]{3,0,2,1:T(8,128)(2,1)S(1)} copy-done((bf16[4096,1,6,128]{3,0,2,1:T(8,128)(2,1)S(1)}, bf16[4096,1,6,128]{3,0,2,1:T(8,128)(2,1)}, u32[]{:S(2)}) %copy-start.1) | copy-done | bytes 6291480
  65.6 2.5 %norm_qkv.1 = (bf16[128,1024]{1,0:T(8,128)(2,1)S(1)}, bf16[512,128]{1,0:T(8,128)(2,1)S(1)}) custom-call(bf16[256,512]{1,0:T(8,128)(2,1)S(1)} %place_rows.1.refs_0_, bf16[256,512]{1,0:T(8,128)(2,1)S(1)} %collective-permute-done.refs_1_, bf16[256,512]{1,0:T(8,128)(2,1)S(1)} %collective-permute-done.1.refs_2_, ...), custom_call_target="tpu_custom_call" | custom-call | flops 1610612736 | bytes 8388608 | tf_op jit(solution)/shard_map/norm_qkv/pallas_call | solution.py:186
  68.1 5.6 %collective-permute-start.8 = (bf16[512,128]{1,0:T(8,128)(2,1)S(1)}, bf16[512,128]{1,0:T(8,128)(2,1)S(1)}, u32[]{:S(2)}, u32[]{:S(2)}) collective-permute-start(bf16[512,128]{1,0:T(8,128)(2,1)S(1)} %get-tuple-element.59.refs_4_), channel_id=1, source_target_pairs={{0,8},{8,0},{16,24},{24,16},{32,40},{40,32},{48,56},{56,48},{64,72... | collective-permute-start | bytes 393224 | tf_op jit(solution)/shard_map/ppermute | solution.py:412
  75.8 1.5 %collective-permute-start.14 = (bf16[1024,128]{1,0:T(8,128)(2,1)S(1)}, bf16[1024,128]{1,0:T(8,128)(2,1)S(1)}, u32[]{:S(2)}, u32[]{:S(2)}) collective-permute-start(bf16[1024,128]{1,0:T(8,128)(2,1)S(1)} %pad_maximum_fusion), channel_id=1, source_target_pairs={{0,144},{8,248},{16,160},{24,136},{32,176},{40,152},{48,192},{56,1... | collective-permute-start | bytes 786440 | tf_op jit(solution)/shard_map/ppermute | solution.py:415
  78.4 2.8 %collective-permute-done.10.refs_4_ = bf16[1024,128]{1,0:T(8,128)(2,1)S(1)} collective-permute-done((bf16[1024,128]{1,0:T(8,128)(2,1)S(1)}, bf16[1024,128]{1,0:T(8,128)(2,1)S(1)}, u32[]{:S(2)}, u32[]{:S(2)}) %collective-permute-start.10) | collective-permute-done | bytes 262176 | tf_op jit(solution)/shard_map/ppermute | solution.py:414
  82.2 1.6 %attend.11 = (f32[136,1024]{1,0:T(8,128)S(1)}, f32[136,1024]{1,0:T(8,128)S(1)}) custom-call(f32[32,128]{1,0:T(8,128)S(1)} %broadcast_in_dim.36.refs_0_, f32[2,1024]{1,0:T(2,128)S(1)} %bitcast.62, bf16[128,1024]{1,0:T(8,128)(2,1)S(1)} %get-tuple-element.57.refs_2_, bf16[128,1024]{1,0:T(8,128)(2,1)S(1)} %collective-permute-done.9.refs_3_, ...), custom_call_target="tpu_custom_call" | custom-call | flops 1073741824 | bytes 2490368 | tf_op jit(solution)/shard_map/attend/pallas_call | solution.py:312
  83.8 5.0 %collective-permute-start.15 = (bf16[1024,128]{1,0:T(8,128)(2,1)S(1)}, bf16[1024,128]{1,0:T(8,128)(2,1)S(1)}, u32[]{:S(2)}, u32[]{:S(2)}) collective-permute-start(bf16[1024,128]{1,0:T(8,128)(2,1)S(1)} %collective-permute-done.14.refs_4_), channel_id=1, source_target_pairs={{0,16},{8,120},{16,32},{24,8},{32,48},{40,24},{48,64},{56,40},{64,... | collective-permute-start | bytes 786440 | tf_op jit(solution)/shard_map/ppermute | solution.py:355
  88.9 1.9 %collective-permute-start.17 = (bf16[512,128]{1,0:T(8,128)(2,1)S(1)}, bf16[512,128]{1,0:T(8,128)(2,1)S(1)}, u32[]{:S(2)}, u32[]{:S(2)}) collective-permute-start(bf16[512,128]{1,0:T(8,128)(2,1)S(1)} %get-tuple-element.59.refs_4_), channel_id=1, source_target_pairs={{0,128},{8,136},{16,144},{24,152},{32,160},{40,168},{48,176},{56,1... | collective-permute-start | bytes 393224 | tf_op jit(solution)/shard_map/ppermute | solution.py:417
  91.1 1.6 %attend.12 = (f32[136,1024]{1,0:T(8,128)S(1)}, f32[136,1024]{1,0:T(8,128)S(1)}) custom-call(f32[32,128]{1,0:T(8,128)S(1)} %broadcast_in_dim.36.refs_0_, f32[2,1024]{1,0:T(2,128)S(1)} %bitcast.63, bf16[128,1024]{1,0:T(8,128)(2,1)S(1)} %get-tuple-element.57.refs_2_, bf16[128,1024]{1,0:T(8,128)(2,1)S(1)} %collective-permute-done.9.refs_3_, ...), custom_call_target="tpu_custom_call" | custom-call | flops 1073741824 | bytes 2490368 | tf_op jit(solution)/shard_map/attend/pallas_call | solution.py:312
  92.7 1.6 %attend.13 = (f32[136,1024]{1,0:T(8,128)S(1)}, f32[136,1024]{1,0:T(8,128)S(1)}) custom-call(f32[32,128]{1,0:T(8,128)S(1)} %broadcast_in_dim.36.refs_0_, f32[2,1024]{1,0:T(2,128)S(1)} %bitcast.64, bf16[128,1024]{1,0:T(8,128)(2,1)S(1)} %get-tuple-element.57.refs_2_, bf16[128,1024]{1,0:T(8,128)(2,1)S(1)} %collective-permute-done.9.refs_3_, ...), custom_call_target="tpu_custom_call" | custom-call | flops 1073741824 | bytes 2490368 | tf_op jit(solution)/shard_map/attend/pallas_call | solution.py:312
  94.3 2.4 %collective-permute-start.16 = (bf16[512,128]{1,0:T(8,128)(2,1)S(1)}, bf16[512,128]{1,0:T(8,128)(2,1)S(1)}, u32[]{:S(2)}, u32[]{:S(2)}) collective-permute-start(bf16[512,128]{1,0:T(8,128)(2,1)S(1)} %slice.25), channel_id=1, source_target_pairs={{0,32},{8,104},{16,48},{24,120},{32,64},{40,8},{48,80},{56,24},{64... | collective-permute-start | bytes 393224 | tf_op jit(solution)/shard_map/ppermute | solution.py:355
  97.8 3.6 %collective-permute-start.13 = (bf16[512,128]{1,0:T(8,128)(2,1)S(1)}, bf16[512,128]{1,0:T(8,128)(2,1)S(1)}, u32[]{:S(2)}, u32[]{:S(2)}) collective-permute-start(bf16[512,128]{1,0:T(8,128)(2,1)S(1)} %slice.24), channel_id=1, source_target_pairs={{0,16},{8,120},{16,32},{24,8},{32,48},{40,24},{48,64},{56,40},{64,... | collective-permute-start | bytes 393224 | tf_op jit(solution)/shard_map/ppermute | solution.py:355
  101.3 1.6 %attend.14 = (f32[136,1024]{1,0:T(8,128)S(1)}, f32[136,1024]{1,0:T(8,128)S(1)}) custom-call(f32[32,128]{1,0:T(8,128)S(1)} %broadcast_in_dim.36.refs_0_, f32[2,1024]{1,0:T(2,128)S(1)} %bitcast.65, bf16[128,1024]{1,0:T(8,128)(2,1)S(1)} %get-tuple-element.57.refs_2_, bf16[128,1024]{1,0:T(8,128)(2,1)S(1)} %collective-permute-done.9.refs_3_, ...), custom_call_target="tpu_custom_call" | custom-call | flops 1073741824 | bytes 2490368 | tf_op jit(solution)/shard_map/attend/pallas_call | solution.py:312
  102.9 1.6 %attend.15 = (f32[136,1024]{1,0:T(8,128)S(1)}, f32[136,1024]{1,0:T(8,128)S(1)}) custom-call(f32[32,128]{1,0:T(8,128)S(1)} %broadcast_in_dim.36.refs_0_, f32[2,1024]{1,0:T(2,128)S(1)} %bitcast.66, bf16[128,1024]{1,0:T(8,128)(2,1)S(1)} %get-tuple-element.57.refs_2_, bf16[128,1024]{1,0:T(8,128)(2,1)S(1)} %collective-permute-done.9.refs_3_, ...), custom_call_target="tpu_custom_call" | custom-call | flops 1073741824 | bytes 2490368 | tf_op jit(solution)/shard_map/attend/pallas_call | solution.py:312
  104.6 1.6 %attend.16 = (f32[136,1024]{1,0:T(8,128)S(1)}, f32[136,1024]{1,0:T(8,128)S(1)}) custom-call(f32[32,128]{1,0:T(8,128)S(1)} %broadcast_in_dim.36.refs_0_, f32[2,1024]{1,0:T(2,128)S(1)} %bitcast.67, bf16[128,1024]{1,0:T(8,128)(2,1)S(1)} %get-tuple-element.57.refs_2_, bf16[128,1024]{1,0:T(8,128)(2,1)S(1)} %collective-permute-done.9.refs_3_, ...), custom_call_target="tpu_custom_call" | custom-call | flops 1073741824 | bytes 2490368 | tf_op jit(solution)/shard_map/attend/pallas_call | solution.py:312
  108.1 1.4 %collective-permute-start.19 = (f32[136,1024]{1,0:T(8,128)S(1)}, f32[136,1024]{1,0:T(8,128)S(1)}, u32[]{:S(2)}, u32[]{:S(2)}) collective-permute-start(f32[136,1024]{1,0:T(8,128)S(1)} %attend.19), channel_id=1, source_target_pairs={{0,8},{8,0},{16,24},{24,16},{32,40},{40,32},{48,56},{56,48},{64,72... | collective-permute-start | bytes 1671176 | tf_op jit(solution)/shard_map/ppermute | solution.py:434
  (61 shorter events, 14.4 us)
Async XLA Ops:
  0.0 14.1 %copy-start = (bf16[160,4608]{1,0:T(8,128)(2,1)S(1)}, bf16[160,4608]{1,0:T(8,128)(2,1)}, u32[]{:S(2)}) copy-start(bf16[160,4608]{1,0:T(8,128)(2,1)} %param.7) | copy-start | bytes 4423684
  0.0 29.2 %copy-start.5 = (s32[1,2]{1,0:T(1,128)S(1)}, s32[1,2]{1,0:T(1,128)}, u32[]{:S(2)}) copy-start(s32[1,2]{1,0:T(1,128)} %span_ref.1) | copy-start | bytes 28
  0.0 17.3 %copy-start.4 = (s32[160]{0:T(256)S(1)}, s32[160]{0:T(256)}, u32[]{:S(2)}) copy-start(s32[160]{0:T(256)} %param.8) | copy-start | bytes 1924
  0.0 43.8 %copy-start.2 = (bf16[256,512]{1,0:T(8,128)(2,1)S(1)}, bf16[256,512]{1,0:T(8,128)(2,1)}, u32[]{:S(2)}) copy-start(bf16[256,512]{1,0:T(8,128)(2,1)} %text_ref.1) | copy-start | bytes 786436
  1.5 21.9 %all-to-all-start = ((s32[32,1,128]{2,1,0:T(1,128)}), s32[32,1,128]{2,1,0:T(1,128)S(1)}, u32[]{:S(2)}, u32[]{:S(2)}) async-start(s32[32,1,128]{2,1,0:T(1,128)} %bitcast.71), calls=%async_computation | async-start | bytes 32768 | tf_op jit(solution)/shard_map/all_to_all | solution.py:372
  24.8 18.9 %all-to-all-start.1 = ((bf16[32,8,640]{2,1,0:T(8,128)(2,1)}), bf16[32,8,640]{2,1,0:T(8,128)(2,1)S(1)}, u32[]{:S(2)}, u32[]{:S(2)}) async-start(bf16[32,8,640]{2,1,0:T(8,128)(2,1)} %bitcast.40), calls=%async_computation.1 | async-start | bytes 655360 | tf_op jit(solution)/shard_map/all_to_all | solution.py:399
  44.2 6.1 %collective-permute-start = (bf16[256,512]{1,0:T(8,128)(2,1)S(1)}, bf16[256,512]{1,0:T(8,128)(2,1)S(1)}, u32[]{:S(2)}, u32[]{:S(2)}) collective-permute-start(bf16[256,512]{1,0:T(8,128)(2,1)S(1)} %place_rows.1.refs_0_), channel_id=1, source_target_pairs={{0,1},{1,0},{2,3},{3,2},{4,5},{5,4},{6,7},{7,6},{8,9},{9,8},{10,11... | collective-permute-start | bytes 786440 | tf_op jit(solution)/shard_map/ppermute | solution.py:80
  44.6 7.1 %collective-permute-start.1 = (bf16[256,512]{1,0:T(8,128)(2,1)S(1)}, bf16[256,512]{1,0:T(8,128)(2,1)S(1)}, u32[]{:S(2)}, u32[]{:S(2)}) collective-permute-start(bf16[256,512]{1,0:T(8,128)(2,1)S(1)} %place_rows.1.refs_0_), channel_id=1, source_target_pairs={{0,2},{1,3},{2,4},{3,5},{4,6},{5,7},{6,0},{7,1},{8,10},{9,11},{10,... | collective-permute-start | bytes 786440 | tf_op jit(solution)/shard_map/ppermute | solution.py:81
  45.9 5.8 %collective-permute-start.2 = (bf16[256,512]{1,0:T(8,128)(2,1)S(1)}, bf16[256,512]{1,0:T(8,128)(2,1)S(1)}, u32[]{:S(2)}, u32[]{:S(2)}) collective-permute-start(bf16[256,512]{1,0:T(8,128)(2,1)S(1)} %place_rows.1.refs_0_), channel_id=1, source_target_pairs={{0,6},{1,7},{2,0},{3,1},{4,2},{5,3},{6,4},{7,5},{8,14},{9,15},{10,... | collective-permute-start | bytes 786440 | tf_op jit(solution)/shard_map/ppermute | solution.py:82
  51.7 6.4 %collective-permute-start.3 = (bf16[256,512]{1,0:T(8,128)(2,1)S(1)}, bf16[256,512]{1,0:T(8,128)(2,1)S(1)}, u32[]{:S(2)}, u32[]{:S(2)}) collective-permute-start(bf16[256,512]{1,0:T(8,128)(2,1)S(1)} %collective-permute-done.1.refs_2_), channel_id=1, source_target_pairs={{0,2},{1,3},{2,4},{3,5},{4,6},{5,7},{6,0},{7,1},{8,10},{9,11},{10,... | collective-permute-start | bytes 786440 | tf_op jit(solution)/shard_map/ppermute | solution.py:88
  52.7 5.4 %collective-permute-start.5 = (bf16[256,512]{1,0:T(8,128)(2,1)S(1)}, bf16[256,512]{1,0:T(8,128)(2,1)S(1)}, u32[]{:S(2)}, u32[]{:S(2)}) collective-permute-start(bf16[256,512]{1,0:T(8,128)(2,1)S(1)} %collective-permute-done.1.refs_2_), channel_id=1, source_target_pairs={{0,1},{1,0},{2,3},{3,2},{4,5},{5,4},{6,7},{7,6},{8,9},{9,8},{10,11... | collective-permute-start | bytes 786440 | tf_op jit(solution)/shard_map/ppermute | solution.py:90
  53.8 5.5 %collective-permute-start.4 = (bf16[256,512]{1,0:T(8,128)(2,1)S(1)}, bf16[256,512]{1,0:T(8,128)(2,1)S(1)}, u32[]{:S(2)}, u32[]{:S(2)}) collective-permute-start(bf16[256,512]{1,0:T(8,128)(2,1)S(1)} %collective-permute-done.refs_1_), channel_id=1, source_target_pairs={{0,6},{1,7},{2,0},{3,1},{4,2},{5,3},{6,4},{7,5},{8,14},{9,15},{10,... | collective-permute-start | bytes 786440 | tf_op jit(solution)/shard_map/ppermute | solution.py:89
  59.4 6.0 %collective-permute-start.6 = (bf16[128,512]{1,0:T(8,128)(2,1)S(1)}, bf16[128,512]{1,0:T(8,128)(2,1)S(1)}, u32[]{:S(2)}, u32[]{:S(2)}) collective-permute-start(bf16[128,512]{1,0:T(8,128)(2,1)S(1)} %slice.22), channel_id=1, source_target_pairs={{0,2},{1,3},{2,4},{3,5},{4,6},{5,7},{6,0},{7,1},{8,10},{9,11},{10,... | collective-permute-start | bytes 393224 | tf_op jit(solution)/shard_map/ppermute | solution.py:95
  60.5 5.0 %collective-permute-start.7 = (bf16[128,512]{1,0:T(8,128)(2,1)S(1)}, bf16[128,512]{1,0:T(8,128)(2,1)S(1)}, u32[]{:S(2)}, u32[]{:S(2)}) collective-permute-start(bf16[128,512]{1,0:T(8,128)(2,1)S(1)} %slice.23), channel_id=1, source_target_pairs={{0,6},{1,7},{2,0},{3,1},{4,2},{5,3},{6,4},{7,5},{8,14},{9,15},{10,... | collective-permute-start | bytes 393224 | tf_op jit(solution)/shard_map/ppermute | solution.py:95
  62.1 2.8 %copy-start.1 = (bf16[4096,1,6,128]{3,0,2,1:T(8,128)(2,1)S(1)}, bf16[4096,1,6,128]{3,0,2,1:T(8,128)(2,1)}, u32[]{:S(2)}) copy-start(bf16[4096,1,6,128]{3,0,2,1:T(8,128)(2,1)} %param.13) | copy-start | bytes 18874372
  64.9 0.7 copy-start.3
  68.1 6.6 %collective-permute-start.8 = (bf16[512,128]{1,0:T(8,128)(2,1)S(1)}, bf16[512,128]{1,0:T(8,128)(2,1)S(1)}, u32[]{:S(2)}, u32[]{:S(2)}) collective-permute-start(bf16[512,128]{1,0:T(8,128)(2,1)S(1)} %get-tuple-element.59.refs_4_), channel_id=1, source_target_pairs={{0,8},{8,0},{16,24},{24,16},{32,40},{40,32},{48,56},{56,48},{64,72... | collective-permute-start | bytes 393224 | tf_op jit(solution)/shard_map/ppermute | solution.py:412
  74.8 2.5 %collective-permute-start.9 = (bf16[128,1024]{1,0:T(8,128)(2,1)S(1)}, bf16[128,1024]{1,0:T(8,128)(2,1)S(1)}, u32[]{:S(2)}, u32[]{:S(2)}) collective-permute-start(bf16[128,1024]{1,0:T(8,128)(2,1)S(1)} %get-tuple-element.57.refs_2_), channel_id=1, source_target_pairs={{0,8},{8,0},{16,24},{24,16},{32,40},{40,32},{48,56},{56,48},{64,72... | collective-permute-start | bytes 786440 | tf_op jit(solution)/shard_map/ppermute | solution.py:416
  75.7 5.5 %collective-permute-start.10 = (bf16[1024,128]{1,0:T(8,128)(2,1)S(1)}, bf16[1024,128]{1,0:T(8,128)(2,1)S(1)}, u32[]{:S(2)}, u32[]{:S(2)}) collective-permute-start(bf16[1024,128]{1,0:T(8,128)(2,1)S(1)} %pad_maximum_fusion), channel_id=1, source_target_pairs={{0,16},{8,120},{16,32},{24,8},{32,48},{40,24},{48,64},{56,40},{64,... | collective-permute-start | bytes 786440 | tf_op jit(solution)/shard_map/ppermute | solution.py:414
  75.8 8.0 %collective-permute-start.14 = (bf16[1024,128]{1,0:T(8,128)(2,1)S(1)}, bf16[1024,128]{1,0:T(8,128)(2,1)S(1)}, u32[]{:S(2)}, u32[]{:S(2)}) collective-permute-start(bf16[1024,128]{1,0:T(8,128)(2,1)S(1)} %pad_maximum_fusion), channel_id=1, source_target_pairs={{0,144},{8,248},{16,160},{24,136},{32,176},{40,152},{48,192},{56,1... | collective-permute-start | bytes 786440 | tf_op jit(solution)/shard_map/ppermute | solution.py:415
  81.2 7.6 %collective-permute-start.11 = (bf16[1024,128]{1,0:T(8,128)(2,1)S(1)}, bf16[1024,128]{1,0:T(8,128)(2,1)S(1)}, u32[]{:S(2)}, u32[]{:S(2)}) collective-permute-start(bf16[1024,128]{1,0:T(8,128)(2,1)S(1)} %collective-permute-done.10.refs_4_), channel_id=1, source_target_pairs={{0,16},{8,120},{16,32},{24,8},{32,48},{40,24},{48,64},{56,40},{64,... | collective-permute-start | bytes 786440 | tf_op jit(solution)/shard_map/ppermute | solution.py:355
  83.8 10.5 %collective-permute-start.15 = (bf16[1024,128]{1,0:T(8,128)(2,1)S(1)}, bf16[1024,128]{1,0:T(8,128)(2,1)S(1)}, u32[]{:S(2)}, u32[]{:S(2)}) collective-permute-start(bf16[1024,128]{1,0:T(8,128)(2,1)S(1)} %collective-permute-done.14.refs_4_), channel_id=1, source_target_pairs={{0,16},{8,120},{16,32},{24,8},{32,48},{40,24},{48,64},{56,40},{64,... | collective-permute-start | bytes 786440 | tf_op jit(solution)/shard_map/ppermute | solution.py:355
  88.8 8.9 %collective-permute-start.12 = (bf16[1024,128]{1,0:T(8,128)(2,1)S(1)}, bf16[1024,128]{1,0:T(8,128)(2,1)S(1)}, u32[]{:S(2)}, u32[]{:S(2)}) collective-permute-start(bf16[1024,128]{1,0:T(8,128)(2,1)S(1)} %collective-permute-done.11.refs_4_), channel_id=1, source_target_pairs={{0,16},{8,120},{16,32},{24,8},{32,48},{40,24},{48,64},{56,40},{64,... | collective-permute-start | bytes 786440 | tf_op jit(solution)/shard_map/ppermute | solution.py:355
  88.9 17.3 %collective-permute-start.17 = (bf16[512,128]{1,0:T(8,128)(2,1)S(1)}, bf16[512,128]{1,0:T(8,128)(2,1)S(1)}, u32[]{:S(2)}, u32[]{:S(2)}) collective-permute-start(bf16[512,128]{1,0:T(8,128)(2,1)S(1)} %get-tuple-element.59.refs_4_), channel_id=1, source_target_pairs={{0,128},{8,136},{16,144},{24,152},{32,160},{40,168},{48,176},{56,1... | collective-permute-start | bytes 393224 | tf_op jit(solution)/shard_map/ppermute | solution.py:417
  90.8 13.8 %collective-permute-start.18 = (bf16[1024,128]{1,0:T(8,128)(2,1)S(1)}, bf16[1024,128]{1,0:T(8,128)(2,1)S(1)}, u32[]{:S(2)}, u32[]{:S(2)}) collective-permute-start(bf16[1024,128]{1,0:T(8,128)(2,1)S(1)} %collective-permute-done.14.refs_4_), channel_id=1, source_target_pairs={{0,32},{8,104},{16,48},{24,120},{32,64},{40,8},{48,80},{56,24},{64... | collective-permute-start | bytes 786440 | tf_op jit(solution)/shard_map/ppermute | solution.py:355
  94.3 12.8 %collective-permute-start.16 = (bf16[512,128]{1,0:T(8,128)(2,1)S(1)}, bf16[512,128]{1,0:T(8,128)(2,1)S(1)}, u32[]{:S(2)}, u32[]{:S(2)}) collective-permute-start(bf16[512,128]{1,0:T(8,128)(2,1)S(1)} %slice.25), channel_id=1, source_target_pairs={{0,32},{8,104},{16,48},{24,120},{32,64},{40,8},{48,80},{56,24},{64... | collective-permute-start | bytes 393224 | tf_op jit(solution)/shard_map/ppermute | solution.py:355
  97.8 9.4 %collective-permute-start.13 = (bf16[512,128]{1,0:T(8,128)(2,1)S(1)}, bf16[512,128]{1,0:T(8,128)(2,1)S(1)}, u32[]{:S(2)}, u32[]{:S(2)}) collective-permute-start(bf16[512,128]{1,0:T(8,128)(2,1)S(1)} %slice.24), channel_id=1, source_target_pairs={{0,16},{8,120},{16,32},{24,8},{32,48},{40,24},{48,64},{56,40},{64,... | collective-permute-start | bytes 393224 | tf_op jit(solution)/shard_map/ppermute | solution.py:355
  108.1 3.0 %collective-permute-start.19 = (f32[136,1024]{1,0:T(8,128)S(1)}, f32[136,1024]{1,0:T(8,128)S(1)}, u32[]{:S(2)}, u32[]{:S(2)}) collective-permute-start(f32[136,1024]{1,0:T(8,128)S(1)} %attend.19), channel_id=1, source_target_pairs={{0,8},{8,0},{16,24},{24,16},{32,40},{40,32},{48,56},{56,48},{64,72... | collective-permute-start | bytes 1671176 | tf_op jit(solution)/shard_map/ppermute | solution.py:434

commit v3 on v2

--- a/solution.py
+++ b/solution.py
@@ -85,16 +85,13 @@
 
 def gather_second(side, down, up):
     return [
+        lax.ppermute(side, "head", y_shift(2)),
         lax.ppermute(down, "head", y_shift(1)),
         lax.ppermute(side, "head", y_shift(-1)),
         lax.ppermute(down, "head", xlo_swap()),
     ]
 
 
-def gather_third(top, low):
-    return [lax.ppermute(top, "head", y_shift(1)), lax.ppermute(low, "head", y_shift(-1))]
-
-
 def block_order(place):
     y, x = place // 2, place % 2
 
@@ -112,9 +109,7 @@
     def block(k):
         if count == 1:
             return blocks[0][:, k * COLS : (k + 1) * COLS].astype(f32)
-        if k < 7:
-            return blocks[k][...].astype(f32)
-        return jnp.concatenate([blocks[7][...], blocks[8][...]], axis=0).astype(f32)
+        return blocks[k][...].astype(f32)
 
     squares = jnp.zeros((rows, COLS), f32)
     for k in range(8):
@@ -401,12 +396,10 @@
     ).reshape(SLOTS, COLS + HD)
     sequence = whole(place_kernel, (ROWS, COLS), "place_rows", mail, text_rows)
     first = lax.optimization_barrier(gather_first(sequence))
-    second = lax.optimization_barrier(gather_second(*first))
-    halves = (second[2][:SPAN], second[1][SPAN:])
-    weight, gain, cosine, sine, halves = lax.optimization_barrier((weight, gain, cosine, sine, halves))
-    third = gather_third(*halves)
+    weight, gain, cosine, sine, first = lax.optimization_barrier((weight, gain, cosine, sine, first))
+    far_side, far, side_up, side_down = gather_second(*first)
     queries, own = project_qkv(
-        [sequence, *first, *second, *third], load_weight(weight), gain, cosine, sine
+        [sequence, *first, far, side_up, side_down, far_side], load_weight(weight), gain, cosine, sine
     )
 
     stream = jnp.concatenate([own, lax.ppermute(own, "ctx", core_swap())], axis=0)

time: 112 us -> 110 us (0.982)
  starting transfers between devices: 49.8 us -> 48.2 us
    ppermute x2 -> x1, waiting for transfers between devices: 0.01 us -> 4.78 us  [gather_second(): lax.ppermute(side, 'head', y_shift(2))]
    ppermute x1, waiting for transfers between devices: 1.91 us -> 0.01 us  [gather_second(): lax.ppermute(down, 'head', y_shift(1))]
    ppermute x1, waiting for transfers between devices: 2.85 us -> 1.15 us  [on_device(): moved = lax.ppermute(stream, 'ctx', z_move())]
    ppermute x1, starting transfers between devices: 5.6 us -> 3.9 us  [on_device(): lax.ppermute(own, 'ctx', core_swap())]
    ppermute x2 -> x1, starting transfers between devices: 2.75 us -> 1.12 us  [gather_second(): lax.ppermute(side, 'head', y_shift(2))]
    ppermute x1, starting transfers between devices: 1.47 us -> 2.95 us  [on_device(): crossed = lax.ppermute(stream, 'ctx', z_cross())]
    ppermute x1, waiting for transfers between devices: 1.26 us -> 0.01 us  [gather_second(): lax.ppermute(side, 'head', y_shift(-1))]
  transfers between devices with their start and end apart: 22 -> 21, of which waited for: 11 -> 10; matrix products, arithmetic and copies ran while one was open for 4% -> 4% of each run, Pallas kernels for 12% -> 12%
where the time goes in v3:
time: 110 us; the launch traced here: 109 us
  starting transfers between devices  48.2 us (44%)
  waiting for transfers between devices  32.6 us (30%)
  Pallas kernels  20.8 us (19%)
  local copies, waits for them, and re-layouts  3.35 us (3%)
  matrix products  3.26 us (3%)
    all_to_all x1, waiting for transfers between devices, on_device(): lax.all_to_all(mail.reshape(OWNERS, CAP, COLS + HD), 'ctx', split_axis=0,...  14.5 us
    pallas_call x10, Pallas kernels, attend(): pl.pallas_call(functools.partial(attend_kernel, first, len(blocks), key_r...  13.6 us
    ppermute x6, starting transfers between devices, send_on(): return lax.ppermute(block[:size], 'ctx', z_move(steps))  13 us
    all_to_all x1, starting transfers between devices, on_device(): lax.all_to_all(my_rows.reshape(OWNERS, 1, HD), 'ctx', split_axis=0, conca...  12.6 us
    all_to_all x1, waiting for transfers between devices, on_device(): lax.all_to_all(my_rows.reshape(OWNERS, 1, HD), 'ctx', split_axis=0, conca...  5.86 us
    ppermute x1, waiting for transfers between devices, gather_second(): lax.ppermute(side, 'head', y_shift(2))  4.78 us
    all_to_all x1, starting transfers between devices, on_device(): lax.all_to_all(mail.reshape(OWNERS, CAP, COLS + HD), 'ctx', split_axis=0,...  4.31 us
    ppermute x1, starting transfers between devices, on_device(): lax.ppermute(own, 'ctx', core_swap())  3.9 us
  transfers between devices with their start and end apart: 21, of which 10 were waited for; matrix products, arithmetic and copies ran while one was open for 4% of the time, Pallas kernels for 12%

profile of v3, /device:TPU:1, one launch (start us, length us, event | category | flops | bytes accessed | tf_op | source)
XLA Modules:
  0.0 109.4 jit_solution(3088191489151334056)
XLA Ops:
  0.0 1.5 %my_entry.1 = s32[32,128]{1,0:T(8,128)} custom-call(s32[1,2]{1,0:T(1,128)} %span_ref.1), custom_call_target="tpu_custom_call" | custom-call | tf_op jit(solution)/shard_map/my_entry/pallas_call | solution.py:360
  1.5 12.6 %all-to-all-start = ((s32[32,1,128]{2,1,0:T(1,128)}), s32[32,1,128]{2,1,0:T(1,128)S(1)}, u32[]{:S(2)}, u32[]{:S(2)}) async-start(s32[32,1,128]{2,1,0:T(1,128)} %bitcast.71), calls=%async_computation | async-start | bytes 32768 | tf_op jit(solution)/shard_map/all_to_all | solution.py:367
  14.1 3.3 %convolution_convert_fusion.rows_ref = bf16[160,512]{1,0:T(8,128)(2,1)S(1)} fusion(bf16[160,4608]{1,0:T(8,128)(2,1)S(1)} %copy-done, bf16[4608,512]{1,0:T(8,128)(2,1)} %param.11), kind=kOutput, calls=%fused_computation | convolution fusion | flops 755056640 | bytes 6356992 | tf_op jit(solution)/shard_map/dot_general | solution.py:370
  17.5 5.9 %all-to-all-done = s32[32,1,128]{2,1,0:T(1,128)S(1)} async-done(((s32[32,1,128]{2,1,0:T(1,128)}), s32[32,1,128]{2,1,0:T(1,128)S(1)}, u32[]{:S(2)}, u32[]{:S(2)}) %all-to-all-start) | async-done | bytes 16416 | tf_op jit(solution)/shard_map/all_to_all | solution.py:367
  23.3 1.5 %route_rows.1 = bf16[256,640]{1,0:T(8,128)(2,1)} custom-call(bf16[160,512]{1,0:T(8,128)(2,1)S(1)} %convolution_convert_fusion.rows_ref, s32[160,1]{1,0:T(8,128)S(1)} %copy.12.pos_ref, s32[32,128]{1,0:T(8,128)S(1)} %bitcast.59), custom_call_target="tpu_custom_call" | custom-call | flops 67108864 | bytes 524288 | tf_op jit(solution)/shard_map/route_rows/pallas_call | solution.py:238
  24.8 4.3 %all-to-all-start.1 = ((bf16[32,8,640]{2,1,0:T(8,128)(2,1)}), bf16[32,8,640]{2,1,0:T(8,128)(2,1)S(1)}, u32[]{:S(2)}, u32[]{:S(2)}) async-start(bf16[32,8,640]{2,1,0:T(8,128)(2,1)} %bitcast.40), calls=%async_computation.1 | async-start | bytes 655360 | tf_op jit(solution)/shard_map/all_to_all | solution.py:394
  29.3 14.5 %all-to-all-done.1 = bf16[32,8,640]{2,1,0:T(8,128)(2,1)S(1)} async-done(((bf16[32,8,640]{2,1,0:T(8,128)(2,1)}), bf16[32,8,640]{2,1,0:T(8,128)(2,1)S(1)}, u32[]{:S(2)}, u32[]{:S(2)}) %all-to-all-start.1) | async-done | bytes 327712 | tf_op jit(solution)/shard_map/all_to_all | solution.py:394
  44.6 1.3 %collective-permute-start.1 = (bf16[256,512]{1,0:T(8,128)(2,1)S(1)}, bf16[256,512]{1,0:T(8,128)(2,1)S(1)}, u32[]{:S(2)}, u32[]{:S(2)}) collective-permute-start(bf16[256,512]{1,0:T(8,128)(2,1)S(1)} %place_rows.1.refs_0_), channel_id=1, source_target_pairs={{0,2},{1,3},{2,4},{3,5},{4,6},{5,7},{6,0},{7,1},{8,10},{9,11},{10,... | collective-permute-start | bytes 786440 | tf_op jit(solution)/shard_map/ppermute | solution.py:81
  45.9 1.4 %collective-permute-start.2 = (bf16[256,512]{1,0:T(8,128)(2,1)S(1)}, bf16[256,512]{1,0:T(8,128)(2,1)S(1)}, u32[]{:S(2)}, u32[]{:S(2)}) collective-permute-start(bf16[256,512]{1,0:T(8,128)(2,1)S(1)} %place_rows.1.refs_0_), channel_id=1, source_target_pairs={{0,6},{1,7},{2,0},{3,1},{4,2},{5,3},{6,4},{7,5},{8,14},{9,15},{10,... | collective-permute-start | bytes 786440 | tf_op jit(solution)/shard_map/ppermute | solution.py:82
  48.0 2.3 %collective-permute-done.refs_1_ = bf16[256,512]{1,0:T(8,128)(2,1)S(1)} collective-permute-done((bf16[256,512]{1,0:T(8,128)(2,1)S(1)}, bf16[256,512]{1,0:T(8,128)(2,1)S(1)}, u32[]{:S(2)}, u32[]{:S(2)}) %collective-permute-start) | collective-permute-done | bytes 262176 | tf_op jit(solution)/shard_map/ppermute | solution.py:80
  50.3 1.4 %collective-permute-done.1.refs_2_ = bf16[256,512]{1,0:T(8,128)(2,1)S(1)} collective-permute-done((bf16[256,512]{1,0:T(8,128)(2,1)S(1)}, bf16[256,512]{1,0:T(8,128)(2,1)S(1)}, u32[]{:S(2)}, u32[]{:S(2)}) %collective-permute-start.1) | collective-permute-done | bytes 262176 | tf_op jit(solution)/shard_map/ppermute | solution.py:81
  52.7 1.7 %collective-permute-start.4 = (bf16[256,512]{1,0:T(8,128)(2,1)S(1)}, bf16[256,512]{1,0:T(8,128)(2,1)S(1)}, u32[]{:S(2)}, u32[]{:S(2)}) collective-permute-start(bf16[256,512]{1,0:T(8,128)(2,1)S(1)} %collective-permute-done.refs_1_), channel_id=1, source_target_pairs={{0,6},{1,7},{2,0},{3,1},{4,2},{5,3},{6,4},{7,5},{8,14},{9,15},{10,... | collective-permute-start | bytes 786440 | tf_op jit(solution)/shard_map/ppermute | solution.py:90
  54.3 1.2 %collective-permute-start.5 = (bf16[256,512]{1,0:T(8,128)(2,1)S(1)}, bf16[256,512]{1,0:T(8,128)(2,1)S(1)}, u32[]{:S(2)}, u32[]{:S(2)}) collective-permute-start(bf16[256,512]{1,0:T(8,128)(2,1)S(1)} %collective-permute-done.1.refs_2_), channel_id=1, source_target_pairs={{0,1},{1,0},{2,3},{3,2},{4,5},{5,4},{6,7},{7,6},{8,9},{9,8},{10,11... | collective-permute-start | bytes 786440 | tf_op jit(solution)/shard_map/ppermute | solution.py:91
  55.5 1.1 %collective-permute-start.6 = (bf16[256,512]{1,0:T(8,128)(2,1)S(1)}, bf16[256,512]{1,0:T(8,128)(2,1)S(1)}, u32[]{:S(2)}, u32[]{:S(2)}) collective-permute-start(bf16[256,512]{1,0:T(8,128)(2,1)S(1)} %collective-permute-done.refs_1_), channel_id=1, source_target_pairs={{0,4},{1,5},{2,6},{3,7},{4,0},{5,1},{6,2},{7,3},{8,12},{9,13},{10,... | collective-permute-start | bytes 786440 | tf_op jit(solution)/shard_map/ppermute | solution.py:88
  56.6 2.8 %copy-done.1 = bf16[4096,1,6,128]{3,0,2,1:T(8,128)(2,1)S(1)} copy-done((bf16[4096,1,6,128]{3,0,2,1:T(8,128)(2,1)S(1)}, bf16[4096,1,6,128]{3,0,2,1:T(8,128)(2,1)}, u32[]{:S(2)}) %copy-start.1) | copy-done | bytes 6291480
  59.9 4.8 %collective-permute-done.6.refs_7_ = bf16[256,512]{1,0:T(8,128)(2,1)S(1)} collective-permute-done((bf16[256,512]{1,0:T(8,128)(2,1)S(1)}, bf16[256,512]{1,0:T(8,128)(2,1)S(1)}, u32[]{:S(2)}, u32[]{:S(2)}) %collective-permute-start.6) | collective-permute-done | bytes 262176 | tf_op jit(solution)/shard_map/ppermute | solution.py:88
  64.7 2.5 %norm_qkv.1 = (bf16[128,1024]{1,0:T(8,128)(2,1)S(1)}, bf16[512,128]{1,0:T(8,128)(2,1)S(1)}) custom-call(bf16[256,512]{1,0:T(8,128)(2,1)S(1)} %place_rows.1.refs_0_, bf16[256,512]{1,0:T(8,128)(2,1)S(1)} %collective-permute-done.refs_1_, bf16[256,512]{1,0:T(8,128)(2,1)S(1)} %collective-permute-done.1.refs_2_, ...), custom_call_target="tpu_custom_call" | custom-call | flops 1610612736 | bytes 8388608 | tf_op jit(solution)/shard_map/norm_qkv/pallas_call | solution.py:181
  67.2 3.9 %collective-permute-start.7 = (bf16[512,128]{1,0:T(8,128)(2,1)S(1)}, bf16[512,128]{1,0:T(8,128)(2,1)S(1)}, u32[]{:S(2)}, u32[]{:S(2)}) collective-permute-start(bf16[512,128]{1,0:T(8,128)(2,1)S(1)} %get-tuple-element.55.refs_4_), channel_id=1, source_target_pairs={{0,8},{8,0},{16,24},{24,16},{32,40},{40,32},{48,56},{56,48},{64,72... | collective-permute-start | bytes 393224 | tf_op jit(solution)/shard_map/ppermute | solution.py:405
  73.4 3.0 %collective-permute-start.13 = (bf16[1024,128]{1,0:T(8,128)(2,1)S(1)}, bf16[1024,128]{1,0:T(8,128)(2,1)S(1)}, u32[]{:S(2)}, u32[]{:S(2)}) collective-permute-start(bf16[1024,128]{1,0:T(8,128)(2,1)S(1)} %pad_maximum_fusion), channel_id=1, source_target_pairs={{0,144},{8,248},{16,160},{24,136},{32,176},{40,152},{48,192},{56,1... | collective-permute-start | bytes 786440 | tf_op jit(solution)/shard_map/ppermute | solution.py:408
  76.4 1.0 attend.10
  77.4 1.1 %collective-permute-done.9.refs_4_ = bf16[1024,128]{1,0:T(8,128)(2,1)S(1)} collective-permute-done((bf16[1024,128]{1,0:T(8,128)(2,1)S(1)}, bf16[1024,128]{1,0:T(8,128)(2,1)S(1)}, u32[]{:S(2)}, u32[]{:S(2)}) %collective-permute-start.9) | collective-permute-done | bytes 262176 | tf_op jit(solution)/shard_map/ppermute | solution.py:407
  78.6 1.2 %collective-permute-start.10 = (bf16[1024,128]{1,0:T(8,128)(2,1)S(1)}, bf16[1024,128]{1,0:T(8,128)(2,1)S(1)}, u32[]{:S(2)}, u32[]{:S(2)}) collective-permute-start(bf16[1024,128]{1,0:T(8,128)(2,1)S(1)} %collective-permute-done.9.refs_4_), channel_id=1, source_target_pairs={{0,16},{8,120},{16,32},{24,8},{32,48},{40,24},{48,64},{56,40},{64,... | collective-permute-start | bytes 786440 | tf_op jit(solution)/shard_map/ppermute | solution.py:350
  79.8 1.6 %attend.11 = (f32[136,1024]{1,0:T(8,128)S(1)}, f32[136,1024]{1,0:T(8,128)S(1)}) custom-call(f32[32,128]{1,0:T(8,128)S(1)} %broadcast_in_dim.36.refs_0_, f32[2,1024]{1,0:T(2,128)S(1)} %bitcast.62, bf16[128,1024]{1,0:T(8,128)(2,1)S(1)} %get-tuple-element.53.refs_2_, bf16[128,1024]{1,0:T(8,128)(2,1)S(1)} %collective-permute-done.8.refs_3_, ...), custom_call_target="tpu_custom_call" | custom-call | flops 1073741824 | bytes 2490368 | tf_op jit(solution)/shard_map/attend/pallas_call | solution.py:307
  81.6 5.6 %collective-permute-start.14 = (bf16[1024,128]{1,0:T(8,128)(2,1)S(1)}, bf16[1024,128]{1,0:T(8,128)(2,1)S(1)}, u32[]{:S(2)}, u32[]{:S(2)}) collective-permute-start(bf16[1024,128]{1,0:T(8,128)(2,1)S(1)} %collective-permute-done.13.refs_4_), channel_id=1, source_target_pairs={{0,16},{8,120},{16,32},{24,8},{32,48},{40,24},{48,64},{56,40},{64,... | collective-permute-start | bytes 786440 | tf_op jit(solution)/shard_map/ppermute | solution.py:350
  87.2 2.2 %collective-permute-start.16 = (bf16[512,128]{1,0:T(8,128)(2,1)S(1)}, bf16[512,128]{1,0:T(8,128)(2,1)S(1)}, u32[]{:S(2)}, u32[]{:S(2)}) collective-permute-start(bf16[512,128]{1,0:T(8,128)(2,1)S(1)} %get-tuple-element.55.refs_4_), channel_id=1, source_target_pairs={{0,128},{8,136},{16,144},{24,152},{32,160},{40,168},{48,176},{56,1... | collective-permute-start | bytes 393224 | tf_op jit(solution)/shard_map/ppermute | solution.py:410
  89.7 1.6 %attend.12 = (f32[136,1024]{1,0:T(8,128)S(1)}, f32[136,1024]{1,0:T(8,128)S(1)}) custom-call(f32[32,128]{1,0:T(8,128)S(1)} %broadcast_in_dim.36.refs_0_, f32[2,1024]{1,0:T(2,128)S(1)} %bitcast.63, bf16[128,1024]{1,0:T(8,128)(2,1)S(1)} %get-tuple-element.53.refs_2_, bf16[128,1024]{1,0:T(8,128)(2,1)S(1)} %collective-permute-done.8.refs_3_, ...), custom_call_target="tpu_custom_call" | custom-call | flops 1073741824 | bytes 2490368 | tf_op jit(solution)/shard_map/attend/pallas_call | solution.py:307
  91.3 1.6 %attend.13 = (f32[136,1024]{1,0:T(8,128)S(1)}, f32[136,1024]{1,0:T(8,128)S(1)}) custom-call(f32[32,128]{1,0:T(8,128)S(1)} %broadcast_in_dim.36.refs_0_, f32[2,1024]{1,0:T(2,128)S(1)} %bitcast.64, bf16[128,1024]{1,0:T(8,128)(2,1)S(1)} %get-tuple-element.53.refs_2_, bf16[128,1024]{1,0:T(8,128)(2,1)S(1)} %collective-permute-done.8.refs_3_, ...), custom_call_target="tpu_custom_call" | custom-call | flops 1073741824 | bytes 2490368 | tf_op jit(solution)/shard_map/attend/pallas_call | solution.py:307
  93.0 2.3 %collective-permute-start.15 = (bf16[512,128]{1,0:T(8,128)(2,1)S(1)}, bf16[512,128]{1,0:T(8,128)(2,1)S(1)}, u32[]{:S(2)}, u32[]{:S(2)}) collective-permute-start(bf16[512,128]{1,0:T(8,128)(2,1)S(1)} %slice.17), channel_id=1, source_target_pairs={{0,32},{8,104},{16,48},{24,120},{32,64},{40,8},{48,80},{56,24},{64... | collective-permute-start | bytes 393224 | tf_op jit(solution)/shard_map/ppermute | solution.py:350
  96.1 3.6 %collective-permute-start.12 = (bf16[512,128]{1,0:T(8,128)(2,1)S(1)}, bf16[512,128]{1,0:T(8,128)(2,1)S(1)}, u32[]{:S(2)}, u32[]{:S(2)}) collective-permute-start(bf16[512,128]{1,0:T(8,128)(2,1)S(1)} %slice.16), channel_id=1, source_target_pairs={{0,16},{8,120},{16,32},{24,8},{32,48},{40,24},{48,64},{56,40},{64,... | collective-permute-start | bytes 393224 | tf_op jit(solution)/shard_map/ppermute | solution.py:350
  99.7 1.6 %attend.14 = (f32[136,1024]{1,0:T(8,128)S(1)}, f32[136,1024]{1,0:T(8,128)S(1)}) custom-call(f32[32,128]{1,0:T(8,128)S(1)} %broadcast_in_dim.36.refs_0_, f32[2,1024]{1,0:T(2,128)S(1)} %bitcast.65, bf16[128,1024]{1,0:T(8,128)(2,1)S(1)} %get-tuple-element.53.refs_2_, bf16[128,1024]{1,0:T(8,128)(2,1)S(1)} %collective-permute-done.8.refs_3_, ...), custom_call_target="tpu_custom_call" | custom-call | flops 1073741824 | bytes 2490368 | tf_op jit(solution)/shard_map/attend/pallas_call | solution.py:307
  101.3 1.6 %attend.15 = (f32[136,1024]{1,0:T(8,128)S(1)}, f32[136,1024]{1,0:T(8,128)S(1)}) custom-call(f32[32,128]{1,0:T(8,128)S(1)} %broadcast_in_dim.36.refs_0_, f32[2,1024]{1,0:T(2,128)S(1)} %bitcast.66, bf16[128,1024]{1,0:T(8,128)(2,1)S(1)} %get-tuple-element.53.refs_2_, bf16[128,1024]{1,0:T(8,128)(2,1)S(1)} %collective-permute-done.8.refs_3_, ...), custom_call_target="tpu_custom_call" | custom-call | flops 1073741824 | bytes 2490368 | tf_op jit(solution)/shard_map/attend/pallas_call | solution.py:307
  102.9 1.6 %attend.16 = (f32[136,1024]{1,0:T(8,128)S(1)}, f32[136,1024]{1,0:T(8,128)S(1)}) custom-call(f32[32,128]{1,0:T(8,128)S(1)} %broadcast_in_dim.36.refs_0_, f32[2,1024]{1,0:T(2,128)S(1)} %bitcast.67, bf16[128,1024]{1,0:T(8,128)(2,1)S(1)} %get-tuple-element.53.refs_2_, bf16[128,1024]{1,0:T(8,128)(2,1)S(1)} %collective-permute-done.8.refs_3_, ...), custom_call_target="tpu_custom_call" | custom-call | flops 1073741824 | bytes 2490368 | tf_op jit(solution)/shard_map/attend/pallas_call | solution.py:307
  (57 shorter events, 11.7 us)
Async XLA Ops:
  0.0 14.1 %copy-start = (bf16[160,4608]{1,0:T(8,128)(2,1)S(1)}, bf16[160,4608]{1,0:T(8,128)(2,1)}, u32[]{:S(2)}) copy-start(bf16[160,4608]{1,0:T(8,128)(2,1)} %param.7) | copy-start | bytes 4423684
  0.0 29.2 %copy-start.5 = (s32[1,2]{1,0:T(1,128)S(1)}, s32[1,2]{1,0:T(1,128)}, u32[]{:S(2)}) copy-start(s32[1,2]{1,0:T(1,128)} %span_ref.1) | copy-start | bytes 28
  0.0 17.3 %copy-start.4 = (s32[160]{0:T(256)S(1)}, s32[160]{0:T(256)}, u32[]{:S(2)}) copy-start(s32[160]{0:T(256)} %param.8) | copy-start | bytes 1924
  0.0 43.8 %copy-start.2 = (bf16[256,512]{1,0:T(8,128)(2,1)S(1)}, bf16[256,512]{1,0:T(8,128)(2,1)}, u32[]{:S(2)}) copy-start(bf16[256,512]{1,0:T(8,128)(2,1)} %text_ref.1) | copy-start | bytes 786436
  1.5 21.9 %all-to-all-start = ((s32[32,1,128]{2,1,0:T(1,128)}), s32[32,1,128]{2,1,0:T(1,128)S(1)}, u32[]{:S(2)}, u32[]{:S(2)}) async-start(s32[32,1,128]{2,1,0:T(1,128)} %bitcast.71), calls=%async_computation | async-start | bytes 32768 | tf_op jit(solution)/shard_map/all_to_all | solution.py:367
  24.8 18.9 %all-to-all-start.1 = ((bf16[32,8,640]{2,1,0:T(8,128)(2,1)}), bf16[32,8,640]{2,1,0:T(8,128)(2,1)S(1)}, u32[]{:S(2)}, u32[]{:S(2)}) async-start(bf16[32,8,640]{2,1,0:T(8,128)(2,1)} %bitcast.40), calls=%async_computation.1 | async-start | bytes 655360 | tf_op jit(solution)/shard_map/all_to_all | solution.py:394
  44.2 6.1 %collective-permute-start = (bf16[256,512]{1,0:T(8,128)(2,1)S(1)}, bf16[256,512]{1,0:T(8,128)(2,1)S(1)}, u32[]{:S(2)}, u32[]{:S(2)}) collective-permute-start(bf16[256,512]{1,0:T(8,128)(2,1)S(1)} %place_rows.1.refs_0_), channel_id=1, source_target_pairs={{0,1},{1,0},{2,3},{3,2},{4,5},{5,4},{6,7},{7,6},{8,9},{9,8},{10,11... | collective-permute-start | bytes 786440 | tf_op jit(solution)/shard_map/ppermute | solution.py:80
  44.6 7.1 %collective-permute-start.1 = (bf16[256,512]{1,0:T(8,128)(2,1)S(1)}, bf16[256,512]{1,0:T(8,128)(2,1)S(1)}, u32[]{:S(2)}, u32[]{:S(2)}) collective-permute-start(bf16[256,512]{1,0:T(8,128)(2,1)S(1)} %place_rows.1.refs_0_), channel_id=1, source_target_pairs={{0,2},{1,3},{2,4},{3,5},{4,6},{5,7},{6,0},{7,1},{8,10},{9,11},{10,... | collective-permute-start | bytes 786440 | tf_op jit(solution)/shard_map/ppermute | solution.py:81
  45.9 5.8 %collective-permute-start.2 = (bf16[256,512]{1,0:T(8,128)(2,1)S(1)}, bf16[256,512]{1,0:T(8,128)(2,1)S(1)}, u32[]{:S(2)}, u32[]{:S(2)}) collective-permute-start(bf16[256,512]{1,0:T(8,128)(2,1)S(1)} %place_rows.1.refs_0_), channel_id=1, source_target_pairs={{0,6},{1,7},{2,0},{3,1},{4,2},{5,3},{6,4},{7,5},{8,14},{9,15},{10,... | collective-permute-start | bytes 786440 | tf_op jit(solution)/shard_map/ppermute | solution.py:82
  51.7 8.2 %collective-permute-start.3 = (bf16[256,512]{1,0:T(8,128)(2,1)S(1)}, bf16[256,512]{1,0:T(8,128)(2,1)S(1)}, u32[]{:S(2)}, u32[]{:S(2)}) collective-permute-start(bf16[256,512]{1,0:T(8,128)(2,1)S(1)} %collective-permute-done.1.refs_2_), channel_id=1, source_target_pairs={{0,2},{1,3},{2,4},{3,5},{4,6},{5,7},{6,0},{7,1},{8,10},{9,11},{10,... | collective-permute-start | bytes 786440 | tf_op jit(solution)/shard_map/ppermute | solution.py:89
  52.7 7.2 %collective-permute-start.4 = (bf16[256,512]{1,0:T(8,128)(2,1)S(1)}, bf16[256,512]{1,0:T(8,128)(2,1)S(1)}, u32[]{:S(2)}, u32[]{:S(2)}) collective-permute-start(bf16[256,512]{1,0:T(8,128)(2,1)S(1)} %collective-permute-done.refs_1_), channel_id=1, source_target_pairs={{0,6},{1,7},{2,0},{3,1},{4,2},{5,3},{6,4},{7,5},{8,14},{9,15},{10,... | collective-permute-start | bytes 786440 | tf_op jit(solution)/shard_map/ppermute | solution.py:90
  54.3 5.6 %collective-permute-start.5 = (bf16[256,512]{1,0:T(8,128)(2,1)S(1)}, bf16[256,512]{1,0:T(8,128)(2,1)S(1)}, u32[]{:S(2)}, u32[]{:S(2)}) collective-permute-start(bf16[256,512]{1,0:T(8,128)(2,1)S(1)} %collective-permute-done.1.refs_2_), channel_id=1, source_target_pairs={{0,1},{1,0},{2,3},{3,2},{4,5},{5,4},{6,7},{7,6},{8,9},{9,8},{10,11... | collective-permute-start | bytes 786440 | tf_op jit(solution)/shard_map/ppermute | solution.py:91
  55.5 9.2 %collective-permute-start.6 = (bf16[256,512]{1,0:T(8,128)(2,1)S(1)}, bf16[256,512]{1,0:T(8,128)(2,1)S(1)}, u32[]{:S(2)}, u32[]{:S(2)}) collective-permute-start(bf16[256,512]{1,0:T(8,128)(2,1)S(1)} %collective-permute-done.refs_1_), channel_id=1, source_target_pairs={{0,4},{1,5},{2,6},{3,7},{4,0},{5,1},{6,2},{7,3},{8,12},{9,13},{10,... | collective-permute-start | bytes 786440 | tf_op jit(solution)/shard_map/ppermute | solution.py:88
  56.6 2.8 %copy-start.1 = (bf16[4096,1,6,128]{3,0,2,1:T(8,128)(2,1)S(1)}, bf16[4096,1,6,128]{3,0,2,1:T(8,128)(2,1)}, u32[]{:S(2)}) copy-start(bf16[4096,1,6,128]{3,0,2,1:T(8,128)(2,1)} %param.13) | copy-start | bytes 18874372
  59.4 5.3 %copy-start.3 = (f32[4096]{0:T(1024)S(1)}, f32[4096]{0:T(1024)}, u32[]{:S(2)}) copy-start(f32[4096]{0:T(1024)} %param.12) | copy-start | bytes 49156
  67.2 4.9 %collective-permute-start.7 = (bf16[512,128]{1,0:T(8,128)(2,1)S(1)}, bf16[512,128]{1,0:T(8,128)(2,1)S(1)}, u32[]{:S(2)}, u32[]{:S(2)}) collective-permute-start(bf16[512,128]{1,0:T(8,128)(2,1)S(1)} %get-tuple-element.55.refs_4_), channel_id=1, source_target_pairs={{0,8},{8,0},{16,24},{24,16},{32,40},{40,32},{48,56},{56,48},{64,72... | collective-permute-start | bytes 393224 | tf_op jit(solution)/shard_map/ppermute | solution.py:405
  72.2 4.2 %collective-permute-start.8 = (bf16[128,1024]{1,0:T(8,128)(2,1)S(1)}, bf16[128,1024]{1,0:T(8,128)(2,1)S(1)}, u32[]{:S(2)}, u32[]{:S(2)}) collective-permute-start(bf16[128,1024]{1,0:T(8,128)(2,1)S(1)} %get-tuple-element.53.refs_2_), channel_id=1, source_target_pairs={{0,8},{8,0},{16,24},{24,16},{32,40},{40,32},{48,56},{56,48},{64,72... | collective-permute-start | bytes 786440 | tf_op jit(solution)/shard_map/ppermute | solution.py:409
  72.9 5.6 %collective-permute-start.9 = (bf16[1024,128]{1,0:T(8,128)(2,1)S(1)}, bf16[1024,128]{1,0:T(8,128)(2,1)S(1)}, u32[]{:S(2)}, u32[]{:S(2)}) collective-permute-start(bf16[1024,128]{1,0:T(8,128)(2,1)S(1)} %pad_maximum_fusion), channel_id=1, source_target_pairs={{0,16},{8,120},{16,32},{24,8},{32,48},{40,24},{48,64},{56,40},{64,... | collective-permute-start | bytes 786440 | tf_op jit(solution)/shard_map/ppermute | solution.py:407
  73.4 8.2 %collective-permute-start.13 = (bf16[1024,128]{1,0:T(8,128)(2,1)S(1)}, bf16[1024,128]{1,0:T(8,128)(2,1)S(1)}, u32[]{:S(2)}, u32[]{:S(2)}) collective-permute-start(bf16[1024,128]{1,0:T(8,128)(2,1)S(1)} %pad_maximum_fusion), channel_id=1, source_target_pairs={{0,144},{8,248},{16,160},{24,136},{32,176},{40,152},{48,192},{56,1... | collective-permute-start | bytes 786440 | tf_op jit(solution)/shard_map/ppermute | solution.py:408
  78.6 8.6 %collective-permute-start.10 = (bf16[1024,128]{1,0:T(8,128)(2,1)S(1)}, bf16[1024,128]{1,0:T(8,128)(2,1)S(1)}, u32[]{:S(2)}, u32[]{:S(2)}) collective-permute-start(bf16[1024,128]{1,0:T(8,128)(2,1)S(1)} %collective-permute-done.9.refs_4_), channel_id=1, source_target_pairs={{0,16},{8,120},{16,32},{24,8},{32,48},{40,24},{48,64},{56,40},{64,... | collective-permute-start | bytes 786440 | tf_op jit(solution)/shard_map/ppermute | solution.py:350
  81.6 11.4 %collective-permute-start.14 = (bf16[1024,128]{1,0:T(8,128)(2,1)S(1)}, bf16[1024,128]{1,0:T(8,128)(2,1)S(1)}, u32[]{:S(2)}, u32[]{:S(2)}) collective-permute-start(bf16[1024,128]{1,0:T(8,128)(2,1)S(1)} %collective-permute-done.13.refs_4_), channel_id=1, source_target_pairs={{0,16},{8,120},{16,32},{24,8},{32,48},{40,24},{48,64},{56,40},{64,... | collective-permute-start | bytes 786440 | tf_op jit(solution)/shard_map/ppermute | solution.py:350
  87.2 8.9 %collective-permute-start.11 = (bf16[1024,128]{1,0:T(8,128)(2,1)S(1)}, bf16[1024,128]{1,0:T(8,128)(2,1)S(1)}, u32[]{:S(2)}, u32[]{:S(2)}) collective-permute-start(bf16[1024,128]{1,0:T(8,128)(2,1)S(1)} %collective-permute-done.10.refs_4_), channel_id=1, source_target_pairs={{0,16},{8,120},{16,32},{24,8},{32,48},{40,24},{48,64},{56,40},{64,... | collective-permute-start | bytes 786440 | tf_op jit(solution)/shard_map/ppermute | solution.py:350
  87.2 17.3 %collective-permute-start.16 = (bf16[512,128]{1,0:T(8,128)(2,1)S(1)}, bf16[512,128]{1,0:T(8,128)(2,1)S(1)}, u32[]{:S(2)}, u32[]{:S(2)}) collective-permute-start(bf16[512,128]{1,0:T(8,128)(2,1)S(1)} %get-tuple-element.55.refs_4_), channel_id=1, source_target_pairs={{0,128},{8,136},{16,144},{24,152},{32,160},{40,168},{48,176},{56,1... | collective-permute-start | bytes 393224 | tf_op jit(solution)/shard_map/ppermute | solution.py:410
  89.4 13.5 %collective-permute-start.17 = (bf16[1024,128]{1,0:T(8,128)(2,1)S(1)}, bf16[1024,128]{1,0:T(8,128)(2,1)S(1)}, u32[]{:S(2)}, u32[]{:S(2)}) collective-permute-start(bf16[1024,128]{1,0:T(8,128)(2,1)S(1)} %collective-permute-done.13.refs_4_), channel_id=1, source_target_pairs={{0,32},{8,104},{16,48},{24,120},{32,64},{40,8},{48,80},{56,24},{64... | collective-permute-start | bytes 786440 | tf_op jit(solution)/shard_map/ppermute | solution.py:350
  93.0 12.5 %collective-permute-start.15 = (bf16[512,128]{1,0:T(8,128)(2,1)S(1)}, bf16[512,128]{1,0:T(8,128)(2,1)S(1)}, u32[]{:S(2)}, u32[]{:S(2)}) collective-permute-start(bf16[512,128]{1,0:T(8,128)(2,1)S(1)} %slice.17), channel_id=1, source_target_pairs={{0,32},{8,104},{16,48},{24,120},{32,64},{40,8},{48,80},{56,24},{64... | collective-permute-start | bytes 393224 | tf_op jit(solution)/shard_map/ppermute | solution.py:350
  96.1 9.4 %collective-permute-start.12 = (bf16[512,128]{1,0:T(8,128)(2,1)S(1)}, bf16[512,128]{1,0:T(8,128)(2,1)S(1)}, u32[]{:S(2)}, u32[]{:S(2)}) collective-permute-start(bf16[512,128]{1,0:T(8,128)(2,1)S(1)} %slice.16), channel_id=1, source_target_pairs={{0,16},{8,120},{16,32},{24,8},{32,48},{40,24},{48,64},{56,40},{64,... | collective-permute-start | bytes 393224 | tf_op jit(solution)/shard_map/ppermute | solution.py:350
  106.5 2.0 %collective-permute-start.18 = (f32[136,1024]{1,0:T(8,128)S(1)}, f32[136,1024]{1,0:T(8,128)S(1)}, u32[]{:S(2)}, u32[]{:S(2)}) collective-permute-start(f32[136,1024]{1,0:T(8,128)S(1)} %attend.19), channel_id=1, source_target_pairs={{0,8},{8,0},{16,24},{24,16},{32,40},{40,32},{48,56},{56,48},{64,72... | collective-permute-start | bytes 1671176 | tf_op jit(solution)/shard_map/ppermute | solution.py:427

commit v4 on v3

--- a/solution.py
+++ b/solution.py
@@ -27,7 +27,7 @@
 STATE = HD + 8
 
 MESSAGES = [(0, 1), (0, 2), (1, 1), (0, 3), (1, 2), (1, 3)]
-SENDS = [(0, 0, 1, 2), (1, 0, 2, 3), (1, 1, 1, 2), (1, 1, 1, 3), (2, 0, 3, 4), (3, 1, 2, 4)]
+SENDS = [(0, 0, 1, 2), (1, 0, 2, 3), (1, 1, 1, 2), (3, 1, 2, 3), (2, 0, 3, 4), (3, 1, 2, 4)]
 
 rope_theta = 500000.0
 norm_eps = 1e-05
@@ -75,21 +75,16 @@
     return jnp.concatenate([cosine, cosine], axis=1), jnp.concatenate([-sine, sine], axis=1)
 
 
-def gather_first(own):
-    return [
-        lax.ppermute(own, "head", xlo_swap()),
-        lax.ppermute(own, "head", y_shift(1)),
-        lax.ppermute(own, "head", y_shift(-1)),
-    ]
-
-
-def gather_second(side, down, up):
-    return [
-        lax.ppermute(side, "head", y_shift(2)),
-        lax.ppermute(down, "head", y_shift(1)),
-        lax.ppermute(side, "head", y_shift(-1)),
-        lax.ppermute(down, "head", xlo_swap()),
-    ]
+def gather_blocks(own):
+    side = lax.ppermute(own, "head", xlo_swap())
+    down = lax.ppermute(own, "head", y_shift(1))
+    up = lax.ppermute(own, "head", y_shift(-1))
+    far_side = lax.ppermute(side, "head", y_shift(2))
+    down, up = lax.optimization_barrier((down, up))
+    far = lax.ppermute(down, "head", y_shift(1))
+    side_up = lax.ppermute(up, "head", xlo_swap())
+    side_down = lax.ppermute(down, "head", xlo_swap())
+    return [own, side, down, up, far, side_up, side_down, far_side]
 
 
 def block_order(place):
@@ -101,14 +96,12 @@
     return [at(0, 0), at(0, 1), at(-1, 0), at(1, 0), at(2, 0), at(1, 1), at(-1, 1), at(2, 1)]
 
 
-def qkv_kernel(rows, count, *refs):
-    blocks, refs = refs[:count], refs[count:]
-    weight_ref, gain_ref, cos_ref, sin_ref = refs[:4]
-    order = block_order(lax.axis_index("head")) if count > 1 else list(range(HEAD_DEVS))
+def qkv_kernel(rows, *refs):
+    blocks = refs[:HEAD_DEVS]
+    weight_ref, gain_ref, cos_ref, sin_ref, query_ref, kv_ref = refs[HEAD_DEVS:]
+    order = block_order(lax.axis_index("head"))
 
     def block(k):
-        if count == 1:
-            return blocks[0][:, k * COLS : (k + 1) * COLS].astype(f32)
         return blocks[k][...].astype(f32)
 
     squares = jnp.zeros((rows, COLS), f32)
@@ -135,7 +128,6 @@
         if j <= GROUPS:
             slab = slab * cosine + pltpu.roll(slab, HD // 2, 1) * sine
         parts.append(slab)
-    query_ref, kv_ref = refs[4:6]
     for j in range(GROUPS + 2):
         if j == GROUPS:
             kv_ref[:ROWS, :] = parts[j].astype(bf16)
@@ -179,7 +171,7 @@
 def project_qkv(blocks, weight, gain, cosine, sine):
     rows = blocks[0].shape[0]
     return pl.pallas_call(
-        functools.partial(qkv_kernel, rows, len(blocks)),
+        functools.partial(qkv_kernel, rows),
         out_shape=(
             jax.ShapeDtypeStruct((HD, QCOLS), bf16),
             jax.ShapeDtypeStruct((2 * ROWS, HD), bf16),
@@ -362,6 +354,7 @@
         out_shape=jax.ShapeDtypeStruct((OWNERS, HD), jnp.int32),
         in_specs=vmem(1),
         out_specs=pl.BlockSpec(memory_space=pltpu.VMEM),
+        compiler_params=pltpu.CompilerParams(vmem_limit_bytes=ATTEND_LIMIT),
         name="my_entry",
     )(span_of)
     table_rows = lax.all_to_all(
@@ -395,12 +388,9 @@
         mail.reshape(OWNERS, CAP, COLS + HD), "ctx", split_axis=0, concat_axis=0, tiled=True
     ).reshape(SLOTS, COLS + HD)
     sequence = whole(place_kernel, (ROWS, COLS), "place_rows", mail, text_rows)
-    first = lax.optimization_barrier(gather_first(sequence))
-    weight, gain, cosine, sine, first = lax.optimization_barrier((weight, gain, cosine, sine, first))
-    far_side, far, side_up, side_down = gather_second(*first)
-    queries, own = project_qkv(
-        [sequence, *first, far, side_up, side_down, far_side], load_weight(weight), gain, cosine, sine
-    )
+    blocks = gather_blocks(sequence)
+    weight, gain, cosine, sine, blocks[3] = lax.optimization_barrier((weight, gain, cosine, sine, blocks[3]))
+    queries, own = project_qkv(blocks, load_weight(weight), gain, cosine, sine)
 
     stream = jnp.concatenate([own, lax.ppermute(own, "ctx", core_swap())], axis=0)
     stream, queries, own = lax.optimization_barrier((stream, queries, own))

time: 110 us -> 109 us (level)
  waiting for transfers between devices: 32.6 us -> 30.6 us
  starting transfers between devices: 48.2 us -> 49.8 us
    ppermute x1, starting transfers between devices: 0.36 us -> 3.24 us  [on_device(): theirs = lax.ppermute(given, 'ctx', core_swap())]
    ppermute x1, starting transfers between devices: 2.19 us -> 0.01 us  [on_device(): side = lax.ppermute(own, 'ctx', xhi_swap())]
    unnamed x14 -> x16, local copies, waits for them, and re-layouts: 2.88 us -> 3.66 us
  transfers between devices with their start and end apart: 21 -> 21, of which waited for: 10 -> 9; matrix products, arithmetic and copies ran while one was open for 4% -> 4% of each run, Pallas kernels for 12% -> 12%
where the time goes in v4:
time: 109 us
  starting transfers between devices  49.8 us (46%)
  waiting for transfers between devices  30.6 us (28%)
  Pallas kernels  20 us (18%)
  local copies, waits for them, and re-layouts  4.12 us (4%)
  matrix products  3.26 us (3%)
    all_to_all x1, waiting for transfers between devices, on_device(): lax.all_to_all(mail.reshape(OWNERS, CAP, COLS + HD), 'ctx', split_axis=0,...  14.6 us
    pallas_call x10, Pallas kernels, attend(): pl.pallas_call(functools.partial(attend_kernel, first, len(blocks), key_r...  13.6 us
    ppermute x6, starting transfers between devices, send_on(): return lax.ppermute(block[:size], 'ctx', z_move(steps))  13.4 us
    all_to_all x1, starting transfers between devices, on_device(): lax.all_to_all(my_rows.reshape(OWNERS, 1, HD), 'ctx', split_axis=0, conca...  12.6 us
    all_to_all x1, waiting for transfers between devices, on_device(): lax.all_to_all(my_rows.reshape(OWNERS, 1, HD), 'ctx', split_axis=0, conca...  5.86 us
    all_to_all x1, starting transfers between devices, on_device(): lax.all_to_all(mail.reshape(OWNERS, CAP, COLS + HD), 'ctx', split_axis=0,...  4.32 us
    ppermute x1, waiting for transfers between devices, gather_blocks(): down = lax.ppermute(own, 'head', y_shift(1))  4.15 us
    ppermute x1, starting transfers between devices, on_device(): lax.ppermute(own, 'ctx', core_swap())  4.12 us
  transfers between devices with their start and end apart: 21, of which 9 were waited for; matrix products, arithmetic and copies ran while one was open for 4% of the time, Pallas kernels for 12%

profile of v4, /device:TPU:1, one launch (start us, length us, event | category | flops | bytes accessed | tf_op | source)
XLA Modules:
  0.0 109.0 jit_solution(5706112071914840538)
XLA Ops:
  1.5 12.6 %all-to-all-start = ((s32[32,1,128]{2,1,0:T(1,128)}), s32[32,1,128]{2,1,0:T(1,128)S(1)}, u32[]{:S(2)}, u32[]{:S(2)}) async-start(s32[32,1,128]{2,1,0:T(1,128)} %bitcast.37), calls=%async_computation | async-start | bytes 32768 | tf_op jit(solution)/shard_map/all_to_all | solution.py:360
  14.1 3.3 %convolution_convert_fusion.rows_ref = bf16[160,512]{1,0:T(8,128)(2,1)S(1)} fusion(bf16[160,4608]{1,0:T(8,128)(2,1)S(1)} %copy-done, bf16[4608,512]{1,0:T(8,128)(2,1)} %param.11), kind=kOutput, calls=%fused_computation | convolution fusion | flops 755056640 | bytes 6356992 | tf_op jit(solution)/shard_map/dot_general | solution.py:363
  17.5 5.9 %all-to-all-done = s32[32,1,128]{2,1,0:T(1,128)S(1)} async-done(((s32[32,1,128]{2,1,0:T(1,128)}), s32[32,1,128]{2,1,0:T(1,128)S(1)}, u32[]{:S(2)}, u32[]{:S(2)}) %all-to-all-start) | async-done | bytes 16416 | tf_op jit(solution)/shard_map/all_to_all | solution.py:360
  23.3 1.5 %route_rows.1 = bf16[256,640]{1,0:T(8,128)(2,1)} custom-call(bf16[160,512]{1,0:T(8,128)(2,1)S(1)} %convolution_convert_fusion.rows_ref, s32[160,1]{1,0:T(8,128)S(1)} %copy.12.pos_ref, s32[32,128]{1,0:T(8,128)S(1)} %bitcast.59), custom_call_target="tpu_custom_call" | custom-call | flops 67108864 | bytes 524288 | tf_op jit(solution)/shard_map/route_rows/pallas_call | solution.py:230
  24.8 4.3 %all-to-all-start.1 = ((bf16[32,8,640]{2,1,0:T(8,128)(2,1)}), bf16[32,8,640]{2,1,0:T(8,128)(2,1)S(1)}, u32[]{:S(2)}, u32[]{:S(2)}) async-start(bf16[32,8,640]{2,1,0:T(8,128)(2,1)} %bitcast.40), calls=%async_computation.1 | async-start | bytes 655360 | tf_op jit(solution)/shard_map/all_to_all | solution.py:387
  29.2 14.6 %all-to-all-done.1 = bf16[32,8,640]{2,1,0:T(8,128)(2,1)S(1)} async-done(((bf16[32,8,640]{2,1,0:T(8,128)(2,1)}), bf16[32,8,640]{2,1,0:T(8,128)(2,1)S(1)}, u32[]{:S(2)}, u32[]{:S(2)}) %all-to-all-start.1) | async-done | bytes 327712 | tf_op jit(solution)/shard_map/all_to_all | solution.py:387
  44.2 1.4 %collective-permute-start.1 = (bf16[256,512]{1,0:T(8,128)(2,1)S(1)}, bf16[256,512]{1,0:T(8,128)(2,1)S(1)}, u32[]{:S(2)}, u32[]{:S(2)}) collective-permute-start(bf16[256,512]{1,0:T(8,128)(2,1)S(1)} %place_rows.1.refs_0_), channel_id=1, source_target_pairs={{0,2},{1,3},{2,4},{3,5},{4,6},{5,7},{6,0},{7,1},{8,10},{9,11},{10,... | collective-permute-start | bytes 786440 | tf_op jit(solution)/shard_map/ppermute | solution.py:80
  45.5 1.5 %collective-permute-start.2 = (bf16[256,512]{1,0:T(8,128)(2,1)S(1)}, bf16[256,512]{1,0:T(8,128)(2,1)S(1)}, u32[]{:S(2)}, u32[]{:S(2)}) collective-permute-start(bf16[256,512]{1,0:T(8,128)(2,1)S(1)} %place_rows.1.refs_0_), channel_id=1, source_target_pairs={{0,6},{1,7},{2,0},{3,1},{4,2},{5,3},{6,4},{7,5},{8,14},{9,15},{10,... | collective-permute-start | bytes 786440 | tf_op jit(solution)/shard_map/ppermute | solution.py:81
  47.5 4.2 %collective-permute-done.1.refs_2_ = bf16[256,512]{1,0:T(8,128)(2,1)S(1)} collective-permute-done((bf16[256,512]{1,0:T(8,128)(2,1)S(1)}, bf16[256,512]{1,0:T(8,128)(2,1)S(1)}, u32[]{:S(2)}, u32[]{:S(2)}) %collective-permute-start.1) | collective-permute-done | bytes 262176 | tf_op jit(solution)/shard_map/ppermute | solution.py:80
  52.9 1.1 %collective-permute-start.4 = (bf16[256,512]{1,0:T(8,128)(2,1)S(1)}, bf16[256,512]{1,0:T(8,128)(2,1)S(1)}, u32[]{:S(2)}, u32[]{:S(2)}) collective-permute-start(bf16[256,512]{1,0:T(8,128)(2,1)S(1)} %collective-permute-done.2.refs_3_), channel_id=1, source_target_pairs={{0,1},{1,0},{2,3},{3,2},{4,5},{5,4},{6,7},{7,6},{8,9},{9,8},{10,11... | collective-permute-start | bytes 786440 | tf_op jit(solution)/shard_map/ppermute | solution.py:85
  54.1 2.8 %collective-permute-start.6 = (bf16[256,512]{1,0:T(8,128)(2,1)S(1)}, bf16[256,512]{1,0:T(8,128)(2,1)S(1)}, u32[]{:S(2)}, u32[]{:S(2)}) collective-permute-start(bf16[256,512]{1,0:T(8,128)(2,1)S(1)} %collective-permute-done.refs_1_), channel_id=1, source_target_pairs={{0,4},{1,5},{2,6},{3,7},{4,0},{5,1},{6,2},{7,3},{8,12},{9,13},{10,... | collective-permute-start | bytes 786440 | tf_op jit(solution)/shard_map/ppermute | solution.py:82
  57.5 2.8 %copy-done.1 = bf16[4096,1,6,128]{3,0,2,1:T(8,128)(2,1)S(1)} copy-done((bf16[4096,1,6,128]{3,0,2,1:T(8,128)(2,1)S(1)}, bf16[4096,1,6,128]{3,0,2,1:T(8,128)(2,1)}, u32[]{:S(2)}) %copy-start.1) | copy-done | bytes 6291480
  60.8 2.1 %collective-permute-done.4.refs_5_ = bf16[256,512]{1,0:T(8,128)(2,1)S(1)} collective-permute-done((bf16[256,512]{1,0:T(8,128)(2,1)S(1)}, bf16[256,512]{1,0:T(8,128)(2,1)S(1)}, u32[]{:S(2)}, u32[]{:S(2)}) %collective-permute-start.4) | collective-permute-done | bytes 262176 | tf_op jit(solution)/shard_map/ppermute | solution.py:85
  62.9 1.3 %collective-permute-done.6.refs_7_ = bf16[256,512]{1,0:T(8,128)(2,1)S(1)} collective-permute-done((bf16[256,512]{1,0:T(8,128)(2,1)S(1)}, bf16[256,512]{1,0:T(8,128)(2,1)S(1)}, u32[]{:S(2)}, u32[]{:S(2)}) %collective-permute-start.6) | collective-permute-done | bytes 262176 | tf_op jit(solution)/shard_map/ppermute | solution.py:82
  64.2 2.5 %norm_qkv.1 = (bf16[128,1024]{1,0:T(8,128)(2,1)S(1)}, bf16[512,128]{1,0:T(8,128)(2,1)S(1)}) custom-call(bf16[256,512]{1,0:T(8,128)(2,1)S(1)} %place_rows.1.refs_0_, bf16[256,512]{1,0:T(8,128)(2,1)S(1)} %collective-permute-done.refs_1_, bf16[256,512]{1,0:T(8,128)(2,1)S(1)} %collective-permute-done.1.refs_2_, ...), custom_call_target="tpu_custom_call" | custom-call | flops 1610612736 | bytes 8388608 | tf_op jit(solution)/shard_map/norm_qkv/pallas_call | solution.py:173
  66.7 4.1 %collective-permute-start.7 = (bf16[512,128]{1,0:T(8,128)(2,1)S(1)}, bf16[512,128]{1,0:T(8,128)(2,1)S(1)}, u32[]{:S(2)}, u32[]{:S(2)}) collective-permute-start(bf16[512,128]{1,0:T(8,128)(2,1)S(1)} %get-tuple-element.49.refs_4_), channel_id=1, source_target_pairs={{0,8},{8,0},{16,24},{24,16},{32,40},{40,32},{48,56},{56,48},{64,72... | collective-permute-start | bytes 393224 | tf_op jit(solution)/shard_map/ppermute | solution.py:395
  72.9 3.0 %collective-permute-start.13 = (bf16[1024,128]{1,0:T(8,128)(2,1)S(1)}, bf16[1024,128]{1,0:T(8,128)(2,1)S(1)}, u32[]{:S(2)}, u32[]{:S(2)}) collective-permute-start(bf16[1024,128]{1,0:T(8,128)(2,1)S(1)} %pad_maximum_fusion), channel_id=1, source_target_pairs={{0,144},{8,248},{16,160},{24,136},{32,176},{40,152},{48,192},{56,1... | collective-permute-start | bytes 786440 | tf_op jit(solution)/shard_map/ppermute | solution.py:398
  76.0 1.0 attend.10
  77.1 1.1 collective-permute-done.9.refs_4_
  78.2 1.7 %collective-permute-start.10 = (bf16[1024,128]{1,0:T(8,128)(2,1)S(1)}, bf16[1024,128]{1,0:T(8,128)(2,1)S(1)}, u32[]{:S(2)}, u32[]{:S(2)}) collective-permute-start(bf16[1024,128]{1,0:T(8,128)(2,1)S(1)} %collective-permute-done.9.refs_4_), channel_id=1, source_target_pairs={{0,16},{8,120},{16,32},{24,8},{32,48},{40,24},{48,64},{56,40},{64,... | collective-permute-start | bytes 786440 | tf_op jit(solution)/shard_map/ppermute | solution.py:342
  79.9 1.6 %attend.11 = (f32[136,1024]{1,0:T(8,128)S(1)}, f32[136,1024]{1,0:T(8,128)S(1)}) custom-call(f32[32,128]{1,0:T(8,128)S(1)} %broadcast_in_dim.36.refs_0_, f32[2,1024]{1,0:T(2,128)S(1)} %bitcast.62, bf16[128,1024]{1,0:T(8,128)(2,1)S(1)} %get-tuple-element.47.refs_2_, bf16[128,1024]{1,0:T(8,128)(2,1)S(1)} %collective-permute-done.8.refs_3_, ...), custom_call_target="tpu_custom_call" | custom-call | flops 1073741824 | bytes 2490368 | tf_op jit(solution)/shard_map/attend/pallas_call | solution.py:299
  81.5 5.5 %collective-permute-start.14 = (bf16[1024,128]{1,0:T(8,128)(2,1)S(1)}, bf16[1024,128]{1,0:T(8,128)(2,1)S(1)}, u32[]{:S(2)}, u32[]{:S(2)}) collective-permute-start(bf16[1024,128]{1,0:T(8,128)(2,1)S(1)} %collective-permute-done.13.refs_4_), channel_id=1, source_target_pairs={{0,16},{8,120},{16,32},{24,8},{32,48},{40,24},{48,64},{56,40},{64,... | collective-permute-start | bytes 786440 | tf_op jit(solution)/shard_map/ppermute | solution.py:342
  87.0 1.6 %attend.12 = (f32[136,1024]{1,0:T(8,128)S(1)}, f32[136,1024]{1,0:T(8,128)S(1)}) custom-call(f32[32,128]{1,0:T(8,128)S(1)} %broadcast_in_dim.36.refs_0_, f32[2,1024]{1,0:T(2,128)S(1)} %bitcast.63, bf16[128,1024]{1,0:T(8,128)(2,1)S(1)} %get-tuple-element.47.refs_2_, bf16[128,1024]{1,0:T(8,128)(2,1)S(1)} %collective-permute-done.8.refs_3_, ...), custom_call_target="tpu_custom_call" | custom-call | flops 1073741824 | bytes 2490368 | tf_op jit(solution)/shard_map/attend/pallas_call | solution.py:299
  88.6 1.6 %attend.13 = (f32[136,1024]{1,0:T(8,128)S(1)}, f32[136,1024]{1,0:T(8,128)S(1)}) custom-call(f32[32,128]{1,0:T(8,128)S(1)} %broadcast_in_dim.36.refs_0_, f32[2,1024]{1,0:T(2,128)S(1)} %bitcast.64, bf16[128,1024]{1,0:T(8,128)(2,1)S(1)} %get-tuple-element.47.refs_2_, bf16[128,1024]{1,0:T(8,128)(2,1)S(1)} %collective-permute-done.8.refs_3_, ...), custom_call_target="tpu_custom_call" | custom-call | flops 1073741824 | bytes 2490368 | tf_op jit(solution)/shard_map/attend/pallas_call | solution.py:299
  90.3 3.1 %collective-permute-start.17 = (bf16[1024,128]{1,0:T(8,128)(2,1)S(1)}, bf16[1024,128]{1,0:T(8,128)(2,1)S(1)}, u32[]{:S(2)}, u32[]{:S(2)}) collective-permute-start(bf16[1024,128]{1,0:T(8,128)(2,1)S(1)} %collective-permute-done.14.refs_4_), channel_id=1, source_target_pairs={{0,16},{8,120},{16,32},{24,8},{32,48},{40,24},{48,64},{56,40},{64,... | collective-permute-start | bytes 786440 | tf_op jit(solution)/shard_map/ppermute | solution.py:342
  93.4 2.0 %collective-permute-start.15 = (bf16[512,128]{1,0:T(8,128)(2,1)S(1)}, bf16[512,128]{1,0:T(8,128)(2,1)S(1)}, u32[]{:S(2)}, u32[]{:S(2)}) collective-permute-start(bf16[512,128]{1,0:T(8,128)(2,1)S(1)} %slice.17), channel_id=1, source_target_pairs={{0,32},{8,104},{16,48},{24,120},{32,64},{40,8},{48,80},{56,24},{64... | collective-permute-start | bytes 393224 | tf_op jit(solution)/shard_map/ppermute | solution.py:342
  95.4 1.1 collective-permute-start.12
  96.5 1.6 %attend.14 = (f32[136,1024]{1,0:T(8,128)S(1)}, f32[136,1024]{1,0:T(8,128)S(1)}) custom-call(f32[32,128]{1,0:T(8,128)S(1)} %broadcast_in_dim.36.refs_0_, f32[2,1024]{1,0:T(2,128)S(1)} %bitcast.65, bf16[128,1024]{1,0:T(8,128)(2,1)S(1)} %get-tuple-element.47.refs_2_, bf16[128,1024]{1,0:T(8,128)(2,1)S(1)} %collective-permute-done.8.refs_3_, ...), custom_call_target="tpu_custom_call" | custom-call | flops 1073741824 | bytes 2490368 | tf_op jit(solution)/shard_map/attend/pallas_call | solution.py:299
  98.1 1.6 %attend.15 = (f32[136,1024]{1,0:T(8,128)S(1)}, f32[136,1024]{1,0:T(8,128)S(1)}) custom-call(f32[32,128]{1,0:T(8,128)S(1)} %broadcast_in_dim.36.refs_0_, f32[2,1024]{1,0:T(2,128)S(1)} %bitcast.66, bf16[128,1024]{1,0:T(8,128)(2,1)S(1)} %get-tuple-element.47.refs_2_, bf16[128,1024]{1,0:T(8,128)(2,1)S(1)} %collective-permute-done.8.refs_3_, ...), custom_call_target="tpu_custom_call" | custom-call | flops 1073741824 | bytes 2490368 | tf_op jit(solution)/shard_map/attend/pallas_call | solution.py:299
  99.7 1.6 %attend.16 = (f32[136,1024]{1,0:T(8,128)S(1)}, f32[136,1024]{1,0:T(8,128)S(1)}) custom-call(f32[32,128]{1,0:T(8,128)S(1)} %broadcast_in_dim.36.refs_0_, f32[2,1024]{1,0:T(2,128)S(1)} %bitcast.67, bf16[128,1024]{1,0:T(8,128)(2,1)S(1)} %get-tuple-element.47.refs_2_, bf16[128,1024]{1,0:T(8,128)(2,1)S(1)} %collective-permute-done.8.refs_3_, ...), custom_call_target="tpu_custom_call" | custom-call | flops 1073741824 | bytes 2490368 | tf_op jit(solution)/shard_map/attend/pallas_call | solution.py:299
  102.3 1.0 attend.19
  103.3 3.2 %collective-permute-start.18 = (f32[136,1024]{1,0:T(8,128)S(1)}, f32[136,1024]{1,0:T(8,128)S(1)}, u32[]{:S(2)}, u32[]{:S(2)}) collective-permute-start(f32[136,1024]{1,0:T(8,128)S(1)} %attend.19), channel_id=1, source_target_pairs={{0,8},{8,0},{16,24},{24,16},{32,40},{40,32},{48,56},{56,48},{64,72... | collective-permute-start | bytes 1671176 | tf_op jit(solution)/shard_map/ppermute | solution.py:417
  (59 shorter events, 10.5 us)
Async XLA Ops:
  0.0 14.1 %copy-start = (bf16[160,4608]{1,0:T(8,128)(2,1)S(1)}, bf16[160,4608]{1,0:T(8,128)(2,1)}, u32[]{:S(2)}) copy-start(bf16[160,4608]{1,0:T(8,128)(2,1)} %param.7) | copy-start | bytes 4423684
  0.0 43.8 %copy-start.2 = (bf16[256,512]{1,0:T(8,128)(2,1)S(1)}, bf16[256,512]{1,0:T(8,128)(2,1)}, u32[]{:S(2)}) copy-start(bf16[256,512]{1,0:T(8,128)(2,1)} %text_ref.1) | copy-start | bytes 786436
  0.0 0.8 copy-start.4
  0.8 16.6 %copy-start.6 = (s32[160]{0:T(256)S(1)}, s32[160]{0:T(256)}, u32[]{:S(2)}) copy-start(s32[160]{0:T(256)} %param.8) | copy-start | bytes 1924
  0.8 28.4 %copy-start.5 = (s32[1,2]{1,0:T(1,128)S(1)}, s32[1,2]{1,0:T(1,128)}, u32[]{:S(2)}) copy-start(s32[1,2]{1,0:T(1,128)} %span_ref.1) | copy-start | bytes 28
  1.5 21.9 %all-to-all-start = ((s32[32,1,128]{2,1,0:T(1,128)}), s32[32,1,128]{2,1,0:T(1,128)S(1)}, u32[]{:S(2)}, u32[]{:S(2)}) async-start(s32[32,1,128]{2,1,0:T(1,128)} %bitcast.37), calls=%async_computation | async-start | bytes 32768 | tf_op jit(solution)/shard_map/all_to_all | solution.py:360
  24.8 18.9 %all-to-all-start.1 = ((bf16[32,8,640]{2,1,0:T(8,128)(2,1)}), bf16[32,8,640]{2,1,0:T(8,128)(2,1)S(1)}, u32[]{:S(2)}, u32[]{:S(2)}) async-start(bf16[32,8,640]{2,1,0:T(8,128)(2,1)} %bitcast.40), calls=%async_computation.1 | async-start | bytes 655360 | tf_op jit(solution)/shard_map/all_to_all | solution.py:387
  44.2 7.5 %collective-permute-start.1 = (bf16[256,512]{1,0:T(8,128)(2,1)S(1)}, bf16[256,512]{1,0:T(8,128)(2,1)S(1)}, u32[]{:S(2)}, u32[]{:S(2)}) collective-permute-start(bf16[256,512]{1,0:T(8,128)(2,1)S(1)} %place_rows.1.refs_0_), channel_id=1, source_target_pairs={{0,2},{1,3},{2,4},{3,5},{4,6},{5,7},{6,0},{7,1},{8,10},{9,11},{10,... | collective-permute-start | bytes 786440 | tf_op jit(solution)/shard_map/ppermute | solution.py:80
  45.5 6.1 %collective-permute-start.2 = (bf16[256,512]{1,0:T(8,128)(2,1)S(1)}, bf16[256,512]{1,0:T(8,128)(2,1)S(1)}, u32[]{:S(2)}, u32[]{:S(2)}) collective-permute-start(bf16[256,512]{1,0:T(8,128)(2,1)S(1)} %place_rows.1.refs_0_), channel_id=1, source_target_pairs={{0,6},{1,7},{2,0},{3,1},{4,2},{5,3},{6,4},{7,5},{8,14},{9,15},{10,... | collective-permute-start | bytes 786440 | tf_op jit(solution)/shard_map/ppermute | solution.py:81
  47.1 7.0 %collective-permute-start = (bf16[256,512]{1,0:T(8,128)(2,1)S(1)}, bf16[256,512]{1,0:T(8,128)(2,1)S(1)}, u32[]{:S(2)}, u32[]{:S(2)}) collective-permute-start(bf16[256,512]{1,0:T(8,128)(2,1)S(1)} %place_rows.1.refs_0_), channel_id=1, source_target_pairs={{0,1},{1,0},{2,3},{3,2},{4,5},{5,4},{6,7},{7,6},{8,9},{9,8},{10,11... | collective-permute-start | bytes 786440 | tf_op jit(solution)/shard_map/ppermute | solution.py:79
  51.6 9.2 %collective-permute-start.3 = (bf16[256,512]{1,0:T(8,128)(2,1)S(1)}, bf16[256,512]{1,0:T(8,128)(2,1)S(1)}, u32[]{:S(2)}, u32[]{:S(2)}) collective-permute-start(bf16[256,512]{1,0:T(8,128)(2,1)S(1)} %collective-permute-done.1.refs_2_), channel_id=1, source_target_pairs={{0,2},{1,3},{2,4},{3,5},{4,6},{5,7},{6,0},{7,1},{8,10},{9,11},{10,... | collective-permute-start | bytes 786440 | tf_op jit(solution)/shard_map/ppermute | solution.py:84
  52.6 8.2 %collective-permute-start.5 = (bf16[256,512]{1,0:T(8,128)(2,1)S(1)}, bf16[256,512]{1,0:T(8,128)(2,1)S(1)}, u32[]{:S(2)}, u32[]{:S(2)}) collective-permute-start(bf16[256,512]{1,0:T(8,128)(2,1)S(1)} %collective-permute-done.1.refs_2_), channel_id=1, source_target_pairs={{0,1},{1,0},{2,3},{3,2},{4,5},{5,4},{6,7},{7,6},{8,9},{9,8},{10,11... | collective-permute-start | bytes 786440 | tf_op jit(solution)/shard_map/ppermute | solution.py:86
  52.9 10.0 %collective-permute-start.4 = (bf16[256,512]{1,0:T(8,128)(2,1)S(1)}, bf16[256,512]{1,0:T(8,128)(2,1)S(1)}, u32[]{:S(2)}, u32[]{:S(2)}) collective-permute-start(bf16[256,512]{1,0:T(8,128)(2,1)S(1)} %collective-permute-done.2.refs_3_), channel_id=1, source_target_pairs={{0,1},{1,0},{2,3},{3,2},{4,5},{5,4},{6,7},{7,6},{8,9},{9,8},{10,11... | collective-permute-start | bytes 786440 | tf_op jit(solution)/shard_map/ppermute | solution.py:85
  54.1 10.1 %collective-permute-start.6 = (bf16[256,512]{1,0:T(8,128)(2,1)S(1)}, bf16[256,512]{1,0:T(8,128)(2,1)S(1)}, u32[]{:S(2)}, u32[]{:S(2)}) collective-permute-start(bf16[256,512]{1,0:T(8,128)(2,1)S(1)} %collective-permute-done.refs_1_), channel_id=1, source_target_pairs={{0,4},{1,5},{2,6},{3,7},{4,0},{5,1},{6,2},{7,3},{8,12},{9,13},{10,... | collective-permute-start | bytes 786440 | tf_op jit(solution)/shard_map/ppermute | solution.py:82
  57.5 2.8 %copy-start.1 = (bf16[4096,1,6,128]{3,0,2,1:T(8,128)(2,1)S(1)}, bf16[4096,1,6,128]{3,0,2,1:T(8,128)(2,1)}, u32[]{:S(2)}) copy-start(bf16[4096,1,6,128]{3,0,2,1:T(8,128)(2,1)} %param.13) | copy-start | bytes 18874372
  60.3 3.9 %copy-start.3 = (f32[4096]{0:T(1024)S(1)}, f32[4096]{0:T(1024)}, u32[]{:S(2)}) copy-start(f32[4096]{0:T(1024)} %param.12) | copy-start | bytes 49156
  66.7 5.1 %collective-permute-start.7 = (bf16[512,128]{1,0:T(8,128)(2,1)S(1)}, bf16[512,128]{1,0:T(8,128)(2,1)S(1)}, u32[]{:S(2)}, u32[]{:S(2)}) collective-permute-start(bf16[512,128]{1,0:T(8,128)(2,1)S(1)} %get-tuple-element.49.refs_4_), channel_id=1, source_target_pairs={{0,8},{8,0},{16,24},{24,16},{32,40},{40,32},{48,56},{56,48},{64,72... | collective-permute-start | bytes 393224 | tf_op jit(solution)/shard_map/ppermute | solution.py:395
  71.9 4.1 %collective-permute-start.8 = (bf16[128,1024]{1,0:T(8,128)(2,1)S(1)}, bf16[128,1024]{1,0:T(8,128)(2,1)S(1)}, u32[]{:S(2)}, u32[]{:S(2)}) collective-permute-start(bf16[128,1024]{1,0:T(8,128)(2,1)S(1)} %get-tuple-element.47.refs_2_), channel_id=1, source_target_pairs={{0,8},{8,0},{16,24},{24,16},{32,40},{40,32},{48,56},{56,48},{64,72... | collective-permute-start | bytes 786440 | tf_op jit(solution)/shard_map/ppermute | solution.py:399
  72.6 5.5 %collective-permute-start.9 = (bf16[1024,128]{1,0:T(8,128)(2,1)S(1)}, bf16[1024,128]{1,0:T(8,128)(2,1)S(1)}, u32[]{:S(2)}, u32[]{:S(2)}) collective-permute-start(bf16[1024,128]{1,0:T(8,128)(2,1)S(1)} %pad_maximum_fusion), channel_id=1, source_target_pairs={{0,16},{8,120},{16,32},{24,8},{32,48},{40,24},{48,64},{56,40},{64,... | collective-permute-start | bytes 786440 | tf_op jit(solution)/shard_map/ppermute | solution.py:397
  72.9 8.6 %collective-permute-start.13 = (bf16[1024,128]{1,0:T(8,128)(2,1)S(1)}, bf16[1024,128]{1,0:T(8,128)(2,1)S(1)}, u32[]{:S(2)}, u32[]{:S(2)}) collective-permute-start(bf16[1024,128]{1,0:T(8,128)(2,1)S(1)} %pad_maximum_fusion), channel_id=1, source_target_pairs={{0,144},{8,248},{16,160},{24,136},{32,176},{40,152},{48,192},{56,1... | collective-permute-start | bytes 786440 | tf_op jit(solution)/shard_map/ppermute | solution.py:398
  78.2 8.8 %collective-permute-start.10 = (bf16[1024,128]{1,0:T(8,128)(2,1)S(1)}, bf16[1024,128]{1,0:T(8,128)(2,1)S(1)}, u32[]{:S(2)}, u32[]{:S(2)}) collective-permute-start(bf16[1024,128]{1,0:T(8,128)(2,1)S(1)} %collective-permute-done.9.refs_4_), channel_id=1, source_target_pairs={{0,16},{8,120},{16,32},{24,8},{32,48},{40,24},{48,64},{56,40},{64,... | collective-permute-start | bytes 786440 | tf_op jit(solution)/shard_map/ppermute | solution.py:342
  81.5 8.8 %collective-permute-start.14 = (bf16[1024,128]{1,0:T(8,128)(2,1)S(1)}, bf16[1024,128]{1,0:T(8,128)(2,1)S(1)}, u32[]{:S(2)}, u32[]{:S(2)}) collective-permute-start(bf16[1024,128]{1,0:T(8,128)(2,1)S(1)} %collective-permute-done.13.refs_4_), channel_id=1, source_target_pairs={{0,16},{8,120},{16,32},{24,8},{32,48},{40,24},{48,64},{56,40},{64,... | collective-permute-start | bytes 786440 | tf_op jit(solution)/shard_map/ppermute | solution.py:342
  86.9 8.5 %collective-permute-start.11 = (bf16[1024,128]{1,0:T(8,128)(2,1)S(1)}, bf16[1024,128]{1,0:T(8,128)(2,1)S(1)}, u32[]{:S(2)}, u32[]{:S(2)}) collective-permute-start(bf16[1024,128]{1,0:T(8,128)(2,1)S(1)} %collective-permute-done.10.refs_4_), channel_id=1, source_target_pairs={{0,16},{8,120},{16,32},{24,8},{32,48},{40,24},{48,64},{56,40},{64,... | collective-permute-start | bytes 786440 | tf_op jit(solution)/shard_map/ppermute | solution.py:342
  90.3 9.5 %collective-permute-start.17 = (bf16[1024,128]{1,0:T(8,128)(2,1)S(1)}, bf16[1024,128]{1,0:T(8,128)(2,1)S(1)}, u32[]{:S(2)}, u32[]{:S(2)}) collective-permute-start(bf16[1024,128]{1,0:T(8,128)(2,1)S(1)} %collective-permute-done.14.refs_4_), channel_id=1, source_target_pairs={{0,16},{8,120},{16,32},{24,8},{32,48},{40,24},{48,64},{56,40},{64,... | collective-permute-start | bytes 786440 | tf_op jit(solution)/shard_map/ppermute | solution.py:342
  93.4 8.0 %collective-permute-start.16 = (bf16[512,128]{1,0:T(8,128)(2,1)S(1)}, bf16[512,128]{1,0:T(8,128)(2,1)S(1)}, u32[]{:S(2)}, u32[]{:S(2)}) collective-permute-start(bf16[512,128]{1,0:T(8,128)(2,1)S(1)} %get-tuple-element.49.refs_4_), channel_id=1, source_target_pairs={{0,128},{8,136},{16,144},{24,152},{32,160},{40,168},{48,176},{56,1... | collective-permute-start | bytes 393224 | tf_op jit(solution)/shard_map/ppermute | solution.py:400
  93.4 8.9 %collective-permute-start.15 = (bf16[512,128]{1,0:T(8,128)(2,1)S(1)}, bf16[512,128]{1,0:T(8,128)(2,1)S(1)}, u32[]{:S(2)}, u32[]{:S(2)}) collective-permute-start(bf16[512,128]{1,0:T(8,128)(2,1)S(1)} %slice.17), channel_id=1, source_target_pairs={{0,32},{8,104},{16,48},{24,120},{32,64},{40,8},{48,80},{56,24},{64... | collective-permute-start | bytes 393224 | tf_op jit(solution)/shard_map/ppermute | solution.py:342
  95.4 6.9 %collective-permute-start.12 = (bf16[512,128]{1,0:T(8,128)(2,1)S(1)}, bf16[512,128]{1,0:T(8,128)(2,1)S(1)}, u32[]{:S(2)}, u32[]{:S(2)}) collective-permute-start(bf16[512,128]{1,0:T(8,128)(2,1)S(1)} %slice.16), channel_id=1, source_target_pairs={{0,16},{8,120},{16,32},{24,8},{32,48},{40,24},{48,64},{56,40},{64,... | collective-permute-start | bytes 393224 | tf_op jit(solution)/shard_map/ppermute | solution.py:342
  103.3 4.8 %collective-permute-start.18 = (f32[136,1024]{1,0:T(8,128)S(1)}, f32[136,1024]{1,0:T(8,128)S(1)}, u32[]{:S(2)}, u32[]{:S(2)}) collective-permute-start(f32[136,1024]{1,0:T(8,128)S(1)} %attend.19), channel_id=1, source_target_pairs={{0,8},{8,0},{16,24},{24,16},{32,40},{40,32},{48,56},{56,48},{64,72... | collective-permute-start | bytes 1671176 | tf_op jit(solution)/shard_map/ppermute | solution.py:417
